TPU v7x, 512 devices: a whole 4x4x16 slice. The times are simulated.
512 devices in a mesh: lon: 32 (over x_hi, z), lat: 16 (over y, x_lo, core).
Axes of the slice: x: 4 (x_hi: 2, x_lo: 2; x = x_hi * 2 + x_lo), y: 4, z: 16, core: 2. Of those that a mesh axis runs over, the one named last changes fastest.
Arguments:
- ensemble: bfloat16 [64, 1024, 4096], P(None, 'lat', 'lon'), may hold values from -6 to 6
- right_side: float32 [1024, 4096], P('lat', 'lon'), may hold values from -40 to 40
- obs_error: float32 [1024, 4096], P('lat', 'lon'), may hold values from 0.3 to 3
- valid: int32 [1024, 4096], P('lat', 'lon'), may hold values 0 or 1
- halfwidth: int32 [2], replicated, may hold values from 16 to 32, as said below
Outputs:
- weights: float32 [1024, 4096], P('lat', 'lon')
- residual: float32 [1024, 4096], P('lat', 'lon')
Inputs may be any that keep to these rules, and one draw needn't show every extreme that they name: `halfwidth`: one of the two half-widths equals 32 in every draw.
All inputs are finite; a program needn't handle non-finite values. No bound on the sum of `valid` on one device may be relied on, other than what follows from the above.
Results may differ from a plain program's by a relative error of at most 0.024.
Values may be sent and summed in bfloat16 or wider, within the bound.
No kernel may reach another device: no remote copies, remote signals or barrier semaphores. Data moves between devices by JAX's collectives and lax.ppermute only.
A program may use at most 64 MiB of HBM per device.

v0:
```python
import jax
import jax.numpy as jnp
from jax import lax
from jax.sharding import PartitionSpec as P

HMAX = 32
ITERS = 3


def extended(cells, sides, width, closed):
    for axis, dim in sides:
        count = lax.axis_size(axis)
        ends = count if closed else count - 1
        head = lax.slice_in_dim(cells, 0, width, axis=dim)
        tail = lax.slice_in_dim(cells, cells.shape[dim] - width, cells.shape[dim], axis=dim)
        cells = jnp.concatenate(
            [
                lax.ppermute(tail, axis, [(i, (i + 1) % count) for i in range(ends)]),
                cells,
                lax.ppermute(head, axis, [((i + 1) % count, i) for i in range(ends)]),
            ],
            axis=dim,
        )
    return cells


def taper_band(half, width, pad):
    rows = jnp.arange(width + 2 * pad)[:, None]
    cols = jnp.arange(width)[None, :]
    offset = (rows - cols - pad).astype(jnp.float32)
    scale = half.astype(jnp.float32)
    ratio = offset / scale
    return jnp.where(jnp.abs(offset) <= scale, jnp.exp(-4.5 * ratio * ratio), 0.0).astype(
        jnp.bfloat16
    )


def residual_norm(vector):
    return lax.psum(jnp.sum(vector * vector), ("lon", "lat"))


def shards(ensemble, right_side, obs_error, valid, halfwidth):
    members, rows, cols = ensemble.shape
    band_lon = taper_band(halfwidth[0], cols, HMAX)
    band_lat = taper_band(halfwidth[1], rows, HMAX)
    maskf = valid.astype(jnp.float32)
    weights = jnp.zeros_like(right_side)
    residual = right_side
    direction = right_side
    norm_now = residual_norm(residual)
    for step in range(ITERS):
        masked = maskf * direction
        product = (ensemble * masked[None]).astype(jnp.bfloat16)
        wide = extended(product, (("lon", 2),), HMAX, True)
        first = jnp.einsum(
            "mai,ij->maj", wide, band_lon, preferred_element_type=jnp.float32
        ).astype(jnp.bfloat16)
        tall = extended(first, (("lat", 1),), HMAX, False)
        second = jnp.einsum("mic,ia->mac", tall, band_lat, preferred_element_type=jnp.float32)
        operate_total = jnp.sum(ensemble * second, axis=0)
        image = maskf * operate_total / (members - 1) + obs_error * direction
        alpha = norm_now / lax.psum(jnp.sum(direction * image), ("lon", "lat"))
        weights = weights + alpha * direction
        residual = residual - alpha * image
        norm_next = residual_norm(residual)
        direction = residual + norm_next / norm_now * direction
        norm_now = norm_next
    return (weights, residual)


def solution(mesh):
    in_specs = (P(None, "lat", "lon"), P("lat", "lon"), P("lat", "lon"), P("lat", "lon"), P())
    out_specs = (P("lat", "lon"), P("lat", "lon"))
    return jax.shard_map(shards, mesh=mesh, in_specs=in_specs, out_specs=out_specs, check_vma=False)
```

profile of v0, /device:TPU:1, one launch (start us, length us, event | category | flops | bytes accessed | tf_op | source)
XLA Modules:
  0.0 667.8 jit_solution(2289896047269255122)
XLA Ops:
  4.6 14.5 %collective-permute-start.1 = (bf16[64,64,32]{1,2,0:T(8,128)(2,1)}, bf16[64,64,32]{1,2,0:T(8,128)(2,1)S(1)}, u32[]{:S(2)}, u32[]{:S(2)}) collective-permute-start(bf16[64,64,32]{1,2,0:T(8,128)(2,1)} %copy.8), channel_id=1, source_target_pairs={{16,0},{32,16},{48,32},{64,48},{80,64},{96,80},{112,96},{128,112},... | collective-permute-start | bytes 786440 | tf_op jit(solution)/shard_map/ppermute | solution.py:20
  22.7 7.3 %collective-permute-done.1 = bf16[64,64,32]{1,2,0:T(8,128)(2,1)S(1)} collective-permute-done((bf16[64,64,32]{1,2,0:T(8,128)(2,1)}, bf16[64,64,32]{1,2,0:T(8,128)(2,1)S(1)}, u32[]{:S(2)}, u32[]{:S(2)}) %collective-permute-start.1) | collective-permute-done | bytes 262176 | tf_op jit(solution)/shard_map/ppermute | solution.py:20
  30.5 7.1 %collective-permute-done = bf16[64,64,32]{1,2,0:T(8,128)(2,1)} collective-permute-done((bf16[64,64,32]{1,2,0:T(8,128)(2,1)S(1)}, bf16[64,64,32]{1,2,0:T(8,128)(2,1)}, u32[]{:S(2)}, u32[]{:S(2)}) %collective-permute-start) | collective-permute-done | bytes 262176 | tf_op jit(solution)/shard_map/ppermute | solution.py:18
  40.5 4.1 collective-permute-start.2
  47.1 3.5 collective-permute-done.2
  50.7 8.2 %collective-permute-done.3 = bf16[64,32,128]{2,1,0:T(8,128)(2,1)S(1)} collective-permute-done((bf16[64,32,128]{2,1,0:T(8,128)(2,1)S(1)}, bf16[64,32,128]{2,1,0:T(8,128)(2,1)S(1)}, u32[]{:S(2)}, u32[]{:S(2)}) %collective-permute-start.3) | collective-permute-done | bytes 524320 | tf_op jit(solution)/shard_map/ppermute | solution.py:20
  60.4 99.6 %all-reduce = (f32[]{:T(128)}, f32[]{:T(128)}) all-reduce(f32[]{:T(128)} %get-tuple-element.3, f32[]{:T(128)} %get-tuple-element.2), channel_id=1, replica_groups=mesh['lon'=32,'lat'=16] {'lon','lat'}, use_global_device_ids=true, to_apply=%region_1.2 | all-reduce | flops 2 | bytes 16 | tf_op jit(solution)/shard_map/psum | solution.py:39
  161.9 99.6 %psum.44 = f32[]{:T(128)} all-reduce(f32[]{:T(128)} %multiply_reduce_fusion.3), channel_id=1, replica_groups=mesh['lon'=32,'lat'=16] {'lon','lat'}, use_global_device_ids=true, to_apply=%region_6.7 | all-reduce | flops 1 | bytes 8 | tf_op jit(solution)/shard_map/psum | solution.py:39
  266.9 3.7 collective-permute-start.5
  273.7 8.2 %collective-permute-done.5 = bf16[64,64,32]{1,2,0:T(8,128)(2,1)} collective-permute-done((bf16[64,64,32]{1,2,0:T(8,128)(2,1)}, bf16[64,64,32]{1,2,0:T(8,128)(2,1)}, u32[]{:S(2)}, u32[]{:S(2)}) %collective-permute-start.5) | collective-permute-done | bytes 262176 | tf_op jit(solution)/shard_map/ppermute | solution.py:20
  283.4 6.6 collective-permute-done.4
  292.5 2.5 fusion.51
  295.1 4.5 collective-permute-start.6
  301.5 4.2 collective-permute-done.6
  305.7 6.7 collective-permute-done.7
  313.6 98.9 %psum.45 = f32[]{:T(128)} all-reduce(f32[]{:T(128)} %multiply_reduce_fusion.2), channel_id=1, replica_groups=mesh['lon'=32,'lat'=16] {'lon','lat'}, use_global_device_ids=true, to_apply=%region_9.10 | all-reduce | flops 1 | bytes 8 | tf_op jit(solution)/shard_map/psum | solution.py:62
  414.4 99.9 %psum.46 = f32[]{:T(128)} all-reduce(f32[]{:T(128)} %multiply_reduce_fusion.1), channel_id=1, replica_groups=mesh['lon'=32,'lat'=16] {'lon','lat'}, use_global_device_ids=true, to_apply=%region_11.12 | all-reduce | flops 1 | bytes 8 | tf_op jit(solution)/shard_map/psum | solution.py:39
  519.8 3.7 collective-permute-start.9
  526.6 8.2 %collective-permute-done.9 = bf16[64,64,32]{1,2,0:T(8,128)(2,1)} collective-permute-done((bf16[64,64,32]{1,2,0:T(8,128)(2,1)}, bf16[64,64,32]{1,2,0:T(8,128)(2,1)}, u32[]{:S(2)}, u32[]{:S(2)}) %collective-permute-start.9) | collective-permute-done | bytes 262176 | tf_op jit(solution)/shard_map/ppermute | solution.py:20
  536.3 6.6 collective-permute-done.8
  547.9 5.2 collective-permute-start.10
  555.1 4.2 collective-permute-done.10
  559.2 6.7 %collective-permute-done.11 = bf16[64,32,128]{2,1,0:T(8,128)(2,1)S(1)} collective-permute-done((bf16[64,32,128]{2,1,0:T(8,128)(2,1)S(1)}, bf16[64,32,128]{2,1,0:T(8,128)(2,1)S(1)}, u32[]{:S(2)}, u32[]{:S(2)}) %collective-permute-start.11) | collective-permute-done | bytes 524320 | tf_op jit(solution)/shard_map/ppermute | solution.py:20
  567.0 98.8 %psum.47 = f32[]{:T(128)} all-reduce(f32[]{:T(128)} %multiply_reduce_fusion), channel_id=1, replica_groups=mesh['lon'=32,'lat'=16] {'lon','lat'}, use_global_device_ids=true, to_apply=%region_14.15 | all-reduce | flops 1 | bytes 8 | tf_op jit(solution)/shard_map/psum | solution.py:62
  (52 shorter events, 46.4 us)
Async XLA Ops:
  4.5 16.9 %copy-start.4 = (s32[2]{0:T(128)S(1)}, s32[2]{0:T(128)}, u32[]{:S(2)}) copy-start(s32[2]{0:T(128)} %param.9) | copy-start | bytes 28
  4.6 25.4 %collective-permute-start.1 = (bf16[64,64,32]{1,2,0:T(8,128)(2,1)}, bf16[64,64,32]{1,2,0:T(8,128)(2,1)S(1)}, u32[]{:S(2)}, u32[]{:S(2)}) collective-permute-start(bf16[64,64,32]{1,2,0:T(8,128)(2,1)} %copy.8), channel_id=1, source_target_pairs={{16,0},{32,16},{48,32},{64,48},{80,64},{96,80},{112,96},{128,112},... | collective-permute-start | bytes 786440 | tf_op jit(solution)/shard_map/ppermute | solution.py:20
  19.5 18.1 %collective-permute-start = (bf16[64,64,32]{1,2,0:T(8,128)(2,1)S(1)}, bf16[64,64,32]{1,2,0:T(8,128)(2,1)}, u32[]{:S(2)}, u32[]{:S(2)}) collective-permute-start(bf16[64,64,32]{1,2,0:T(8,128)(2,1)S(1)} %copy.7), channel_id=1, source_target_pairs={{0,16},{16,32},{32,48},{48,64},{64,80},{80,96},{96,112},{112,128},... | collective-permute-start | bytes 786440 | tf_op jit(solution)/shard_map/ppermute | solution.py:18
  40.4 18.5 %copy-start = (bf16[64,64,128]{2,1,0:T(8,128)(2,1)S(1)}, bf16[64,64,128]{2,1,0:T(8,128)(2,1)}, u32[]{:S(2)}) copy-start(bf16[64,64,128]{2,1,0:T(8,128)(2,1)} %param.5) | copy-start | bytes 3145732
  40.5 10.2 %collective-permute-start.2 = (bf16[64,32,128]{2,1,0:T(8,128)(2,1)S(1)}, bf16[64,32,128]{2,1,0:T(8,128)(2,1)S(1)}, u32[]{:S(2)}, u32[]{:S(2)}) collective-permute-start(bf16[64,32,128]{2,1,0:T(8,128)(2,1)S(1)} %get-tuple-element.14), channel_id=1, source_target_pairs={{0,1},{1,2},{2,3},{3,4},{4,5},{5,6},{6,7},{7,8},{8,9},{9,10},{10,1... | collective-permute-start | bytes 1572872 | tf_op jit(solution)/shard_map/ppermute | solution.py:18
  44.6 14.3 %collective-permute-start.3 = (bf16[64,32,128]{2,1,0:T(8,128)(2,1)S(1)}, bf16[64,32,128]{2,1,0:T(8,128)(2,1)S(1)}, u32[]{:S(2)}, u32[]{:S(2)}) collective-permute-start(bf16[64,32,128]{2,1,0:T(8,128)(2,1)S(1)} %get-tuple-element.15), channel_id=1, source_target_pairs={{1,0},{2,1},{3,2},{4,3},{5,4},{6,5},{7,6},{8,7},{9,8},{10,9},{11,1... | collective-permute-start | bytes 1572872 | tf_op jit(solution)/shard_map/ppermute | solution.py:20
  58.9 0.8 copy-start.1
  58.9 0.8 copy-start.2
  58.9 0.8 copy-start.3
  266.9 15.0 %collective-permute-start.5 = (bf16[64,64,32]{1,2,0:T(8,128)(2,1)}, bf16[64,64,32]{1,2,0:T(8,128)(2,1)}, u32[]{:S(2)}, u32[]{:S(2)}) collective-permute-start(bf16[64,64,32]{1,2,0:T(8,128)(2,1)} %copy.12), channel_id=1, source_target_pairs={{16,0},{32,16},{48,32},{64,48},{80,64},{96,80},{112,96},{128,112},... | collective-permute-start | bytes 786440 | tf_op jit(solution)/shard_map/ppermute | solution.py:20
  271.8 18.3 %collective-permute-start.4 = (bf16[64,64,32]{1,2,0:T(8,128)(2,1)}, bf16[64,64,32]{1,2,0:T(8,128)(2,1)}, u32[]{:S(2)}, u32[]{:S(2)}) collective-permute-start(bf16[64,64,32]{1,2,0:T(8,128)(2,1)} %copy.11), channel_id=1, source_target_pairs={{0,16},{16,32},{32,48},{48,64},{64,80},{80,96},{96,112},{112,128},... | collective-permute-start | bytes 786440 | tf_op jit(solution)/shard_map/ppermute | solution.py:18
  295.1 10.7 %collective-permute-start.6 = (bf16[64,32,128]{2,1,0:T(8,128)(2,1)S(1)}, bf16[64,32,128]{2,1,0:T(8,128)(2,1)S(1)}, u32[]{:S(2)}, u32[]{:S(2)}) collective-permute-start(bf16[64,32,128]{2,1,0:T(8,128)(2,1)S(1)} %get-tuple-element.10), channel_id=1, source_target_pairs={{0,1},{1,2},{2,3},{3,4},{4,5},{5,6},{6,7},{7,8},{8,9},{9,10},{10,1... | collective-permute-start | bytes 1572872 | tf_op jit(solution)/shard_map/ppermute | solution.py:18
  299.6 12.8 %collective-permute-start.7 = (bf16[64,32,128]{2,1,0:T(8,128)(2,1)S(1)}, bf16[64,32,128]{2,1,0:T(8,128)(2,1)S(1)}, u32[]{:S(2)}, u32[]{:S(2)}) collective-permute-start(bf16[64,32,128]{2,1,0:T(8,128)(2,1)S(1)} %get-tuple-element.11), channel_id=1, source_target_pairs={{1,0},{2,1},{3,2},{4,3},{5,4},{6,5},{7,6},{8,7},{9,8},{10,9},{11,1... | collective-permute-start | bytes 1572872 | tf_op jit(solution)/shard_map/ppermute | solution.py:20
  519.8 15.0 %collective-permute-start.9 = (bf16[64,64,32]{1,2,0:T(8,128)(2,1)}, bf16[64,64,32]{1,2,0:T(8,128)(2,1)}, u32[]{:S(2)}, u32[]{:S(2)}) collective-permute-start(bf16[64,64,32]{1,2,0:T(8,128)(2,1)} %copy.16), channel_id=1, source_target_pairs={{16,0},{32,16},{48,32},{64,48},{80,64},{96,80},{112,96},{128,112},... | collective-permute-start | bytes 786440 | tf_op jit(solution)/shard_map/ppermute | solution.py:20
  524.7 18.3 %collective-permute-start.8 = (bf16[64,64,32]{1,2,0:T(8,128)(2,1)}, bf16[64,64,32]{1,2,0:T(8,128)(2,1)}, u32[]{:S(2)}, u32[]{:S(2)}) collective-permute-start(bf16[64,64,32]{1,2,0:T(8,128)(2,1)} %copy.15), channel_id=1, source_target_pairs={{0,16},{16,32},{32,48},{48,64},{64,80},{80,96},{96,112},{112,128},... | collective-permute-start | bytes 786440 | tf_op jit(solution)/shard_map/ppermute | solution.py:18
  547.9 11.3 %collective-permute-start.10 = (bf16[64,32,128]{2,1,0:T(8,128)(2,1)S(1)}, bf16[64,32,128]{2,1,0:T(8,128)(2,1)S(1)}, u32[]{:S(2)}, u32[]{:S(2)}) collective-permute-start(bf16[64,32,128]{2,1,0:T(8,128)(2,1)S(1)} %get-tuple-element.6), channel_id=1, source_target_pairs={{0,1},{1,2},{2,3},{3,4},{4,5},{5,6},{6,7},{7,8},{8,9},{9,10},{10,1... | collective-permute-start | bytes 1572872 | tf_op jit(solution)/shard_map/ppermute | solution.py:18
  553.1 12.8 %collective-permute-start.11 = (bf16[64,32,128]{2,1,0:T(8,128)(2,1)S(1)}, bf16[64,32,128]{2,1,0:T(8,128)(2,1)S(1)}, u32[]{:S(2)}, u32[]{:S(2)}) collective-permute-start(bf16[64,32,128]{2,1,0:T(8,128)(2,1)S(1)} %get-tuple-element.7), channel_id=1, source_target_pairs={{1,0},{2,1},{3,2},{4,3},{5,4},{6,5},{7,6},{8,7},{9,8},{10,9},{11,1... | collective-permute-start | bytes 1572872 | tf_op jit(solution)/shard_map/ppermute | solution.py:20
where the time goes:
time: 669 us; the launch traced here: 668 us
  blocking collectives  497 us (74%)
  waiting for transfers between devices  77.7 us (12%)
  starting transfers between devices  47.2 us (7%)
  local copies, waits for them, and re-layouts  22.9 us (3%)
  between operations  8.68 us (1%)
  matrix products  7.68 us (1%)
  other arithmetic  6.91 us (1%)
    psum x3, blocking collectives, residual_norm(): return lax.psum(jnp.sum(vector * vector), ('lon', 'lat'))  299 us
    psum x2, blocking collectives, shards(): alpha = norm_now / lax.psum(jnp.sum(direction * image), ('lon', 'lat'))  198 us
    ppermute x6, waiting for transfers between devices, extended(): lax.ppermute(head, axis, [((i + 1) % count, i) for i in range(ends)])  45.4 us
    ppermute x6, waiting for transfers between devices, extended(): lax.ppermute(tail, axis, [(i, (i + 1) % count) for i in range(ends)])  32.3 us
    ppermute x6, starting transfers between devices, extended(): lax.ppermute(head, axis, [((i + 1) % count, i) for i in range(ends)])  27.7 us
    ppermute x6, starting transfers between devices, extended(): lax.ppermute(tail, axis, [(i, (i + 1) % count) for i in range(ends)])  19.6 us
  transfers between devices with their start and end apart: 12, of which 12 were waited for; matrix products, arithmetic and copies ran while one was open for 1% of the time, Pallas kernels for 0%

commit v1 on v0

v1 whole, which is shorter than its diff:
```python
import functools

import jax
import jax.numpy as jnp
from jax import lax
from jax.experimental import pallas as pl
from jax.experimental.pallas import tpu as pltpu
from jax.sharding import PartitionSpec as P

HMAX = 32
BLOCKS = 4
VMEM_LIMIT = 40 * 1024 * 1024


def shift(cells, axis, step, closed):
    count = lax.axis_size(axis)
    pairs = [(i, (i + step) % count) for i in range(count) if closed or 0 <= i + step < count]
    return lax.ppermute(cells, axis, pairs)


def taper_weight(offset, half):
    offset = offset.astype(jnp.float32)
    scale = half.astype(jnp.float32)
    ratio = offset / scale
    return jnp.where(jnp.abs(offset) <= scale, jnp.exp(-4.5 * ratio * ratio), 0.0).astype(
        jnp.bfloat16
    )


def lon_bands(half, cols):
    lane = jnp.arange(cols)
    strip = jnp.where(lane % 64 < 32, lane % 64 - 32, cols + lane % 64 - 32)
    source = jnp.concatenate([lane, strip])
    offset = source[:, None] - lane[None, :]
    weight = taper_weight(offset, half)
    member = jnp.concatenate([jnp.full((cols,), -1), lane // 64])
    pair = jnp.arange(2)
    keep = (member[None, :] == -1) | (member[None, :] == pair[:, None])
    return jnp.where(keep[:, :, None], weight[None], jnp.zeros((), jnp.bfloat16))


def lat_band(half, rows):
    row = jnp.arange(rows)
    halo = jnp.arange(HMAX)
    source = jnp.concatenate([row, halo - HMAX, rows + halo])
    return taper_weight(source[None, :] - row[:, None], half)


def split3(x):
    hi = x.astype(jnp.bfloat16)
    rest = x - hi.astype(jnp.float32)
    mid = rest.astype(jnp.bfloat16)
    low = (rest - mid.astype(jnp.float32)).astype(jnp.bfloat16)
    return hi, mid, low


def join3(ref, first):
    parts = [ref[first + k].astype(jnp.float32) for k in range(3)]
    return parts[0] + parts[1] + parts[2]


def lanes(shape):
    return lax.broadcasted_iota(jnp.int32, shape, len(shape) - 1)


def edge_tiles(q):
    lane = lanes(q.shape)
    right = jnp.where(lane >= 96, q, 0.0)
    right = right + pltpu.roll(right, 64, 1)
    right = right + pltpu.roll(right, 32, 1)
    left = jnp.where(lane < 32, q, 0.0)
    left = left + pltpu.roll(left, 64, 1)
    left = left + pltpu.roll(left, 32, 1)
    return right, left


def pack_kernel(ens, right_side, valid, east, west, south, north):
    members, rows, cols = ens.shape
    source = lax.broadcasted_iota(jnp.int32, (4 * cols, 2 * cols), 0)
    target = lax.broadcasted_iota(jnp.int32, (4 * cols, 2 * cols), 1)
    lane = target % cols
    wanted = (lane // 32) * cols + lane % 32 + jnp.where(target < cols, 96, 0)
    select = jnp.where(source == wanted, 1.0, 0.0).astype(jnp.bfloat16)
    for i in range(members // 4):
        quad = jnp.concatenate([ens[4 * i + g] for g in range(4)], axis=1)
        both = jnp.dot(quad, select, preferred_element_type=jnp.float32).astype(jnp.bfloat16)
        east[i] = both[:, :cols]
        west[i] = both[:, cols:]
    q = valid[...].astype(jnp.float32) * right_side[...]
    right, left = edge_tiles(q)
    for k, part in enumerate(split3(right)):
        east[members // 4 + k] = part
    for k, part in enumerate(split3(left)):
        west[members // 4 + k] = part
    south[0:members] = ens[:, rows - HMAX :, :]
    north[0:members] = ens[:, :HMAX, :]
    for k, part in enumerate(split3(q)):
        south[members + k] = part[rows - HMAX :]
        north[members + k] = part[:HMAX]


def sides_kernel(from_west, from_east, sides, q_sides, south, north):
    planes, rows, cols = sides.shape
    quads = planes // 2
    source = lax.broadcasted_iota(jnp.int32, (2 * cols, 2 * cols), 0)
    target = lax.broadcasted_iota(jnp.int32, (2 * cols, 2 * cols), 1)
    wanted = (target // 64) * 32 + target % 32 + jnp.where(target % 64 < 32, 0, cols)
    select = jnp.where(source == wanted, 1.0, 0.0).astype(jnp.bfloat16)
    for i in range(quads):
        pair = jnp.concatenate([from_west[i], from_east[i]], axis=1)
        both = jnp.dot(pair, select, preferred_element_type=jnp.float32).astype(jnp.bfloat16)
        for k in range(2):
            part = both[:, k * cols : (k + 1) * cols]
            sides[2 * i + k] = part
            south[2 * i + k] = part[rows - HMAX :]
            north[2 * i + k] = part[:HMAX]
    left = lanes((rows, cols)) % 64 < 32
    q = jnp.where(left, join3(from_west, quads), join3(from_east, quads))
    q_sides[...] = q
    for k, part in enumerate(split3(q)):
        south[planes + k] = part[rows - HMAX :]
        north[planes + k] = part[:HMAX]


def merge_kernel(vector, valid, from_west, from_east, q_sides, south, north):
    rows, cols = vector.shape
    q = valid[...].astype(jnp.float32) * vector[...]
    side = jnp.where(lanes((rows, cols)) % 64 < 32, from_west[...], from_east[...])
    q_sides[...] = side
    south[0:HMAX] = q[rows - HMAX :]
    south[HMAX:] = side[rows - HMAX :]
    north[0:HMAX] = q[:HMAX]
    north[HMAX:] = side[:HMAX]


def gram_lanes(vectors):
    lane = lanes((1, 128))
    out = jnp.zeros((1, 128), jnp.float32)
    for k, (i, j) in enumerate(GRAM):
        out = jnp.where(lane == k, jnp.sum(vectors[i] * vectors[j], keepdims=True), out)
    return out


GRAM = [(0, 0), (0, 1), (0, 2), (0, 3), (1, 1), (1, 2), (1, 3), (2, 2), (2, 3)]


def high_low(x):
    high = x.astype(jnp.bfloat16)
    return high, (x - high.astype(jnp.float32)).astype(jnp.bfloat16)


def apply_kernel(
    step, members, vector, valid, obs_error, q_sides, north_q, south_q, ens, sides,
    north, north_sides, south, south_sides, lon_band, lat_weights, *rest,
):
    earlier, (out, east, west), total = rest[: step], rest[step:-1][:3], rest[-1]
    extra = rest[step:-1][3:]
    block = pl.program_id(0)
    rows, cols = vector.shape

    @pl.when(block == 0)
    def _():
        total[...] = jnp.zeros_like(total)

    q = valid[...].astype(jnp.float32) * vector[...]
    if step == 0:
        above, above_sides = join3(north_q, 0), join3(north_q, 3)
        below, below_sides = join3(south_q, 0), join3(south_q, 3)
    else:
        above, above_sides = north_q[:HMAX], north_q[HMAX:]
        below, below_sides = south_q[:HMAX], south_q[HMAX:]
    tall = jnp.concatenate([q, above, below], axis=0)
    tall_sides = jnp.concatenate([q_sides[...], above_sides, below_sides], axis=0)
    lat = lat_weights[...]
    lat2 = jnp.concatenate([lat, lat], axis=1)
    acc = total[...]
    for j in range(sides.shape[0]):
        plane = jnp.concatenate([sides[j], north_sides[j], south_sides[j]], axis=0)
        side_high, side_low = high_low(plane.astype(jnp.float32) * tall_sides)
        for k in range(2):
            m = 2 * j + k
            own = ens[m]
            anomaly = jnp.concatenate([own, north[m], south[m]], axis=0)
            high, low = high_low(anomaly.astype(jnp.float32) * tall)
            band = lon_band[k]
            first = jnp.dot(
                jnp.concatenate([high, side_high], axis=1), band,
                preferred_element_type=jnp.float32,
            ) + jnp.dot(
                jnp.concatenate([low, side_low], axis=1), band,
                preferred_element_type=jnp.float32,
            )
            second = jnp.dot(
                lat2, jnp.concatenate(high_low(first), axis=0),
                preferred_element_type=jnp.float32,
            )
            acc = acc + own.astype(jnp.float32) * second
    total[...] = acc

    @pl.when(block == pl.num_programs(0) - 1)
    def _():
        maskf = valid[...].astype(jnp.float32)
        image = maskf * acc / (members - 1) + obs_error[...] * vector[...]
        out[...] = image
        east[...], west[...] = edge_tiles(maskf * image)
        if step == 2:
            vectors = [ref[...] for ref in earlier] + [vector[...], image]
            extra[0][...] = jnp.broadcast_to(gram_lanes(vectors)[None], extra[0].shape)


def apply(step, members, vector, valid, obs_error, q_sides, north_q, south_q, ens, sides,
          north, north_sides, south, south_sides, lon_band, lat_weights, earlier=(), peers=0):
    rows, cols = vector.shape
    per = members // BLOCKS

    def whole(a):
        return pl.BlockSpec(a.shape, lambda b, n=a.ndim: (0,) * n)

    def part(count, height):
        return pl.BlockSpec((count, height, cols), lambda b: (b, 0, 0))

    field = jax.ShapeDtypeStruct((rows, cols), jnp.float32)
    outs = [field] * 3
    if step == 2:
        outs.append(jax.ShapeDtypeStruct((peers, 1, 128), jnp.float32))
    return pl.pallas_call(
        functools.partial(apply_kernel, step, members),
        grid=(BLOCKS,),
        in_specs=[
            whole(vector), whole(valid), whole(obs_error), whole(q_sides), whole(north_q),
            whole(south_q), part(per, rows), part(per // 2, rows), part(per, HMAX),
            part(per // 2, HMAX), part(per, HMAX), part(per // 2, HMAX), whole(lon_band),
            whole(lat_weights),
        ] + [whole(a) for a in earlier],
        out_specs=[whole(a) for a in outs],
        out_shape=outs,
        scratch_shapes=[pltpu.VMEM((rows, cols), jnp.float32)],
        compiler_params=pltpu.CompilerParams(vmem_limit_bytes=VMEM_LIMIT),
        name=f"apply_{step}",
    )(vector, valid, obs_error, q_sides, north_q, south_q, ens, sides, north, north_sides,
      south, south_sides, lon_band, lat_weights, *earlier)


def sum_kernel(parts, out):
    out[...] = jnp.broadcast_to(jnp.sum(parts[...], axis=0, keepdims=True), out.shape)


def solve_kernel(parts, v0, v1, v2, v3, weights, residual):
    sums = jnp.sum(parts[...], axis=0)
    lane = lanes(sums.shape)
    gram = {}
    for k, (i, j) in enumerate(GRAM):
        value = jnp.sum(jnp.where(lane == k, sums, 0.0), keepdims=True)
        gram[i, j] = gram[j, i] = value

    def inner(a, b):
        total = None
        for i, x in a.items():
            for j, y in b.items():
                term = x * y * gram[i, j]
                total = term if total is None else total + term
        return total

    def combine(a, scale, b):
        out = dict(a)
        for i, y in b.items():
            out[i] = out[i] + scale * y if i in out else scale * y
        return out

    one = jnp.ones((1, 1), jnp.float32)
    w, r, d = {}, {0: one}, {0: one}
    now = inner(r, r)
    for step in range(3):
        image = {i + 1: x for i, x in d.items()}
        alpha = now / inner(d, image)
        w = combine(w, alpha, d)
        r = combine(r, -alpha, image)
        if step < 2:
            later = inner(r, r)
            d = combine(r, later / now, d)
            now = later
    basis = [v0[...], v1[...], v2[...], v3[...]]
    weights[...] = w[0] * basis[0] + w[1] * basis[1] + w[2] * basis[2]
    residual[...] = r[0] * basis[0] + r[1] * basis[1] + r[2] * basis[2] + r[3] * basis[3]


def call(kernel, outs, *args):
    return pl.pallas_call(
        kernel,
        out_shape=outs,
        compiler_params=pltpu.CompilerParams(vmem_limit_bytes=VMEM_LIMIT),
        name=kernel.__name__,
    )(*args)


def shards(ensemble, right_side, obs_error, valid, halfwidth):
    members, rows, cols = ensemble.shape
    quads, planes = members // 4, members // 2
    bf16 = functools.partial(jax.ShapeDtypeStruct, dtype=jnp.bfloat16)
    f32 = functools.partial(jax.ShapeDtypeStruct, dtype=jnp.float32)
    lon_band = lon_bands(halfwidth[0], cols)
    lat_weights = lat_band(halfwidth[1], rows)

    east, west, south, north = call(
        pack_kernel,
        [bf16((quads + 3, rows, cols))] * 2 + [bf16((members + 3, HMAX, cols))] * 2,
        ensemble, right_side, valid,
    )
    from_west = shift(east, "lon", 1, True)
    from_east = shift(west, "lon", -1, True)
    from_north = shift(south, "lat", 1, False)
    from_south = shift(north, "lat", -1, False)
    sides, q_sides, south, north = call(
        sides_kernel,
        [bf16((planes, rows, cols)), f32((rows, cols))] + [bf16((planes + 3, HMAX, cols))] * 2,
        from_west, from_east,
    )
    north_sides = shift(south, "lat", 1, False)
    south_sides = shift(north, "lat", -1, False)
    north_q = jnp.concatenate([from_north[members:], north_sides[planes:]])
    south_q = jnp.concatenate([from_south[members:], south_sides[planes:]])

    vectors = [right_side]
    for step in range(3):
        out = apply(
            step, members, vectors[-1], valid, obs_error, q_sides, north_q, south_q, ensemble,
            sides, from_north, north_sides, from_south, south_sides, lon_band, lat_weights,
            vectors[:step], lax.axis_size("lat"),
        )
        vectors.append(out[0])
        if step < 2:
            left = shift(out[1], "lon", 1, True)
            right = shift(out[2], "lon", -1, True)
            q_sides, south, north = call(
                merge_kernel, [f32((rows, cols))] + [f32((2 * HMAX, cols))] * 2,
                out[0], valid, left, right,
            )
            north_q = shift(south, "lat", 1, False)
            south_q = shift(north, "lat", -1, False)
    parts = lax.all_to_all(out[3], "lat", 0, 0)
    parts = call(sum_kernel, f32((lax.axis_size("lon"), 1, 128)), parts)
    parts = lax.all_to_all(parts, "lon", 0, 0)
    return tuple(call(solve_kernel, [f32((rows, cols))] * 2, parts, *vectors))


def solution(mesh):
    in_specs = (P(None, "lat", "lon"), P("lat", "lon"), P("lat", "lon"), P("lat", "lon"), P())
    out_specs = (P("lat", "lon"), P("lat", "lon"))
    return jax.shard_map(shards, mesh=mesh, in_specs=in_specs, out_specs=out_specs, check_vma=False)
```

time: 669 us -> 156 us (0.23)
  blocking collectives: 497 us -> 34.1 us
  waiting for transfers between devices: 77.7 us -> 14.4 us
  Pallas kernels: 0 us -> 38.7 us
  local copies, waits for them, and re-layouts: 22.9 us -> 4.71 us
  starting transfers between devices: 47.2 us -> 60.3 us
  matrix products: 7.68 us -> 0 us
    psum x5 -> x0, blocking collectives: 497 us -> none  [the longest x3 299 us: residual_norm(): return lax.psum(jnp.sum(vector * vector), ('lon', 'lat'))]
    ppermute x12 -> x14, waiting for transfers between devices: 77.7 us -> 14.4 us  [shift(): return lax.ppermute(cells, axis, pairs)]
    pallas_call x0 -> x9, Pallas kernels: none -> 38.7 us  [the longest x3 36.4 us: apply(): pl.pallas_call(functools.partial(apply_kernel, step, members), grid=(BLOC...]
    all_to_all x0 -> x2, blocking collectives: none -> 34.1 us  [the longest x1 20.8 us: shards(): parts = lax.all_to_all(parts, 'lon', 0, 0)]
    ppermute x12 -> x14, starting transfers between devices: 47.2 us -> 60.3 us  [shift(): return lax.ppermute(cells, axis, pairs)]
    slice x13 -> x5, local copies, waits for them, and re-layouts: 12.8 us -> 0.6 us  [the longest x1 0.58 us: shards(): lat_weights = lat_band(halfwidth[1], rows)]
    ppermute x6 -> x0, local copies, waits for them, and re-layouts: 9.77 us -> none  [the longest x3 6.29 us: extended(): lax.ppermute(tail, axis, [(i, (i + 1) % count) for i in range(ends)])]
    dot_general x6 -> x0, matrix products: 7.68 us -> none  [the longest x3 6.3 us: shards(): jnp.einsum('mai,ij->maj', wide, band_lon, preferred_element_type=jnp.floa...]
  transfers between devices with their start and end apart: 12 -> 14, of which waited for: 12 -> 5; matrix products, arithmetic and copies ran while one was open for 1% -> 1% of each run, Pallas kernels for 0% -> 0%
where the time goes in v1:
time: 156 us; the launch traced here: 155 us
  starting transfers between devices  60.3 us (39%)
  Pallas kernels  38.7 us (25%)
  blocking collectives  34.1 us (22%)
  waiting for transfers between devices  14.4 us (9%)
  local copies, waits for them, and re-layouts  4.71 us (3%)
  between operations  2.31 us (1%)
    ppermute x14, starting transfers between devices, shift(): return lax.ppermute(cells, axis, pairs)  60.3 us
    pallas_call x3, Pallas kernels, apply(): pl.pallas_call(functools.partial(apply_kernel, step, members), grid=(BLOC...  36.4 us
    all_to_all x1, blocking collectives, shards(): parts = lax.all_to_all(parts, 'lon', 0, 0)  20.8 us
    ppermute x14, waiting for transfers between devices, shift(): return lax.ppermute(cells, axis, pairs)  14.4 us
    all_to_all x1, blocking collectives, shards(): parts = lax.all_to_all(out[3], 'lat', 0, 0)  13.3 us
    unnamed x12, local copies, waits for them, and re-layouts  4.1 us
  transfers between devices with their start and end apart: 14, of which 5 were waited for; matrix products, arithmetic and copies ran while one was open for 1% of the time, Pallas kernels for 0%

profile of v1, /device:TPU:1, one launch (start us, length us, event | category | flops | bytes accessed | tf_op | source)
XLA Modules:
  0.0 154.9 jit_solution(18172036702583649859)
XLA Ops:
  0.6 1.2 copy-done
  4.3 4.4 %collective-permute-start = (bf16[19,64,128]{2,1,0:T(8,128)(2,1)S(1)}, bf16[19,64,128]{2,1,0:T(8,128)(2,1)S(1)}, u32[]{:S(2)}, u32[]{:S(2)}) collective-permute-start(bf16[19,64,128]{2,1,0:T(8,128)(2,1)S(1)} %get-tuple-element.24), channel_id=1, source_target_pairs={{0,16},{16,32},{32,48},{48,64},{64,80},{80,96},{96,112},{112,128},... | collective-permute-start | bytes 933896 | tf_op jit(solution)/shard_map/ppermute | solution.py:18
  8.7 12.0 %collective-permute-start.1 = (bf16[19,64,128]{2,1,0:T(8,128)(2,1)S(1)}, bf16[19,64,128]{2,1,0:T(8,128)(2,1)S(1)}, u32[]{:S(2)}, u32[]{:S(2)}) collective-permute-start(bf16[19,64,128]{2,1,0:T(8,128)(2,1)S(1)} %get-tuple-element.25), channel_id=1, source_target_pairs={{0,496},{16,0},{32,16},{48,32},{64,48},{80,64},{96,80},{112,96},{1... | collective-permute-start | bytes 933896 | tf_op jit(solution)/shard_map/ppermute | solution.py:18
  20.6 2.9 %collective-permute-start.4 = (bf16[67,32,128]{2,1,0:T(8,128)(2,1)S(1)}, bf16[67,32,128]{2,1,0:T(8,128)(2,1)S(1)}, u32[]{:S(2)}, u32[]{:S(2)}) collective-permute-start(bf16[67,32,128]{2,1,0:T(8,128)(2,1)S(1)} %get-tuple-element.29), channel_id=1, source_target_pairs={{1,0},{2,1},{3,2},{4,3},{5,4},{6,5},{7,6},{8,7},{9,8},{10,9},{11,1... | collective-permute-start | bytes 1646600 | tf_op jit(solution)/shard_map/ppermute | solution.py:18
  23.5 2.7 %collective-permute-start.2 = (bf16[67,32,128]{2,1,0:T(8,128)(2,1)S(1)}, bf16[67,32,128]{2,1,0:T(8,128)(2,1)S(1)}, u32[]{:S(2)}, u32[]{:S(2)}) collective-permute-start(bf16[67,32,128]{2,1,0:T(8,128)(2,1)S(1)} %get-tuple-element.27), channel_id=1, source_target_pairs={{0,1},{1,2},{2,3},{3,4},{4,5},{5,6},{6,7},{7,8},{8,9},{9,10},{10,1... | collective-permute-start | bytes 1646600 | tf_op jit(solution)/shard_map/ppermute | solution.py:18
  29.6 1.9 %collective-permute-start.5 = (bf16[35,32,128]{2,1,0:T(8,128)(2,1)S(1)}, bf16[35,32,128]{2,1,0:T(8,128)(2,1)S(1)}, u32[]{:S(2)}, u32[]{:S(2)}) collective-permute-start(bf16[35,32,128]{2,1,0:T(8,128)(2,1)S(1)} %get-tuple-element.30), channel_id=1, source_target_pairs={{1,0},{2,1},{3,2},{4,3},{5,4},{6,5},{7,6},{8,7},{9,8},{10,9},{11,1... | collective-permute-start | bytes 860168 | tf_op jit(solution)/shard_map/ppermute | solution.py:18
  31.7 3.6 %collective-permute-start.3 = (bf16[35,32,128]{2,1,0:T(8,128)(2,1)S(1)}, bf16[35,32,128]{2,1,0:T(8,128)(2,1)S(1)}, u32[]{:S(2)}, u32[]{:S(2)}) collective-permute-start(bf16[35,32,128]{2,1,0:T(8,128)(2,1)S(1)} %get-tuple-element.28), channel_id=1, source_target_pairs={{0,1},{1,2},{2,3},{3,4},{4,5},{5,6},{6,7},{7,8},{8,9},{9,10},{10,1... | collective-permute-start | bytes 860168 | tf_op jit(solution)/shard_map/ppermute | solution.py:18
  35.4 5.4 %collective-permute-done.5.south_sides = bf16[35,32,128]{2,1,0:T(8,128)(2,1)S(1)} collective-permute-done((bf16[35,32,128]{2,1,0:T(8,128)(2,1)S(1)}, bf16[35,32,128]{2,1,0:T(8,128)(2,1)S(1)}, u32[]{:S(2)}, u32[]{:S(2)}) %collective-permute-start.5) | collective-permute-done | bytes 286752 | tf_op jit(solution)/shard_map/ppermute | solution.py:18
  41.5 11.9 %apply_0.1 = (f32[64,128]{1,0:T(8,128)S(1)}, f32[64,128]{1,0:T(8,128)S(1)}, f32[64,128]{1,0:T(8,128)S(1)}) custom-call(f32[64,128]{1,0:T(8,128)S(1)} %copy-done.3, s32[64,128]{1,0:T(8,128)S(1)} %copy-done.2, f32[64,128]{1,0:T(8,128)S(1)} %copy-done.4, f32[64,128]{1,0:T(8,128)S(1)} %get-tuple-element.26.q_sides, ...), custom_call_target="tpu_custom_call" | custom-call | tf_op jit(solution)/shard_map/apply_0/pallas_call | solution.py:226
  53.5 1.9 %collective-permute-start.6 = (f32[64,128]{1,0:T(8,128)S(1)}, f32[64,128]{1,0:T(8,128)S(1)}, u32[]{:S(2)}, u32[]{:S(2)}) collective-permute-start(f32[64,128]{1,0:T(8,128)S(1)} %get-tuple-element.33), channel_id=1, source_target_pairs={{0,16},{16,32},{32,48},{48,64},{64,80},{80,96},{96,112},{112,128},... | collective-permute-start | bytes 98312 | tf_op jit(solution)/shard_map/ppermute | solution.py:18
  55.4 11.4 %collective-permute-start.7 = (f32[64,128]{1,0:T(8,128)S(1)}, f32[64,128]{1,0:T(8,128)S(1)}, u32[]{:S(2)}, u32[]{:S(2)}) collective-permute-start(f32[64,128]{1,0:T(8,128)S(1)} %get-tuple-element.34), channel_id=1, source_target_pairs={{0,496},{16,0},{32,16},{48,32},{64,48},{80,64},{96,80},{112,96},{1... | collective-permute-start | bytes 98312 | tf_op jit(solution)/shard_map/ppermute | solution.py:18
  66.8 1.0 collective-permute-done.7.from_east
  67.8 2.0 %collective-permute-start.8 = (f32[64,128]{1,0:T(8,128)S(1)}, f32[64,128]{1,0:T(8,128)S(1)}, u32[]{:S(2)}, u32[]{:S(2)}) collective-permute-start(f32[64,128]{1,0:T(8,128)S(1)} %get-tuple-element.36), channel_id=1, source_target_pairs={{0,1},{1,2},{2,3},{3,4},{4,5},{5,6},{6,7},{7,8},{8,9},{9,10},{10,1... | collective-permute-start | bytes 98312 | tf_op jit(solution)/shard_map/ppermute | solution.py:18
  69.8 2.3 %collective-permute-start.9 = (f32[64,128]{1,0:T(8,128)S(1)}, f32[64,128]{1,0:T(8,128)S(1)}, u32[]{:S(2)}, u32[]{:S(2)}) collective-permute-start(f32[64,128]{1,0:T(8,128)S(1)} %get-tuple-element.37), channel_id=1, source_target_pairs={{1,0},{2,1},{3,2},{4,3},{5,4},{6,5},{7,6},{8,7},{9,8},{10,9},{11,1... | collective-permute-start | bytes 98312 | tf_op jit(solution)/shard_map/ppermute | solution.py:18
  72.1 3.1 %collective-permute-done.9.south_q = f32[64,128]{1,0:T(8,128)S(1)} collective-permute-done((f32[64,128]{1,0:T(8,128)S(1)}, f32[64,128]{1,0:T(8,128)S(1)}, u32[]{:S(2)}, u32[]{:S(2)}) %collective-permute-start.9) | collective-permute-done | bytes 32800 | tf_op jit(solution)/shard_map/ppermute | solution.py:18
  75.2 11.9 %apply_1.1 = (f32[64,128]{1,0:T(8,128)S(1)}, f32[64,128]{1,0:T(8,128)S(1)}, f32[64,128]{1,0:T(8,128)S(1)}) custom-call(f32[64,128]{1,0:T(8,128)S(1)} %get-tuple-element.32.vector.rest_1_.v1, s32[64,128]{1,0:T(8,128)S(1)} %copy-done.2, f32[64,128]{1,0:T(8,128)S(1)} %copy-done.4, f32[64,128]{1,0:T(8,128)S(1)} %get-tuple-element.35.q_sides, ...), custom_call_target="tpu_custom_call" | custom-call | tf_op jit(solution)/shard_map/apply_1/pallas_call | solution.py:226
  87.1 1.9 %collective-permute-start.10 = (f32[64,128]{1,0:T(8,128)S(1)}, f32[64,128]{1,0:T(8,128)S(1)}, u32[]{:S(2)}, u32[]{:S(2)}) collective-permute-start(f32[64,128]{1,0:T(8,128)S(1)} %get-tuple-element.39), channel_id=1, source_target_pairs={{0,16},{16,32},{32,48},{48,64},{64,80},{80,96},{96,112},{112,128},... | collective-permute-start | bytes 98312 | tf_op jit(solution)/shard_map/ppermute | solution.py:18
  89.1 8.1 %collective-permute-start.11 = (f32[64,128]{1,0:T(8,128)S(1)}, f32[64,128]{1,0:T(8,128)S(1)}, u32[]{:S(2)}, u32[]{:S(2)}) collective-permute-start(f32[64,128]{1,0:T(8,128)S(1)} %get-tuple-element.40), channel_id=1, source_target_pairs={{0,496},{16,0},{32,16},{48,32},{64,48},{80,64},{96,80},{112,96},{1... | collective-permute-start | bytes 98312 | tf_op jit(solution)/shard_map/ppermute | solution.py:18
  98.2 3.3 %collective-permute-start.12 = (f32[64,128]{1,0:T(8,128)S(1)}, f32[64,128]{1,0:T(8,128)S(1)}, u32[]{:S(2)}, u32[]{:S(2)}) collective-permute-start(f32[64,128]{1,0:T(8,128)S(1)} %get-tuple-element.42), channel_id=1, source_target_pairs={{0,1},{1,2},{2,3},{3,4},{4,5},{5,6},{6,7},{7,8},{8,9},{9,10},{10,1... | collective-permute-start | bytes 98312 | tf_op jit(solution)/shard_map/ppermute | solution.py:18
  101.5 1.9 %collective-permute-start.13 = (f32[64,128]{1,0:T(8,128)S(1)}, f32[64,128]{1,0:T(8,128)S(1)}, u32[]{:S(2)}, u32[]{:S(2)}) collective-permute-start(f32[64,128]{1,0:T(8,128)S(1)} %get-tuple-element.43), channel_id=1, source_target_pairs={{1,0},{2,1},{3,2},{4,3},{5,4},{6,5},{7,6},{8,7},{9,8},{10,9},{11,1... | collective-permute-start | bytes 98312 | tf_op jit(solution)/shard_map/ppermute | solution.py:18
  103.4 4.0 %collective-permute-done.13.south_q = f32[64,128]{1,0:T(8,128)S(1)} collective-permute-done((f32[64,128]{1,0:T(8,128)S(1)}, f32[64,128]{1,0:T(8,128)S(1)}, u32[]{:S(2)}, u32[]{:S(2)}) %collective-permute-start.13) | collective-permute-done | bytes 32800 | tf_op jit(solution)/shard_map/ppermute | solution.py:18
  107.4 12.6 %apply_2.1 = (f32[64,128]{1,0:T(8,128)S(1)}, f32[64,128]{1,0:T(8,128)}, f32[64,128]{1,0:T(8,128)}, f32[16,1,128]{2,1,0:T(1,128)S(1)}) custom-call(f32[64,128]{1,0:T(8,128)S(1)} %get-tuple-element.38.vector.v2, s32[64,128]{1,0:T(8,128)S(1)} %copy-done.2, f32[64,128]{1,0:T(8,128)S(1)} %copy-done.4, f32[64,128]{1,0:T(8,128)S(1)} %get-tuple-element.41.q_sides, ...), custom_call_target="tpu_custom_call" | custom-call | tf_op jit(solution)/shard_map/apply_2/pallas_call | solution.py:226
  119.9 13.3 %all_to_all.10.parts = f32[16,1,128]{2,1,0:T(1,128)S(1)} all-to-all(f32[16,1,128]{2,1,0:T(1,128)S(1)} %get-tuple-element.44), channel_id=1, replica_groups=mesh['lon'=32,'lat'=16] {'lat'}, dimensions={0} | all-to-all | bytes 16384 | tf_op jit(solution)/shard_map/all_to_all | solution.py:340
  133.2 20.8 %all_to_all.11.parts = f32[32,1,128]{2,1,0:T(1,128)S(1)} all-to-all(f32[32,1,128]{2,1,0:T(1,128)S(1)} %sum_kernel.1), channel_id=1, replica_groups=mesh['lon'=32,'lat'=16] {'lon'}, dimensions={0} | all-to-all | bytes 32768 | tf_op jit(solution)/shard_map/all_to_all | solution.py:342
  (47 shorter events, 7.2 us)
Async XLA Ops:
  0.6 1.2 copy-start
  1.9 0.8 copy-start.2
  2.6 0.8 copy-start.3
  3.4 37.4 %copy-start.1 = (bf16[64,64,128]{2,1,0:T(8,128)(2,1)S(1)}, bf16[64,64,128]{2,1,0:T(8,128)(2,1)}, u32[]{:S(2)}) copy-start(bf16[64,64,128]{2,1,0:T(8,128)(2,1)} %ens.7) | copy-start | bytes 3145732
  4.3 24.8 %collective-permute-start = (bf16[19,64,128]{2,1,0:T(8,128)(2,1)S(1)}, bf16[19,64,128]{2,1,0:T(8,128)(2,1)S(1)}, u32[]{:S(2)}, u32[]{:S(2)}) collective-permute-start(bf16[19,64,128]{2,1,0:T(8,128)(2,1)S(1)} %get-tuple-element.24), channel_id=1, source_target_pairs={{0,16},{16,32},{32,48},{48,64},{64,80},{80,96},{96,112},{112,128},... | collective-permute-start | bytes 933896 | tf_op jit(solution)/shard_map/ppermute | solution.py:18
  8.7 20.5 %collective-permute-start.1 = (bf16[19,64,128]{2,1,0:T(8,128)(2,1)S(1)}, bf16[19,64,128]{2,1,0:T(8,128)(2,1)S(1)}, u32[]{:S(2)}, u32[]{:S(2)}) collective-permute-start(bf16[19,64,128]{2,1,0:T(8,128)(2,1)S(1)} %get-tuple-element.25), channel_id=1, source_target_pairs={{0,496},{16,0},{32,16},{48,32},{64,48},{80,64},{96,80},{112,96},{1... | collective-permute-start | bytes 933896 | tf_op jit(solution)/shard_map/ppermute | solution.py:18
  20.6 14.7 %collective-permute-start.4 = (bf16[67,32,128]{2,1,0:T(8,128)(2,1)S(1)}, bf16[67,32,128]{2,1,0:T(8,128)(2,1)S(1)}, u32[]{:S(2)}, u32[]{:S(2)}) collective-permute-start(bf16[67,32,128]{2,1,0:T(8,128)(2,1)S(1)} %get-tuple-element.29), channel_id=1, source_target_pairs={{1,0},{2,1},{3,2},{4,3},{5,4},{6,5},{7,6},{8,7},{9,8},{10,9},{11,1... | collective-permute-start | bytes 1646600 | tf_op jit(solution)/shard_map/ppermute | solution.py:18
  23.5 11.9 %collective-permute-start.2 = (bf16[67,32,128]{2,1,0:T(8,128)(2,1)S(1)}, bf16[67,32,128]{2,1,0:T(8,128)(2,1)S(1)}, u32[]{:S(2)}, u32[]{:S(2)}) collective-permute-start(bf16[67,32,128]{2,1,0:T(8,128)(2,1)S(1)} %get-tuple-element.27), channel_id=1, source_target_pairs={{0,1},{1,2},{2,3},{3,4},{4,5},{5,6},{6,7},{7,8},{8,9},{9,10},{10,1... | collective-permute-start | bytes 1646600 | tf_op jit(solution)/shard_map/ppermute | solution.py:18
  26.2 0.7 copy-start.5
  29.6 11.1 %collective-permute-start.5 = (bf16[35,32,128]{2,1,0:T(8,128)(2,1)S(1)}, bf16[35,32,128]{2,1,0:T(8,128)(2,1)S(1)}, u32[]{:S(2)}, u32[]{:S(2)}) collective-permute-start(bf16[35,32,128]{2,1,0:T(8,128)(2,1)S(1)} %get-tuple-element.30), channel_id=1, source_target_pairs={{1,0},{2,1},{3,2},{4,3},{5,4},{6,5},{7,6},{8,7},{9,8},{10,9},{11,1... | collective-permute-start | bytes 860168 | tf_op jit(solution)/shard_map/ppermute | solution.py:18
  31.7 9.1 %collective-permute-start.3 = (bf16[35,32,128]{2,1,0:T(8,128)(2,1)S(1)}, bf16[35,32,128]{2,1,0:T(8,128)(2,1)S(1)}, u32[]{:S(2)}, u32[]{:S(2)}) collective-permute-start(bf16[35,32,128]{2,1,0:T(8,128)(2,1)S(1)} %get-tuple-element.28), channel_id=1, source_target_pairs={{0,1},{1,2},{2,3},{3,4},{4,5},{5,6},{6,7},{7,8},{8,9},{9,10},{10,1... | collective-permute-start | bytes 860168 | tf_op jit(solution)/shard_map/ppermute | solution.py:18
  40.8 0.8 copy-start.4
  53.5 13.3 %collective-permute-start.6 = (f32[64,128]{1,0:T(8,128)S(1)}, f32[64,128]{1,0:T(8,128)S(1)}, u32[]{:S(2)}, u32[]{:S(2)}) collective-permute-start(f32[64,128]{1,0:T(8,128)S(1)} %get-tuple-element.33), channel_id=1, source_target_pairs={{0,16},{16,32},{32,48},{48,64},{64,80},{80,96},{96,112},{112,128},... | collective-permute-start | bytes 98312 | tf_op jit(solution)/shard_map/ppermute | solution.py:18
  55.4 12.4 %collective-permute-start.7 = (f32[64,128]{1,0:T(8,128)S(1)}, f32[64,128]{1,0:T(8,128)S(1)}, u32[]{:S(2)}, u32[]{:S(2)}) collective-permute-start(f32[64,128]{1,0:T(8,128)S(1)} %get-tuple-element.34), channel_id=1, source_target_pairs={{0,496},{16,0},{32,16},{48,32},{64,48},{80,64},{96,80},{112,96},{1... | collective-permute-start | bytes 98312 | tf_op jit(solution)/shard_map/ppermute | solution.py:18
  67.8 4.3 %collective-permute-start.8 = (f32[64,128]{1,0:T(8,128)S(1)}, f32[64,128]{1,0:T(8,128)S(1)}, u32[]{:S(2)}, u32[]{:S(2)}) collective-permute-start(f32[64,128]{1,0:T(8,128)S(1)} %get-tuple-element.36), channel_id=1, source_target_pairs={{0,1},{1,2},{2,3},{3,4},{4,5},{5,6},{6,7},{7,8},{8,9},{9,10},{10,1... | collective-permute-start | bytes 98312 | tf_op jit(solution)/shard_map/ppermute | solution.py:18
  69.8 5.4 %collective-permute-start.9 = (f32[64,128]{1,0:T(8,128)S(1)}, f32[64,128]{1,0:T(8,128)S(1)}, u32[]{:S(2)}, u32[]{:S(2)}) collective-permute-start(f32[64,128]{1,0:T(8,128)S(1)} %get-tuple-element.37), channel_id=1, source_target_pairs={{1,0},{2,1},{3,2},{4,3},{5,4},{6,5},{7,6},{8,7},{9,8},{10,9},{11,1... | collective-permute-start | bytes 98312 | tf_op jit(solution)/shard_map/ppermute | solution.py:18
  87.1 10.0 %collective-permute-start.10 = (f32[64,128]{1,0:T(8,128)S(1)}, f32[64,128]{1,0:T(8,128)S(1)}, u32[]{:S(2)}, u32[]{:S(2)}) collective-permute-start(f32[64,128]{1,0:T(8,128)S(1)} %get-tuple-element.39), channel_id=1, source_target_pairs={{0,16},{16,32},{32,48},{48,64},{64,80},{80,96},{96,112},{112,128},... | collective-permute-start | bytes 98312 | tf_op jit(solution)/shard_map/ppermute | solution.py:18
  89.1 9.1 %collective-permute-start.11 = (f32[64,128]{1,0:T(8,128)S(1)}, f32[64,128]{1,0:T(8,128)S(1)}, u32[]{:S(2)}, u32[]{:S(2)}) collective-permute-start(f32[64,128]{1,0:T(8,128)S(1)} %get-tuple-element.40), channel_id=1, source_target_pairs={{0,496},{16,0},{32,16},{48,32},{64,48},{80,64},{96,80},{112,96},{1... | collective-permute-start | bytes 98312 | tf_op jit(solution)/shard_map/ppermute | solution.py:18
  98.2 5.2 %collective-permute-start.12 = (f32[64,128]{1,0:T(8,128)S(1)}, f32[64,128]{1,0:T(8,128)S(1)}, u32[]{:S(2)}, u32[]{:S(2)}) collective-permute-start(f32[64,128]{1,0:T(8,128)S(1)} %get-tuple-element.42), channel_id=1, source_target_pairs={{0,1},{1,2},{2,3},{3,4},{4,5},{5,6},{6,7},{7,8},{8,9},{9,10},{10,1... | collective-permute-start | bytes 98312 | tf_op jit(solution)/shard_map/ppermute | solution.py:18
  101.5 5.9 %collective-permute-start.13 = (f32[64,128]{1,0:T(8,128)S(1)}, f32[64,128]{1,0:T(8,128)S(1)}, u32[]{:S(2)}, u32[]{:S(2)}) collective-permute-start(f32[64,128]{1,0:T(8,128)S(1)} %get-tuple-element.43), channel_id=1, source_target_pairs={{1,0},{2,1},{3,2},{4,3},{5,4},{6,5},{7,6},{8,7},{9,8},{10,9},{11,1... | collective-permute-start | bytes 98312 | tf_op jit(solution)/shard_map/ppermute | solution.py:18

commit v2 on v1

--- a/solution.py
+++ b/solution.py
@@ -8,7 +8,7 @@
 from jax.sharding import PartitionSpec as P
 
 HMAX = 32
-BLOCKS = 4
+BLOCKS = 1
 VMEM_LIMIT = 40 * 1024 * 1024
 
 
@@ -174,27 +174,29 @@
     lat = lat_weights[...]
     lat2 = jnp.concatenate([lat, lat], axis=1)
     acc = total[...]
-    for j in range(sides.shape[0]):
+    n = sides.shape[0]
+    own_band = lon_band[0][:cols]
+    own_band2 = jnp.concatenate([own_band, own_band], axis=0)
+    side_band = jnp.concatenate([lon_band[0][cols:], lon_band[1][cols:]], axis=1)
+    side_band2 = jnp.concatenate([side_band, side_band], axis=0)
+    lo_list, hi_list = [], []
+    for j in range(n):
         plane = jnp.concatenate([sides[j], north_sides[j], south_sides[j]], axis=0)
-        side_high, side_low = high_low(plane.astype(jnp.float32) * tall_sides)
+        hi_list.append(jnp.concatenate(high_low(plane.astype(jnp.float32) * tall_sides), axis=1))
+    side = jnp.dot(jnp.concatenate(hi_list, axis=0), side_band2, preferred_element_type=jnp.float32)
+    for m in range(2 * n):
+        anomaly = jnp.concatenate([ens[m], north[m], south[m]], axis=0)
+        lo_list.append(jnp.concatenate(high_low(anomaly.astype(jnp.float32) * tall), axis=1))
+    main = jnp.dot(jnp.concatenate(lo_list, axis=0), own_band2, preferred_element_type=jnp.float32)
+    for j in range(n):
+        cs = []
         for k in range(2):
             m = 2 * j + k
-            own = ens[m]
-            anomaly = jnp.concatenate([own, north[m], south[m]], axis=0)
-            high, low = high_low(anomaly.astype(jnp.float32) * tall)
-            band = lon_band[k]
-            first = jnp.dot(
-                jnp.concatenate([high, side_high], axis=1), band,
-                preferred_element_type=jnp.float32,
-            ) + jnp.dot(
-                jnp.concatenate([low, side_low], axis=1), band,
-                preferred_element_type=jnp.float32,
-            )
-            second = jnp.dot(
-                lat2, jnp.concatenate(high_low(first), axis=0),
-                preferred_element_type=jnp.float32,
-            )
-            acc = acc + own.astype(jnp.float32) * second
+            first = main[128 * m : 128 * m + 128] + side[128 * j : 128 * j + 128, 128 * k : 128 * k + 128]
+            cs.append(jnp.concatenate(high_low(first), axis=0))
+        second = jnp.dot(lat2, jnp.concatenate(cs, axis=1), preferred_element_type=jnp.float32)
+        for k in range(2):
+            acc = acc + ens[2 * j + k].astype(jnp.float32) * second[:, 128 * k : 128 * k + 128]
     total[...] = acc
 
     @pl.when(block == pl.num_programs(0) - 1)

time: 156 us -> 128 us (0.82)
  Pallas kernels: 38.7 us -> 11.5 us
    pallas_call x3, Pallas kernels: 36.4 us -> 9.2 us  [apply(): pl.pallas_call(functools.partial(apply_kernel, step, members), grid=(BLOC...]
where the time goes in v2:
time: 128 us
  starting transfers between devices  60.3 us (47%)
  blocking collectives  34.1 us (27%)
  waiting for transfers between devices  14.4 us (11%)
  Pallas kernels  11.5 us (9%)
  local copies, waits for them, and re-layouts  4.71 us (4%)
  between operations  2.31 us (2%)
    ppermute x14, starting transfers between devices, shift(): return lax.ppermute(cells, axis, pairs)  60.3 us
    all_to_all x1, blocking collectives, shards(): parts = lax.all_to_all(parts, 'lon', 0, 0)  20.8 us
    ppermute x14, waiting for transfers between devices, shift(): return lax.ppermute(cells, axis, pairs)  14.4 us
    all_to_all x1, blocking collectives, shards(): parts = lax.all_to_all(out[3], 'lat', 0, 0)  13.3 us
    pallas_call x3, Pallas kernels, apply(): pl.pallas_call(functools.partial(apply_kernel, step, members), grid=(BLOC...  9.2 us
    unnamed x12, local copies, waits for them, and re-layouts  4.1 us
  transfers between devices with their start and end apart: 14, of which 5 were waited for; matrix products, arithmetic and copies ran while one was open for 1% of the time, Pallas kernels for 0%

profile of v2, /device:TPU:1, one launch (start us, length us, event | category | flops | bytes accessed | tf_op | source)
XLA Modules:
  0.0 127.7 jit_solution(16450977280201673775)
XLA Ops:
  0.6 1.2 copy-done
  4.3 4.4 %collective-permute-start = (bf16[19,64,128]{2,1,0:T(8,128)(2,1)S(1)}, bf16[19,64,128]{2,1,0:T(8,128)(2,1)S(1)}, u32[]{:S(2)}, u32[]{:S(2)}) collective-permute-start(bf16[19,64,128]{2,1,0:T(8,128)(2,1)S(1)} %get-tuple-element.24), channel_id=1, source_target_pairs={{0,16},{16,32},{32,48},{48,64},{64,80},{80,96},{96,112},{112,128},... | collective-permute-start | bytes 933896 | tf_op jit(solution)/shard_map/ppermute | solution.py:18
  8.7 12.0 %collective-permute-start.1 = (bf16[19,64,128]{2,1,0:T(8,128)(2,1)S(1)}, bf16[19,64,128]{2,1,0:T(8,128)(2,1)S(1)}, u32[]{:S(2)}, u32[]{:S(2)}) collective-permute-start(bf16[19,64,128]{2,1,0:T(8,128)(2,1)S(1)} %get-tuple-element.25), channel_id=1, source_target_pairs={{0,496},{16,0},{32,16},{48,32},{64,48},{80,64},{96,80},{112,96},{1... | collective-permute-start | bytes 933896 | tf_op jit(solution)/shard_map/ppermute | solution.py:18
  20.6 2.9 %collective-permute-start.4 = (bf16[67,32,128]{2,1,0:T(8,128)(2,1)S(1)}, bf16[67,32,128]{2,1,0:T(8,128)(2,1)S(1)}, u32[]{:S(2)}, u32[]{:S(2)}) collective-permute-start(bf16[67,32,128]{2,1,0:T(8,128)(2,1)S(1)} %get-tuple-element.29), channel_id=1, source_target_pairs={{1,0},{2,1},{3,2},{4,3},{5,4},{6,5},{7,6},{8,7},{9,8},{10,9},{11,1... | collective-permute-start | bytes 1646600 | tf_op jit(solution)/shard_map/ppermute | solution.py:18
  23.5 2.7 %collective-permute-start.2 = (bf16[67,32,128]{2,1,0:T(8,128)(2,1)S(1)}, bf16[67,32,128]{2,1,0:T(8,128)(2,1)S(1)}, u32[]{:S(2)}, u32[]{:S(2)}) collective-permute-start(bf16[67,32,128]{2,1,0:T(8,128)(2,1)S(1)} %get-tuple-element.27), channel_id=1, source_target_pairs={{0,1},{1,2},{2,3},{3,4},{4,5},{5,6},{6,7},{7,8},{8,9},{9,10},{10,1... | collective-permute-start | bytes 1646600 | tf_op jit(solution)/shard_map/ppermute | solution.py:18
  29.6 1.9 %collective-permute-start.5 = (bf16[35,32,128]{2,1,0:T(8,128)(2,1)S(1)}, bf16[35,32,128]{2,1,0:T(8,128)(2,1)S(1)}, u32[]{:S(2)}, u32[]{:S(2)}) collective-permute-start(bf16[35,32,128]{2,1,0:T(8,128)(2,1)S(1)} %get-tuple-element.30), channel_id=1, source_target_pairs={{1,0},{2,1},{3,2},{4,3},{5,4},{6,5},{7,6},{8,7},{9,8},{10,9},{11,1... | collective-permute-start | bytes 860168 | tf_op jit(solution)/shard_map/ppermute | solution.py:18
  31.7 3.6 %collective-permute-start.3 = (bf16[35,32,128]{2,1,0:T(8,128)(2,1)S(1)}, bf16[35,32,128]{2,1,0:T(8,128)(2,1)S(1)}, u32[]{:S(2)}, u32[]{:S(2)}) collective-permute-start(bf16[35,32,128]{2,1,0:T(8,128)(2,1)S(1)} %get-tuple-element.28), channel_id=1, source_target_pairs={{0,1},{1,2},{2,3},{3,4},{4,5},{5,6},{6,7},{7,8},{8,9},{9,10},{10,1... | collective-permute-start | bytes 860168 | tf_op jit(solution)/shard_map/ppermute | solution.py:18
  35.4 5.4 %collective-permute-done.5.south_sides = bf16[35,32,128]{2,1,0:T(8,128)(2,1)S(1)} collective-permute-done((bf16[35,32,128]{2,1,0:T(8,128)(2,1)S(1)}, bf16[35,32,128]{2,1,0:T(8,128)(2,1)S(1)}, u32[]{:S(2)}, u32[]{:S(2)}) %collective-permute-start.5) | collective-permute-done | bytes 286752 | tf_op jit(solution)/shard_map/ppermute | solution.py:18
  41.5 2.8 %apply_0.1 = (f32[64,128]{1,0:T(8,128)S(1)}, f32[64,128]{1,0:T(8,128)S(1)}, f32[64,128]{1,0:T(8,128)S(1)}) custom-call(f32[64,128]{1,0:T(8,128)S(1)} %copy-done.3, s32[64,128]{1,0:T(8,128)S(1)} %copy-done.2, f32[64,128]{1,0:T(8,128)S(1)} %copy-done.4, f32[64,128]{1,0:T(8,128)S(1)} %get-tuple-element.26.q_sides, ...), custom_call_target="tpu_custom_call" | custom-call | tf_op jit(solution)/shard_map/apply_0/pallas_call | solution.py:228
  44.4 1.9 %collective-permute-start.6 = (f32[64,128]{1,0:T(8,128)S(1)}, f32[64,128]{1,0:T(8,128)S(1)}, u32[]{:S(2)}, u32[]{:S(2)}) collective-permute-start(f32[64,128]{1,0:T(8,128)S(1)} %get-tuple-element.33), channel_id=1, source_target_pairs={{0,16},{16,32},{32,48},{48,64},{64,80},{80,96},{96,112},{112,128},... | collective-permute-start | bytes 98312 | tf_op jit(solution)/shard_map/ppermute | solution.py:18
  46.3 11.4 %collective-permute-start.7 = (f32[64,128]{1,0:T(8,128)S(1)}, f32[64,128]{1,0:T(8,128)S(1)}, u32[]{:S(2)}, u32[]{:S(2)}) collective-permute-start(f32[64,128]{1,0:T(8,128)S(1)} %get-tuple-element.34), channel_id=1, source_target_pairs={{0,496},{16,0},{32,16},{48,32},{64,48},{80,64},{96,80},{112,96},{1... | collective-permute-start | bytes 98312 | tf_op jit(solution)/shard_map/ppermute | solution.py:18
  57.7 1.0 collective-permute-done.7.from_east
  58.7 2.0 %collective-permute-start.8 = (f32[64,128]{1,0:T(8,128)S(1)}, f32[64,128]{1,0:T(8,128)S(1)}, u32[]{:S(2)}, u32[]{:S(2)}) collective-permute-start(f32[64,128]{1,0:T(8,128)S(1)} %get-tuple-element.36), channel_id=1, source_target_pairs={{0,1},{1,2},{2,3},{3,4},{4,5},{5,6},{6,7},{7,8},{8,9},{9,10},{10,1... | collective-permute-start | bytes 98312 | tf_op jit(solution)/shard_map/ppermute | solution.py:18
  60.7 2.3 %collective-permute-start.9 = (f32[64,128]{1,0:T(8,128)S(1)}, f32[64,128]{1,0:T(8,128)S(1)}, u32[]{:S(2)}, u32[]{:S(2)}) collective-permute-start(f32[64,128]{1,0:T(8,128)S(1)} %get-tuple-element.37), channel_id=1, source_target_pairs={{1,0},{2,1},{3,2},{4,3},{5,4},{6,5},{7,6},{8,7},{9,8},{10,9},{11,1... | collective-permute-start | bytes 98312 | tf_op jit(solution)/shard_map/ppermute | solution.py:18
  63.1 3.1 %collective-permute-done.9.south_q = f32[64,128]{1,0:T(8,128)S(1)} collective-permute-done((f32[64,128]{1,0:T(8,128)S(1)}, f32[64,128]{1,0:T(8,128)S(1)}, u32[]{:S(2)}, u32[]{:S(2)}) %collective-permute-start.9) | collective-permute-done | bytes 32800 | tf_op jit(solution)/shard_map/ppermute | solution.py:18
  66.1 2.8 %apply_1.1 = (f32[64,128]{1,0:T(8,128)S(1)}, f32[64,128]{1,0:T(8,128)S(1)}, f32[64,128]{1,0:T(8,128)S(1)}) custom-call(f32[64,128]{1,0:T(8,128)S(1)} %get-tuple-element.32.vector.rest_1_.v1, s32[64,128]{1,0:T(8,128)S(1)} %copy-done.2, f32[64,128]{1,0:T(8,128)S(1)} %copy-done.4, f32[64,128]{1,0:T(8,128)S(1)} %get-tuple-element.35.q_sides, ...), custom_call_target="tpu_custom_call" | custom-call | tf_op jit(solution)/shard_map/apply_1/pallas_call | solution.py:228
  69.0 1.9 %collective-permute-start.10 = (f32[64,128]{1,0:T(8,128)S(1)}, f32[64,128]{1,0:T(8,128)S(1)}, u32[]{:S(2)}, u32[]{:S(2)}) collective-permute-start(f32[64,128]{1,0:T(8,128)S(1)} %get-tuple-element.39), channel_id=1, source_target_pairs={{0,16},{16,32},{32,48},{48,64},{64,80},{80,96},{96,112},{112,128},... | collective-permute-start | bytes 98312 | tf_op jit(solution)/shard_map/ppermute | solution.py:18
  70.9 8.1 %collective-permute-start.11 = (f32[64,128]{1,0:T(8,128)S(1)}, f32[64,128]{1,0:T(8,128)S(1)}, u32[]{:S(2)}, u32[]{:S(2)}) collective-permute-start(f32[64,128]{1,0:T(8,128)S(1)} %get-tuple-element.40), channel_id=1, source_target_pairs={{0,496},{16,0},{32,16},{48,32},{64,48},{80,64},{96,80},{112,96},{1... | collective-permute-start | bytes 98312 | tf_op jit(solution)/shard_map/ppermute | solution.py:18
  80.0 3.3 %collective-permute-start.12 = (f32[64,128]{1,0:T(8,128)S(1)}, f32[64,128]{1,0:T(8,128)S(1)}, u32[]{:S(2)}, u32[]{:S(2)}) collective-permute-start(f32[64,128]{1,0:T(8,128)S(1)} %get-tuple-element.42), channel_id=1, source_target_pairs={{0,1},{1,2},{2,3},{3,4},{4,5},{5,6},{6,7},{7,8},{8,9},{9,10},{10,1... | collective-permute-start | bytes 98312 | tf_op jit(solution)/shard_map/ppermute | solution.py:18
  83.3 1.9 %collective-permute-start.13 = (f32[64,128]{1,0:T(8,128)S(1)}, f32[64,128]{1,0:T(8,128)S(1)}, u32[]{:S(2)}, u32[]{:S(2)}) collective-permute-start(f32[64,128]{1,0:T(8,128)S(1)} %get-tuple-element.43), channel_id=1, source_target_pairs={{1,0},{2,1},{3,2},{4,3},{5,4},{6,5},{7,6},{8,7},{9,8},{10,9},{11,1... | collective-permute-start | bytes 98312 | tf_op jit(solution)/shard_map/ppermute | solution.py:18
  85.3 3.9 %collective-permute-done.13.south_q = f32[64,128]{1,0:T(8,128)S(1)} collective-permute-done((f32[64,128]{1,0:T(8,128)S(1)}, f32[64,128]{1,0:T(8,128)S(1)}, u32[]{:S(2)}, u32[]{:S(2)}) %collective-permute-start.13) | collective-permute-done | bytes 32800 | tf_op jit(solution)/shard_map/ppermute | solution.py:18
  89.2 3.5 %apply_2.1 = (f32[64,128]{1,0:T(8,128)S(1)}, f32[64,128]{1,0:T(8,128)}, f32[64,128]{1,0:T(8,128)}, f32[16,1,128]{2,1,0:T(1,128)S(1)}) custom-call(f32[64,128]{1,0:T(8,128)S(1)} %get-tuple-element.38.vector.v2, s32[64,128]{1,0:T(8,128)S(1)} %copy-done.2, f32[64,128]{1,0:T(8,128)S(1)} %copy-done.4, f32[64,128]{1,0:T(8,128)S(1)} %get-tuple-element.41.q_sides, ...), custom_call_target="tpu_custom_call" | custom-call | tf_op jit(solution)/shard_map/apply_2/pallas_call | solution.py:228
  92.7 13.3 %all_to_all.10.parts = f32[16,1,128]{2,1,0:T(1,128)S(1)} all-to-all(f32[16,1,128]{2,1,0:T(1,128)S(1)} %get-tuple-element.44), channel_id=1, replica_groups=mesh['lon'=32,'lat'=16] {'lat'}, dimensions={0} | all-to-all | bytes 16384 | tf_op jit(solution)/shard_map/all_to_all | solution.py:342
  106.0 20.8 %all_to_all.11.parts = f32[32,1,128]{2,1,0:T(1,128)S(1)} all-to-all(f32[32,1,128]{2,1,0:T(1,128)S(1)} %sum_kernel.1), channel_id=1, replica_groups=mesh['lon'=32,'lat'=16] {'lon'}, dimensions={0} | all-to-all | bytes 32768 | tf_op jit(solution)/shard_map/all_to_all | solution.py:344
  (47 shorter events, 7.2 us)
Async XLA Ops:
  0.6 1.2 copy-start
  1.9 0.8 copy-start.2
  2.6 0.8 copy-start.3
  3.4 37.4 %copy-start.1 = (bf16[64,64,128]{2,1,0:T(8,128)(2,1)S(1)}, bf16[64,64,128]{2,1,0:T(8,128)(2,1)}, u32[]{:S(2)}) copy-start(bf16[64,64,128]{2,1,0:T(8,128)(2,1)} %ens.7) | copy-start | bytes 3145732
  4.3 24.8 %collective-permute-start = (bf16[19,64,128]{2,1,0:T(8,128)(2,1)S(1)}, bf16[19,64,128]{2,1,0:T(8,128)(2,1)S(1)}, u32[]{:S(2)}, u32[]{:S(2)}) collective-permute-start(bf16[19,64,128]{2,1,0:T(8,128)(2,1)S(1)} %get-tuple-element.24), channel_id=1, source_target_pairs={{0,16},{16,32},{32,48},{48,64},{64,80},{80,96},{96,112},{112,128},... | collective-permute-start | bytes 933896 | tf_op jit(solution)/shard_map/ppermute | solution.py:18
  8.7 20.5 %collective-permute-start.1 = (bf16[19,64,128]{2,1,0:T(8,128)(2,1)S(1)}, bf16[19,64,128]{2,1,0:T(8,128)(2,1)S(1)}, u32[]{:S(2)}, u32[]{:S(2)}) collective-permute-start(bf16[19,64,128]{2,1,0:T(8,128)(2,1)S(1)} %get-tuple-element.25), channel_id=1, source_target_pairs={{0,496},{16,0},{32,16},{48,32},{64,48},{80,64},{96,80},{112,96},{1... | collective-permute-start | bytes 933896 | tf_op jit(solution)/shard_map/ppermute | solution.py:18
  20.6 14.7 %collective-permute-start.4 = (bf16[67,32,128]{2,1,0:T(8,128)(2,1)S(1)}, bf16[67,32,128]{2,1,0:T(8,128)(2,1)S(1)}, u32[]{:S(2)}, u32[]{:S(2)}) collective-permute-start(bf16[67,32,128]{2,1,0:T(8,128)(2,1)S(1)} %get-tuple-element.29), channel_id=1, source_target_pairs={{1,0},{2,1},{3,2},{4,3},{5,4},{6,5},{7,6},{8,7},{9,8},{10,9},{11,1... | collective-permute-start | bytes 1646600 | tf_op jit(solution)/shard_map/ppermute | solution.py:18
  23.5 11.9 %collective-permute-start.2 = (bf16[67,32,128]{2,1,0:T(8,128)(2,1)S(1)}, bf16[67,32,128]{2,1,0:T(8,128)(2,1)S(1)}, u32[]{:S(2)}, u32[]{:S(2)}) collective-permute-start(bf16[67,32,128]{2,1,0:T(8,128)(2,1)S(1)} %get-tuple-element.27), channel_id=1, source_target_pairs={{0,1},{1,2},{2,3},{3,4},{4,5},{5,6},{6,7},{7,8},{8,9},{9,10},{10,1... | collective-permute-start | bytes 1646600 | tf_op jit(solution)/shard_map/ppermute | solution.py:18
  26.2 0.7 copy-start.5
  29.6 11.1 %collective-permute-start.5 = (bf16[35,32,128]{2,1,0:T(8,128)(2,1)S(1)}, bf16[35,32,128]{2,1,0:T(8,128)(2,1)S(1)}, u32[]{:S(2)}, u32[]{:S(2)}) collective-permute-start(bf16[35,32,128]{2,1,0:T(8,128)(2,1)S(1)} %get-tuple-element.30), channel_id=1, source_target_pairs={{1,0},{2,1},{3,2},{4,3},{5,4},{6,5},{7,6},{8,7},{9,8},{10,9},{11,1... | collective-permute-start | bytes 860168 | tf_op jit(solution)/shard_map/ppermute | solution.py:18
  31.7 9.1 %collective-permute-start.3 = (bf16[35,32,128]{2,1,0:T(8,128)(2,1)S(1)}, bf16[35,32,128]{2,1,0:T(8,128)(2,1)S(1)}, u32[]{:S(2)}, u32[]{:S(2)}) collective-permute-start(bf16[35,32,128]{2,1,0:T(8,128)(2,1)S(1)} %get-tuple-element.28), channel_id=1, source_target_pairs={{0,1},{1,2},{2,3},{3,4},{4,5},{5,6},{6,7},{7,8},{8,9},{9,10},{10,1... | collective-permute-start | bytes 860168 | tf_op jit(solution)/shard_map/ppermute | solution.py:18
  40.8 0.8 copy-start.4
  44.4 13.3 %collective-permute-start.6 = (f32[64,128]{1,0:T(8,128)S(1)}, f32[64,128]{1,0:T(8,128)S(1)}, u32[]{:S(2)}, u32[]{:S(2)}) collective-permute-start(f32[64,128]{1,0:T(8,128)S(1)} %get-tuple-element.33), channel_id=1, source_target_pairs={{0,16},{16,32},{32,48},{48,64},{64,80},{80,96},{96,112},{112,128},... | collective-permute-start | bytes 98312 | tf_op jit(solution)/shard_map/ppermute | solution.py:18
  46.3 12.4 %collective-permute-start.7 = (f32[64,128]{1,0:T(8,128)S(1)}, f32[64,128]{1,0:T(8,128)S(1)}, u32[]{:S(2)}, u32[]{:S(2)}) collective-permute-start(f32[64,128]{1,0:T(8,128)S(1)} %get-tuple-element.34), channel_id=1, source_target_pairs={{0,496},{16,0},{32,16},{48,32},{64,48},{80,64},{96,80},{112,96},{1... | collective-permute-start | bytes 98312 | tf_op jit(solution)/shard_map/ppermute | solution.py:18
  58.7 4.3 %collective-permute-start.8 = (f32[64,128]{1,0:T(8,128)S(1)}, f32[64,128]{1,0:T(8,128)S(1)}, u32[]{:S(2)}, u32[]{:S(2)}) collective-permute-start(f32[64,128]{1,0:T(8,128)S(1)} %get-tuple-element.36), channel_id=1, source_target_pairs={{0,1},{1,2},{2,3},{3,4},{4,5},{5,6},{6,7},{7,8},{8,9},{9,10},{10,1... | collective-permute-start | bytes 98312 | tf_op jit(solution)/shard_map/ppermute | solution.py:18
  60.7 5.4 %collective-permute-start.9 = (f32[64,128]{1,0:T(8,128)S(1)}, f32[64,128]{1,0:T(8,128)S(1)}, u32[]{:S(2)}, u32[]{:S(2)}) collective-permute-start(f32[64,128]{1,0:T(8,128)S(1)} %get-tuple-element.37), channel_id=1, source_target_pairs={{1,0},{2,1},{3,2},{4,3},{5,4},{6,5},{7,6},{8,7},{9,8},{10,9},{11,1... | collective-permute-start | bytes 98312 | tf_op jit(solution)/shard_map/ppermute | solution.py:18
  69.0 10.0 %collective-permute-start.10 = (f32[64,128]{1,0:T(8,128)S(1)}, f32[64,128]{1,0:T(8,128)S(1)}, u32[]{:S(2)}, u32[]{:S(2)}) collective-permute-start(f32[64,128]{1,0:T(8,128)S(1)} %get-tuple-element.39), channel_id=1, source_target_pairs={{0,16},{16,32},{32,48},{48,64},{64,80},{80,96},{96,112},{112,128},... | collective-permute-start | bytes 98312 | tf_op jit(solution)/shard_map/ppermute | solution.py:18
  70.9 9.1 %collective-permute-start.11 = (f32[64,128]{1,0:T(8,128)S(1)}, f32[64,128]{1,0:T(8,128)S(1)}, u32[]{:S(2)}, u32[]{:S(2)}) collective-permute-start(f32[64,128]{1,0:T(8,128)S(1)} %get-tuple-element.40), channel_id=1, source_target_pairs={{0,496},{16,0},{32,16},{48,32},{64,48},{80,64},{96,80},{112,96},{1... | collective-permute-start | bytes 98312 | tf_op jit(solution)/shard_map/ppermute | solution.py:18
  80.0 5.2 %collective-permute-start.12 = (f32[64,128]{1,0:T(8,128)S(1)}, f32[64,128]{1,0:T(8,128)S(1)}, u32[]{:S(2)}, u32[]{:S(2)}) collective-permute-start(f32[64,128]{1,0:T(8,128)S(1)} %get-tuple-element.42), channel_id=1, source_target_pairs={{0,1},{1,2},{2,3},{3,4},{4,5},{5,6},{6,7},{7,8},{8,9},{9,10},{10,1... | collective-permute-start | bytes 98312 | tf_op jit(solution)/shard_map/ppermute | solution.py:18
  83.3 5.9 %collective-permute-start.13 = (f32[64,128]{1,0:T(8,128)S(1)}, f32[64,128]{1,0:T(8,128)S(1)}, u32[]{:S(2)}, u32[]{:S(2)}) collective-permute-start(f32[64,128]{1,0:T(8,128)S(1)} %get-tuple-element.43), channel_id=1, source_target_pairs={{1,0},{2,1},{3,2},{4,3},{5,4},{6,5},{7,6},{8,7},{9,8},{10,9},{11,1... | collective-permute-start | bytes 98312 | tf_op jit(solution)/shard_map/ppermute | solution.py:18

commit v3 on v0

v3 whole, which is shorter than its diff:
```python
import functools

import jax
import jax.numpy as jnp
from jax import lax
from jax.experimental import pallas as pl
from jax.experimental.pallas import tpu as pltpu
from jax.sharding import Mesh
from jax.sharding import PartitionSpec as P

HMAX = 32
VMEM_LIMIT = 40 * 1024 * 1024


LON = ("far", "near")


def shift(cells, axis, step, closed):
    count = lax.axis_size(axis)
    pairs = [(i, (i + step) % count) for i in range(count) if closed or 0 <= i + step < count]
    return lax.ppermute(cells, axis, pairs)


def taper_weight(offset, half):
    offset = offset.astype(jnp.float32)
    scale = half.astype(jnp.float32)
    ratio = offset / scale
    return jnp.where(jnp.abs(offset) <= scale, jnp.exp(-4.5 * ratio * ratio), 0.0).astype(
        jnp.bfloat16
    )


def lon_bands(half, cols):
    lane = jnp.arange(cols)
    own = taper_weight(lane[:, None] - lane[None, :], half)
    strip = jnp.where(lane % 64 < 32, lane % 64 - 32, cols + lane % 64 - 32)
    both = jnp.arange(2 * cols)
    weight = taper_weight(strip[:, None] - both[None, :] % cols, half)
    keep = lane[:, None] // 64 == both[None, :] // cols
    side = jnp.where(keep, weight, jnp.zeros((), jnp.bfloat16))
    return jnp.concatenate([own, own]), jnp.concatenate([side, side])


def lat_band(half, rows):
    row = jnp.arange(rows)
    halo = jnp.arange(HMAX)
    target = jnp.concatenate([row, halo - HMAX, rows + halo])
    source = jnp.concatenate([row, row])
    return taper_weight(source[None, :] - target[:, None], half)


def split3(x):
    hi = x.astype(jnp.bfloat16)
    rest = x - hi.astype(jnp.float32)
    mid = rest.astype(jnp.bfloat16)
    low = (rest - mid.astype(jnp.float32)).astype(jnp.bfloat16)
    return hi, mid, low


def join3(ref, first):
    parts = [ref[first + k].astype(jnp.float32) for k in range(3)]
    return parts[0] + parts[1] + parts[2]


def lanes(shape):
    return lax.broadcasted_iota(jnp.int32, shape, len(shape) - 1)


def edge_tiles(q):
    lane = lanes(q.shape)
    right = jnp.where(lane >= 96, q, 0.0)
    right = right + pltpu.roll(right, 64, 1)
    right = right + pltpu.roll(right, 32, 1)
    left = jnp.where(lane < 32, q, 0.0)
    left = left + pltpu.roll(left, 64, 1)
    left = left + pltpu.roll(left, 32, 1)
    return right, left


def pack_kernel(ens, q, valid, east, west, south, north):
    members, rows, cols = ens.shape
    source = lax.broadcasted_iota(jnp.int32, (4 * cols, 2 * cols), 0)
    target = lax.broadcasted_iota(jnp.int32, (4 * cols, 2 * cols), 1)
    lane = target % cols
    wanted = (lane // 32) * cols + lane % 32 + jnp.where(target < cols, 96, 0)
    select = jnp.where(source == wanted, 1.0, 0.0).astype(jnp.bfloat16)
    quads = jnp.concatenate(
        [
            jnp.concatenate([ens[4 * i + g] for g in range(4)], axis=1)
            for i in range(members // 4)
        ],
        axis=0,
    )
    both = jnp.dot(quads, select, preferred_element_type=jnp.float32).astype(jnp.bfloat16)
    for i in range(members // 4):
        east[i] = both[rows * i : rows * (i + 1), :cols]
        west[i] = both[rows * i : rows * (i + 1), cols:]
    right, left = edge_tiles(q[...])
    for k, part in enumerate(split3(right)):
        east[members // 4 + k] = part
    for k, part in enumerate(split3(left)):
        west[members // 4 + k] = part
    mask = valid[...].astype(jnp.float32).astype(jnp.bfloat16)
    south[:members] = ens[:, rows - HMAX :, :]
    south[members] = mask[rows - HMAX :]
    north[:members] = ens[:, :HMAX, :]
    north[members] = mask[:HMAX]


def sides_kernel(from_west, from_east, sides, q_sides):
    planes, rows, cols = sides.shape
    quads = planes // 2
    source = lax.broadcasted_iota(jnp.int32, (2 * cols, 2 * cols), 0)
    target = lax.broadcasted_iota(jnp.int32, (2 * cols, 2 * cols), 1)
    wanted = (target // 64) * 32 + target % 32 + jnp.where(target % 64 < 32, 0, cols)
    select = jnp.where(source == wanted, 1.0, 0.0).astype(jnp.bfloat16)
    pairs = jnp.concatenate(
        [jnp.concatenate([from_west[i], from_east[i]], axis=1) for i in range(quads)], axis=0
    )
    both = jnp.dot(pairs, select, preferred_element_type=jnp.float32).astype(jnp.bfloat16)
    for i in range(quads):
        for k in range(2):
            sides[2 * i + k] = both[rows * i : rows * (i + 1), k * cols : (k + 1) * cols]
    left = lanes((rows, cols)) % 64 < 32
    q_sides[...] = jnp.where(left, join3(from_west, quads), join3(from_east, quads))


def gram_lanes(vectors, last):
    lane = lanes((1, 128))
    out = jnp.where(lane == len(GRAM), last, 0.0)
    for k, (i, j) in enumerate(GRAM):
        out = jnp.where(lane == k, jnp.sum(vectors[i] * vectors[j], keepdims=True), out)
    return out


GRAM = [(0, 0), (0, 1), (0, 2), (1, 1), (1, 2), (2, 2)]


def high_low(x):
    high = x.astype(jnp.bfloat16)
    return high, (x - high.astype(jnp.float32)).astype(jnp.bfloat16)


def taper_kernel(step, vector, valid, obs_error, *refs):
    if step == 0:
        q_sides, refs = refs[0][...], refs[1:]
    else:
        left, right, refs = refs[0], refs[1], refs[2:]
        q_sides = jnp.where(lanes(left.shape) % 64 < 32, left[...], right[...])
    ens, sides, above, below, lon_band, side_band, lat = refs[:7]
    part, up, down = refs[-3:]
    members, rows, cols = ens.shape
    count = members // 2
    maskf = valid[...].astype(jnp.float32)
    q = maskf * vector[...]
    side = jnp.concatenate(
        [
            jnp.concatenate(high_low(sides[j].astype(jnp.float32) * q_sides), axis=1)
            for j in range(count)
        ],
        axis=0,
    )
    side = jnp.dot(side, side_band[...], preferred_element_type=jnp.float32)
    main = jnp.concatenate(
        [
            jnp.concatenate(high_low(ens[m].astype(jnp.float32) * q), axis=1)
            for m in range(members)
        ],
        axis=0,
    )
    main = jnp.dot(main, lon_band[...], preferred_element_type=jnp.float32)
    total = jnp.zeros((rows + 2 * HMAX, cols), jnp.float32)
    for j in range(count):
        first = [
            main[rows * (2 * j + k) : rows * (2 * j + k + 1)]
            + side[rows * j : rows * (j + 1), cols * k : cols * (k + 1)]
            for k in range(2)
        ]
        pair = jnp.concatenate(high_low(jnp.concatenate(first, axis=1)), axis=0)
        second = jnp.dot(lat[...], pair, preferred_element_type=jnp.float32)
        for k in range(2):
            m = 2 * j + k
            there = jnp.concatenate([ens[m], above[m], below[m]], axis=0).astype(jnp.float32)
            total = total + there * second[:, cols * k : cols * (k + 1)]
    total = total / (members - 1)
    image = maskf * total[:rows] + obs_error[...] * vector[...]
    upward, downward = total[rows : rows + HMAX], total[rows + HMAX :]
    part[...] = image
    up[:HMAX] = upward
    down[:HMAX] = downward
    if step == 1:
        up[HMAX:] = image[:HMAX]
        down[HMAX:] = image[rows - HMAX :]


def gram_kernel(v0, v1, v2, part, up, down, q_north, q_south, gram):
    vectors = [v0[...], v1[...], v2[...]]
    around = q_north[...] * up[...] + q_south[...] * down[...]
    last = jnp.sum(vectors[2] * part[...], keepdims=True) + jnp.sum(around, keepdims=True)
    gram[...] = jnp.broadcast_to(gram_lanes(vectors, last)[None], gram.shape)


def whole_image(part, from_north, from_south, valid):
    around = jnp.concatenate([from_north[:HMAX], from_south[:HMAX]], axis=0)
    maskf = valid[...].astype(jnp.float32)
    return part[...] + maskf * around, maskf


def finish_kernel(step, part, from_north, from_south, valid, *refs):
    out, east, west = refs[-5:-2] if step == 1 else refs
    image, maskf = whole_image(part, from_north, from_south, valid)
    out[...] = image
    east[...], west[...] = edge_tiles(maskf * image)
    if step == 1:
        up, down, above, below = refs[:4]
        q_north, q_south = refs[-2:]
        edge = above.shape[0] - 1
        mask_north = above[edge].astype(jnp.float32)
        mask_south = below[edge].astype(jnp.float32)
        q_north[...] = mask_north * (from_north[HMAX:] + mask_north * up[:HMAX])
        q_south[...] = mask_south * (from_south[HMAX:] + mask_south * down[:HMAX])


def sum_kernel(parts, out):
    out[...] = jnp.broadcast_to(jnp.sum(parts[...], axis=0, keepdims=True), out.shape)


def solve_kernel(parts, v0, v1, v2, part, from_north, from_south, valid, weights, residual):
    sums = jnp.sum(parts[...], axis=0)
    lane = lanes(sums.shape)
    gram = {}
    for k, (i, j) in enumerate(GRAM + [(2, 3)]):
        value = jnp.sum(jnp.where(lane == k, sums, 0.0), keepdims=True)
        gram[i, j] = gram[j, i] = value
    gram[0, 3], gram[1, 3] = gram[1, 2], gram[2, 2]

    def inner(a, b):
        total = None
        for i, x in a.items():
            for j, y in b.items():
                term = x * y * gram[i, j]
                total = term if total is None else total + term
        return total

    def combine(a, scale, b):
        out = dict(a)
        for i, y in b.items():
            out[i] = out[i] + scale * y if i in out else scale * y
        return out

    one = jnp.ones((1, 1), jnp.float32)
    w, r, d = {}, {0: one}, {0: one}
    now = inner(r, r)
    for step in range(3):
        image = {i + 1: x for i, x in d.items()}
        alpha = now / inner(d, image)
        w = combine(w, alpha, d)
        r = combine(r, -alpha, image)
        if step < 2:
            later = inner(r, r)
            d = combine(r, later / now, d)
            now = later
    basis = [v0[...], v1[...], v2[...], whole_image(part, from_north, from_south, valid)[0]]
    weights[...] = w[0] * basis[0] + w[1] * basis[1] + w[2] * basis[2]
    residual[...] = r[0] * basis[0] + r[1] * basis[1] + r[2] * basis[2] + r[3] * basis[3]


def call(kernel, outs, *args, name=None, flops=0, **more):
    return pl.pallas_call(
        kernel,
        out_shape=outs,
        compiler_params=pltpu.CompilerParams(vmem_limit_bytes=VMEM_LIMIT),
        cost_estimate=pl.CostEstimate(
            flops=flops, transcendentals=0, bytes_accessed=sum(a.size * a.dtype.itemsize for a in args)
        ),
        name=name or kernel.__name__,
        **more,
    )(*args)


def shards(ensemble, right_side, obs_error, valid, halfwidth):
    members, rows, cols = ensemble.shape
    quads, planes = members // 4, members // 2
    bf16 = functools.partial(jax.ShapeDtypeStruct, dtype=jnp.bfloat16)
    f32 = functools.partial(jax.ShapeDtypeStruct, dtype=jnp.float32)
    lon_band, side_band = lon_bands(halfwidth[0], cols)
    lat = lat_band(halfwidth[1], rows)
    q = valid.astype(jnp.float32) * right_side
    east, west, south, north = call(
        pack_kernel,
        [bf16((quads + 3, rows, cols))] * 2 + [bf16((members + 1, HMAX, cols))] * 2,
        ensemble, q, valid,
    )
    from_west = shift(east, LON, 1, True)
    from_east = shift(west, LON, -1, True)
    above = shift(south, "lat", 1, False)
    below = shift(north, "lat", -1, False)
    sides, q_sides = call(
        sides_kernel, [bf16((planes, rows, cols)), f32((rows, cols))], from_west, from_east
    )
    around = [q_sides]
    vectors, more = [right_side], []
    flops = 8 * members * rows * cols * (cols + rows)
    for step in range(3):
        vector = vectors[-1]
        message = f32((2 * HMAX if step == 1 else HMAX, cols))
        outs = [f32((rows, cols)), message, message]
        part, up, down = call(
            functools.partial(taper_kernel, step), outs,
            vector, valid, obs_error, *around, ensemble, sides, above, below, lon_band,
            side_band, lat, name=f"taper_{step}", flops=flops,
        )
        from_north = shift(down, "lat", 1, False)
        from_south = shift(up, "lat", -1, False)
        if step == 2:
            break
        outs = [f32((rows, cols))] * 3
        if step == 1:
            outs += [f32((HMAX, cols))] * 2
            more = [up, down, above, below]
        image, east, west, *more = call(
            functools.partial(finish_kernel, step), outs, part, from_north, from_south, valid,
            *more, name=f"finish_{step}",
        )
        vectors.append(image)
        around = [shift(east, LON, 1, True), shift(west, LON, -1, True)]
    gram = call(
        gram_kernel, f32((lax.axis_size("far") * lax.axis_size("lat"), 1, 128)),
        *vectors, part, up, down, *more,
    )
    parts = lax.all_to_all(gram, ("far", "lat"), 0, 0)
    parts = call(sum_kernel, f32((lax.axis_size("near"), 1, 128)), parts)
    parts = lax.all_to_all(parts, "near", 0, 0)
    return tuple(
        call(
            solve_kernel, [f32((rows, cols))] * 2, parts, *vectors, part, from_north, from_south,
            valid,
        )
    )


def solution(mesh):
    devices = mesh.devices
    parts = 2 if devices.shape[0] % 2 == 0 else 1
    mesh = Mesh(
        devices.reshape(parts, devices.shape[0] // parts, devices.shape[1]), LON + ("lat",)
    )
    in_specs = (P(None, "lat", LON), P("lat", LON), P("lat", LON), P("lat", LON), P())
    out_specs = (P("lat", LON), P("lat", LON))
    return jax.shard_map(shards, mesh=mesh, in_specs=in_specs, out_specs=out_specs, check_vma=False)
```

time: 669 us -> 113 us (0.17)
  blocking collectives: 497 us -> 15.3 us
  waiting for transfers between devices: 77.7 us -> 24.1 us
  local copies, waits for them, and re-layouts: 22.9 us -> 2.46 us
  starting transfers between devices: 47.2 us -> 59.9 us
  matrix products: 7.68 us -> 0 us
  Pallas kernels: 0 us -> 7.35 us
    psum x5 -> x0, blocking collectives: 497 us -> none  [the longest x3 299 us: residual_norm(): return lax.psum(jnp.sum(vector * vector), ('lon', 'lat'))]
    ppermute x12 -> x14, waiting for transfers between devices: 77.7 us -> 21.4 us  [shift(): return lax.ppermute(cells, axis, pairs)]
    all_to_all x0 -> x1, blocking collectives: none -> 15.3 us  [shards(): parts = lax.all_to_all(gram, ('far', 'lat'), 0, 0)]
    slice x13 -> x1, local copies, waits for them, and re-layouts: 12.8 us -> 0.58 us  [shards(): lat = lat_band(halfwidth[1], rows)]
    ppermute x6 -> x0, local copies, waits for them, and re-layouts: 9.77 us -> none  [the longest x3 6.29 us: extended(): lax.ppermute(tail, axis, [(i, (i + 1) % count) for i in range(ends)])]
    dot_general x6 -> x0, matrix products: 7.68 us -> none  [the longest x3 6.3 us: shards(): jnp.einsum('mai,ij->maj', wide, band_lon, preferred_element_type=jnp.floa...]
    ppermute x12 -> x14, starting transfers between devices: 47.2 us -> 54.7 us  [shift(): return lax.ppermute(cells, axis, pairs)]
    pallas_call x0 -> x10, Pallas kernels: none -> 7.35 us  [call(): pl.pallas_call(kernel, out_shape=outs, compiler_params=pltpu.CompilerPara...]
  transfers between devices with their start and end apart: 12 -> 15, of which waited for: 12 -> 8; matrix products, arithmetic and copies ran while one was open for 1% -> 1% of each run, Pallas kernels for 0% -> 0%
where the time goes in v3:
time: 113 us
  starting transfers between devices  59.9 us (53%)
  waiting for transfers between devices  24.1 us (21%)
  blocking collectives  15.3 us (14%)
  Pallas kernels  7.35 us (7%)
  local copies, waits for them, and re-layouts  2.46 us (2%)
  between operations  2.27 us (2%)
  other arithmetic  1.2 us (1%)
    ppermute x14, starting transfers between devices, shift(): return lax.ppermute(cells, axis, pairs)  54.7 us
    ppermute x14, waiting for transfers between devices, shift(): return lax.ppermute(cells, axis, pairs)  21.4 us
    all_to_all x1, blocking collectives, shards(): parts = lax.all_to_all(gram, ('far', 'lat'), 0, 0)  15.3 us
    pallas_call x10, Pallas kernels, call(): pl.pallas_call(kernel, out_shape=outs, compiler_params=pltpu.CompilerPara...  7.35 us
    all_to_all x1, starting transfers between devices, shards(): parts = lax.all_to_all(parts, 'near', 0, 0)  5.16 us
    all_to_all x1, waiting for transfers between devices, shards(): parts = lax.all_to_all(parts, 'near', 0, 0)  2.73 us
  transfers between devices with their start and end apart: 15, of which 8 were waited for; matrix products, arithmetic and copies ran while one was open for 1% of the time, Pallas kernels for 0%

profile of v3, /device:TPU:1, one launch (start us, length us, event | category | flops | bytes accessed | tf_op | source)
XLA Modules:
  0.0 112.5 jit_solution(574505977784073385)
XLA Ops:
  3.1 4.4 %collective-permute-start = (bf16[19,64,128]{2,1,0:T(8,128)(2,1)S(1)}, bf16[19,64,128]{2,1,0:T(8,128)(2,1)S(1)}, u32[]{:S(2)}, u32[]{:S(2)}) collective-permute-start(bf16[19,64,128]{2,1,0:T(8,128)(2,1)S(1)} %get-tuple-element.25), channel_id=1, source_target_pairs={{0,16},{16,32},{32,48},{48,64},{64,80},{80,96},{96,112},{112,128},... | collective-permute-start | bytes 933896 | tf_op jit(solution)/shard_map/ppermute | solution.py:21
  7.5 12.0 %collective-permute-start.1 = (bf16[19,64,128]{2,1,0:T(8,128)(2,1)S(1)}, bf16[19,64,128]{2,1,0:T(8,128)(2,1)S(1)}, u32[]{:S(2)}, u32[]{:S(2)}) collective-permute-start(bf16[19,64,128]{2,1,0:T(8,128)(2,1)S(1)} %get-tuple-element.26), channel_id=1, source_target_pairs={{0,496},{16,0},{32,16},{48,32},{64,48},{80,64},{96,80},{112,96},{1... | collective-permute-start | bytes 933896 | tf_op jit(solution)/shard_map/ppermute | solution.py:21
  19.5 3.1 %collective-permute-start.2 = (bf16[65,32,128]{2,1,0:T(8,128)(2,1)S(1)}, bf16[65,32,128]{2,1,0:T(8,128)(2,1)S(1)}, u32[]{:S(2)}, u32[]{:S(2)}) collective-permute-start(bf16[65,32,128]{2,1,0:T(8,128)(2,1)S(1)} %get-tuple-element.29), channel_id=1, source_target_pairs={{0,1},{1,2},{2,3},{3,4},{4,5},{5,6},{6,7},{7,8},{8,9},{9,10},{10,1... | collective-permute-start | bytes 1597448 | tf_op jit(solution)/shard_map/ppermute | solution.py:21
  22.6 1.9 %collective-permute-start.3 = (bf16[65,32,128]{2,1,0:T(8,128)(2,1)S(1)}, bf16[65,32,128]{2,1,0:T(8,128)(2,1)S(1)}, u32[]{:S(2)}, u32[]{:S(2)}) collective-permute-start(bf16[65,32,128]{2,1,0:T(8,128)(2,1)S(1)} %get-tuple-element.30), channel_id=1, source_target_pairs={{1,0},{2,1},{3,2},{4,3},{5,4},{6,5},{7,6},{8,7},{9,8},{10,9},{11,1... | collective-permute-start | bytes 1597448 | tf_op jit(solution)/shard_map/ppermute | solution.py:21
  28.8 8.3 %collective-permute-done.3.refs_4_.refs_5_.refs_3_ = bf16[65,32,128]{2,1,0:T(8,128)(2,1)S(1)} collective-permute-done((bf16[65,32,128]{2,1,0:T(8,128)(2,1)S(1)}, bf16[65,32,128]{2,1,0:T(8,128)(2,1)S(1)}, u32[]{:S(2)}, u32[]{:S(2)}) %collective-permute-start.3) | collective-permute-done | bytes 532512 | tf_op jit(solution)/shard_map/ppermute | solution.py:21
  37.1 1.5 %taper_0.1 = (f32[64,128]{1,0:T(8,128)S(1)}, f32[32,128]{1,0:T(8,128)S(1)}, f32[32,128]{1,0:T(8,128)S(1)}) custom-call(f32[64,128]{1,0:T(8,128)S(1)} %copy-done.3, s32[64,128]{1,0:T(8,128)S(1)} %copy-done.2, f32[64,128]{1,0:T(8,128)S(1)} %copy-done.4, f32[64,128]{1,0:T(8,128)S(1)} %get-tuple-element.27.refs_0_, bf16[64,64,128]{2,1,0:T(8,128)(2,1)S(1)} %copy-done.1, ...), custom_call_target="tpu_custom_call" | custom-call | flops 805306368 | bytes 2998272 | tf_op jit(solution)/shard_map/taper_0/pallas_call | solution.py:269
  38.6 1.9 %collective-permute-start.4 = (f32[32,128]{1,0:T(8,128)S(1)}, f32[32,128]{1,0:T(8,128)S(1)}, u32[]{:S(2)}, u32[]{:S(2)}) collective-permute-start(f32[32,128]{1,0:T(8,128)S(1)} %get-tuple-element.32), channel_id=1, source_target_pairs={{0,1},{1,2},{2,3},{3,4},{4,5},{5,6},{6,7},{7,8},{8,9},{9,10},{10,1... | collective-permute-start | bytes 49160 | tf_op jit(solution)/shard_map/ppermute | solution.py:21
  40.6 2.4 %collective-permute-start.5 = (f32[32,128]{1,0:T(8,128)S(1)}, f32[32,128]{1,0:T(8,128)S(1)}, u32[]{:S(2)}, u32[]{:S(2)}) collective-permute-start(f32[32,128]{1,0:T(8,128)S(1)} %get-tuple-element.33), channel_id=1, source_target_pairs={{1,0},{2,1},{3,2},{4,3},{5,4},{6,5},{7,6},{8,7},{9,8},{10,9},{11,1... | collective-permute-start | bytes 49160 | tf_op jit(solution)/shard_map/ppermute | solution.py:21
  43.0 2.6 %collective-permute-done.5.from_south = f32[32,128]{1,0:T(8,128)S(1)} collective-permute-done((f32[32,128]{1,0:T(8,128)S(1)}, f32[32,128]{1,0:T(8,128)S(1)}, u32[]{:S(2)}, u32[]{:S(2)}) %collective-permute-start.5) | collective-permute-done | bytes 16416 | tf_op jit(solution)/shard_map/ppermute | solution.py:21
  45.8 1.9 %collective-permute-start.6 = (f32[64,128]{1,0:T(8,128)S(1)}, f32[64,128]{1,0:T(8,128)S(1)}, u32[]{:S(2)}, u32[]{:S(2)}) collective-permute-start(f32[64,128]{1,0:T(8,128)S(1)} %get-tuple-element.35), channel_id=1, source_target_pairs={{0,16},{16,32},{32,48},{48,64},{64,80},{80,96},{96,112},{112,128},... | collective-permute-start | bytes 98312 | tf_op jit(solution)/shard_map/ppermute | solution.py:21
  47.7 7.5 %collective-permute-start.7 = (f32[64,128]{1,0:T(8,128)S(1)}, f32[64,128]{1,0:T(8,128)S(1)}, u32[]{:S(2)}, u32[]{:S(2)}) collective-permute-start(f32[64,128]{1,0:T(8,128)S(1)} %get-tuple-element.36), channel_id=1, source_target_pairs={{0,496},{16,0},{32,16},{48,32},{64,48},{80,64},{96,80},{112,96},{1... | collective-permute-start | bytes 98312 | tf_op jit(solution)/shard_map/ppermute | solution.py:21
  56.2 1.6 %taper_1.1 = (f32[64,128]{1,0:T(8,128)S(1)}, f32[64,128]{1,0:T(8,128)S(1)}, f32[64,128]{1,0:T(8,128)S(1)}) custom-call(f32[64,128]{1,0:T(8,128)S(1)} %get-tuple-element.34.vector.v1, s32[64,128]{1,0:T(8,128)S(1)} %copy-done.2, f32[64,128]{1,0:T(8,128)S(1)} %copy-done.4, f32[64,128]{1,0:T(8,128)S(1)} %collective-permute-done.6.refs_0_, ...), custom_call_target="tpu_custom_call" | custom-call | flops 805306368 | bytes 3031040 | tf_op jit(solution)/shard_map/taper_1/pallas_call | solution.py:269
  57.8 2.9 %collective-permute-start.8 = (f32[64,128]{1,0:T(8,128)S(1)}, f32[64,128]{1,0:T(8,128)S(1)}, u32[]{:S(2)}, u32[]{:S(2)}) collective-permute-start(f32[64,128]{1,0:T(8,128)S(1)} %get-tuple-element.38.refs_1_), channel_id=1, source_target_pairs={{0,1},{1,2},{2,3},{3,4},{4,5},{5,6},{6,7},{7,8},{8,9},{9,10},{10,1... | collective-permute-start | bytes 98312 | tf_op jit(solution)/shard_map/ppermute | solution.py:21
  60.7 1.9 %collective-permute-start.9 = (f32[64,128]{1,0:T(8,128)S(1)}, f32[64,128]{1,0:T(8,128)S(1)}, u32[]{:S(2)}, u32[]{:S(2)}) collective-permute-start(f32[64,128]{1,0:T(8,128)S(1)} %get-tuple-element.39.refs_0_), channel_id=1, source_target_pairs={{1,0},{2,1},{3,2},{4,3},{5,4},{6,5},{7,6},{8,7},{9,8},{10,9},{11,1... | collective-permute-start | bytes 98312 | tf_op jit(solution)/shard_map/ppermute | solution.py:21
  62.6 4.1 %collective-permute-done.9.from_south = f32[64,128]{1,0:T(8,128)S(1)} collective-permute-done((f32[64,128]{1,0:T(8,128)S(1)}, f32[64,128]{1,0:T(8,128)S(1)}, u32[]{:S(2)}, u32[]{:S(2)}) %collective-permute-start.9) | collective-permute-done | bytes 32800 | tf_op jit(solution)/shard_map/ppermute | solution.py:21
  66.9 1.9 %collective-permute-start.10 = (f32[64,128]{1,0:T(8,128)S(1)}, f32[64,128]{1,0:T(8,128)S(1)}, u32[]{:S(2)}, u32[]{:S(2)}) collective-permute-start(f32[64,128]{1,0:T(8,128)S(1)} %get-tuple-element.41), channel_id=1, source_target_pairs={{0,16},{16,32},{32,48},{48,64},{64,80},{80,96},{96,112},{112,128},... | collective-permute-start | bytes 98312 | tf_op jit(solution)/shard_map/ppermute | solution.py:21
  68.8 7.9 %collective-permute-start.11 = (f32[64,128]{1,0:T(8,128)S(1)}, f32[64,128]{1,0:T(8,128)S(1)}, u32[]{:S(2)}, u32[]{:S(2)}) collective-permute-start(f32[64,128]{1,0:T(8,128)S(1)} %get-tuple-element.42), channel_id=1, source_target_pairs={{0,496},{16,0},{32,16},{48,32},{64,48},{80,64},{96,80},{112,96},{1... | collective-permute-start | bytes 98312 | tf_op jit(solution)/shard_map/ppermute | solution.py:21
  77.7 1.6 %taper_2.1 = (f32[64,128]{1,0:T(8,128)S(1)}, f32[32,128]{1,0:T(8,128)S(1)}, f32[32,128]{1,0:T(8,128)S(1)}) custom-call(f32[64,128]{1,0:T(8,128)S(1)} %get-tuple-element.40.vector.v2, s32[64,128]{1,0:T(8,128)S(1)} %copy-done.2, f32[64,128]{1,0:T(8,128)S(1)} %copy-done.4, f32[64,128]{1,0:T(8,128)S(1)} %collective-permute-done.10.refs_0_, ...), custom_call_target="tpu_custom_call" | custom-call | flops 805306368 | bytes 3031040 | tf_op jit(solution)/shard_map/taper_2/pallas_call | solution.py:269
  79.4 15.3 %all_to_all.10.parts = f32[32,1,128]{2,1,0:T(1,128)S(1)} all-to-all(f32[32,1,128]{2,1,0:T(1,128)S(1)} %gram_kernel.1), channel_id=1, replica_groups=mesh['far'=2,'near'=16,'lat'=16] {'far','lat'}, dimensions={0} | all-to-all | bytes 32768 | tf_op jit(solution)/shard_map/all_to_all | solution.py:331
  95.3 5.2 %all-to-all-start.1 = ((f32[16,1,128]{2,1,0:T(1,128)}), f32[16,1,128]{2,1,0:T(1,128)S(1)}, u32[]{:S(2)}, u32[]{:S(2)}) async-start(f32[16,1,128]{2,1,0:T(1,128)} %sum_kernel.1), calls=%async_computation.1 | async-start | bytes 16384 | tf_op jit(solution)/shard_map/all_to_all | solution.py:333
  100.5 3.1 %collective-permute-start.12 = (f32[32,128]{1,0:T(8,128)S(1)}, f32[32,128]{1,0:T(8,128)S(1)}, u32[]{:S(2)}, u32[]{:S(2)}) collective-permute-start(f32[32,128]{1,0:T(8,128)S(1)} %get-tuple-element.45.down), channel_id=1, source_target_pairs={{0,1},{1,2},{2,3},{3,4},{4,5},{5,6},{6,7},{7,8},{8,9},{9,10},{10,1... | collective-permute-start | bytes 49160 | tf_op jit(solution)/shard_map/ppermute | solution.py:21
  103.6 1.9 %collective-permute-start.13 = (f32[32,128]{1,0:T(8,128)S(1)}, f32[32,128]{1,0:T(8,128)S(1)}, u32[]{:S(2)}, u32[]{:S(2)}) collective-permute-start(f32[32,128]{1,0:T(8,128)S(1)} %get-tuple-element.44.up), channel_id=1, source_target_pairs={{1,0},{2,1},{3,2},{4,3},{5,4},{6,5},{7,6},{8,7},{9,8},{10,9},{11,1... | collective-permute-start | bytes 49160 | tf_op jit(solution)/shard_map/ppermute | solution.py:21
  105.6 3.4 %collective-permute-done.13.from_south = f32[32,128]{1,0:T(8,128)S(1)} collective-permute-done((f32[32,128]{1,0:T(8,128)S(1)}, f32[32,128]{1,0:T(8,128)S(1)}, u32[]{:S(2)}, u32[]{:S(2)}) %collective-permute-start.13) | collective-permute-done | bytes 16416 | tf_op jit(solution)/shard_map/ppermute | solution.py:21
  109.0 2.7 %all-to-all-done.1.parts = f32[16,1,128]{2,1,0:T(1,128)S(1)} async-done(((f32[16,1,128]{2,1,0:T(1,128)}), f32[16,1,128]{2,1,0:T(1,128)S(1)}, u32[]{:S(2)}, u32[]{:S(2)}) %all-to-all-start.1) | async-done | bytes 8224 | tf_op jit(solution)/shard_map/all_to_all | solution.py:333
  (41 shorter events, 9.3 us)
Async XLA Ops:
  0.6 0.8 copy-start.2
  1.5 1.2 %copy-start = (bf16[64,64,128]{2,1,0:T(8,128)(2,1)S(1)}, bf16[64,64,128]{2,1,0:T(8,128)(2,1)}, u32[]{:S(2)}) copy-start(bf16[64,64,128]{2,1,0:T(8,128)(2,1)} %refs_2_.3) | copy-start | bytes 3145732
  2.7 34.4 %copy-start.1 = (bf16[64,64,128]{2,1,0:T(8,128)(2,1)S(1)}, bf16[64,64,128]{2,1,0:T(8,128)(2,1)}, u32[]{:S(2)}) copy-start(bf16[64,64,128]{2,1,0:T(8,128)(2,1)} %refs_2_.3) | copy-start | bytes 3145732
  3.1 24.3 %collective-permute-start = (bf16[19,64,128]{2,1,0:T(8,128)(2,1)S(1)}, bf16[19,64,128]{2,1,0:T(8,128)(2,1)S(1)}, u32[]{:S(2)}, u32[]{:S(2)}) collective-permute-start(bf16[19,64,128]{2,1,0:T(8,128)(2,1)S(1)} %get-tuple-element.25), channel_id=1, source_target_pairs={{0,16},{16,32},{32,48},{48,64},{64,80},{80,96},{96,112},{112,128},... | collective-permute-start | bytes 933896 | tf_op jit(solution)/shard_map/ppermute | solution.py:21
  7.5 20.0 %collective-permute-start.1 = (bf16[19,64,128]{2,1,0:T(8,128)(2,1)S(1)}, bf16[19,64,128]{2,1,0:T(8,128)(2,1)S(1)}, u32[]{:S(2)}, u32[]{:S(2)}) collective-permute-start(bf16[19,64,128]{2,1,0:T(8,128)(2,1)S(1)} %get-tuple-element.26), channel_id=1, source_target_pairs={{0,496},{16,0},{32,16},{48,32},{64,48},{80,64},{96,80},{112,96},{1... | collective-permute-start | bytes 933896 | tf_op jit(solution)/shard_map/ppermute | solution.py:21
  19.5 9.3 %collective-permute-start.2 = (bf16[65,32,128]{2,1,0:T(8,128)(2,1)S(1)}, bf16[65,32,128]{2,1,0:T(8,128)(2,1)S(1)}, u32[]{:S(2)}, u32[]{:S(2)}) collective-permute-start(bf16[65,32,128]{2,1,0:T(8,128)(2,1)S(1)} %get-tuple-element.29), channel_id=1, source_target_pairs={{0,1},{1,2},{2,3},{3,4},{4,5},{5,6},{6,7},{7,8},{8,9},{9,10},{10,1... | collective-permute-start | bytes 1597448 | tf_op jit(solution)/shard_map/ppermute | solution.py:21
  22.6 14.5 %collective-permute-start.3 = (bf16[65,32,128]{2,1,0:T(8,128)(2,1)S(1)}, bf16[65,32,128]{2,1,0:T(8,128)(2,1)S(1)}, u32[]{:S(2)}, u32[]{:S(2)}) collective-permute-start(bf16[65,32,128]{2,1,0:T(8,128)(2,1)S(1)} %get-tuple-element.30), channel_id=1, source_target_pairs={{1,0},{2,1},{3,2},{4,3},{5,4},{6,5},{7,6},{8,7},{9,8},{10,9},{11,1... | collective-permute-start | bytes 1597448 | tf_op jit(solution)/shard_map/ppermute | solution.py:21
  24.5 0.7 copy-start.5
  27.5 9.6 %copy-start.3 = (f32[64,128]{1,0:T(8,128)S(1)}, f32[64,128]{1,0:T(8,128)}, u32[]{:S(2)}) copy-start(f32[64,128]{1,0:T(8,128)} %v0.3) | copy-start | bytes 98308
  27.5 9.6 %copy-start.4 = (f32[64,128]{1,0:T(8,128)S(1)}, f32[64,128]{1,0:T(8,128)}, u32[]{:S(2)}) copy-start(f32[64,128]{1,0:T(8,128)} %obs_error.5) | copy-start | bytes 98308
  38.6 4.3 %collective-permute-start.4 = (f32[32,128]{1,0:T(8,128)S(1)}, f32[32,128]{1,0:T(8,128)S(1)}, u32[]{:S(2)}, u32[]{:S(2)}) collective-permute-start(f32[32,128]{1,0:T(8,128)S(1)} %get-tuple-element.32), channel_id=1, source_target_pairs={{0,1},{1,2},{2,3},{3,4},{4,5},{5,6},{6,7},{7,8},{8,9},{9,10},{10,1... | collective-permute-start | bytes 49160 | tf_op jit(solution)/shard_map/ppermute | solution.py:21
  40.6 5.1 %collective-permute-start.5 = (f32[32,128]{1,0:T(8,128)S(1)}, f32[32,128]{1,0:T(8,128)S(1)}, u32[]{:S(2)}, u32[]{:S(2)}) collective-permute-start(f32[32,128]{1,0:T(8,128)S(1)} %get-tuple-element.33), channel_id=1, source_target_pairs={{1,0},{2,1},{3,2},{4,3},{5,4},{6,5},{7,6},{8,7},{9,8},{10,9},{11,1... | collective-permute-start | bytes 49160 | tf_op jit(solution)/shard_map/ppermute | solution.py:21
  45.8 9.4 %collective-permute-start.6 = (f32[64,128]{1,0:T(8,128)S(1)}, f32[64,128]{1,0:T(8,128)S(1)}, u32[]{:S(2)}, u32[]{:S(2)}) collective-permute-start(f32[64,128]{1,0:T(8,128)S(1)} %get-tuple-element.35), channel_id=1, source_target_pairs={{0,16},{16,32},{32,48},{48,64},{64,80},{80,96},{96,112},{112,128},... | collective-permute-start | bytes 98312 | tf_op jit(solution)/shard_map/ppermute | solution.py:21
  47.7 8.5 %collective-permute-start.7 = (f32[64,128]{1,0:T(8,128)S(1)}, f32[64,128]{1,0:T(8,128)S(1)}, u32[]{:S(2)}, u32[]{:S(2)}) collective-permute-start(f32[64,128]{1,0:T(8,128)S(1)} %get-tuple-element.36), channel_id=1, source_target_pairs={{0,496},{16,0},{32,16},{48,32},{64,48},{80,64},{96,80},{112,96},{1... | collective-permute-start | bytes 98312 | tf_op jit(solution)/shard_map/ppermute | solution.py:21
  57.8 4.9 %collective-permute-start.8 = (f32[64,128]{1,0:T(8,128)S(1)}, f32[64,128]{1,0:T(8,128)S(1)}, u32[]{:S(2)}, u32[]{:S(2)}) collective-permute-start(f32[64,128]{1,0:T(8,128)S(1)} %get-tuple-element.38.refs_1_), channel_id=1, source_target_pairs={{0,1},{1,2},{2,3},{3,4},{4,5},{5,6},{6,7},{7,8},{8,9},{9,10},{10,1... | collective-permute-start | bytes 98312 | tf_op jit(solution)/shard_map/ppermute | solution.py:21
  60.7 6.0 %collective-permute-start.9 = (f32[64,128]{1,0:T(8,128)S(1)}, f32[64,128]{1,0:T(8,128)S(1)}, u32[]{:S(2)}, u32[]{:S(2)}) collective-permute-start(f32[64,128]{1,0:T(8,128)S(1)} %get-tuple-element.39.refs_0_), channel_id=1, source_target_pairs={{1,0},{2,1},{3,2},{4,3},{5,4},{6,5},{7,6},{8,7},{9,8},{10,9},{11,1... | collective-permute-start | bytes 98312 | tf_op jit(solution)/shard_map/ppermute | solution.py:21
  66.9 9.8 %collective-permute-start.10 = (f32[64,128]{1,0:T(8,128)S(1)}, f32[64,128]{1,0:T(8,128)S(1)}, u32[]{:S(2)}, u32[]{:S(2)}) collective-permute-start(f32[64,128]{1,0:T(8,128)S(1)} %get-tuple-element.41), channel_id=1, source_target_pairs={{0,16},{16,32},{32,48},{48,64},{64,80},{80,96},{96,112},{112,128},... | collective-permute-start | bytes 98312 | tf_op jit(solution)/shard_map/ppermute | solution.py:21
  68.8 8.9 %collective-permute-start.11 = (f32[64,128]{1,0:T(8,128)S(1)}, f32[64,128]{1,0:T(8,128)S(1)}, u32[]{:S(2)}, u32[]{:S(2)}) collective-permute-start(f32[64,128]{1,0:T(8,128)S(1)} %get-tuple-element.42), channel_id=1, source_target_pairs={{0,496},{16,0},{32,16},{48,32},{64,48},{80,64},{96,80},{112,96},{1... | collective-permute-start | bytes 98312 | tf_op jit(solution)/shard_map/ppermute | solution.py:21
  95.3 16.4 %all-to-all-start.1 = ((f32[16,1,128]{2,1,0:T(1,128)}), f32[16,1,128]{2,1,0:T(1,128)S(1)}, u32[]{:S(2)}, u32[]{:S(2)}) async-start(f32[16,1,128]{2,1,0:T(1,128)} %sum_kernel.1), calls=%async_computation.1 | async-start | bytes 16384 | tf_op jit(solution)/shard_map/all_to_all | solution.py:333
  100.5 5.1 %collective-permute-start.12 = (f32[32,128]{1,0:T(8,128)S(1)}, f32[32,128]{1,0:T(8,128)S(1)}, u32[]{:S(2)}, u32[]{:S(2)}) collective-permute-start(f32[32,128]{1,0:T(8,128)S(1)} %get-tuple-element.45.down), channel_id=1, source_target_pairs={{0,1},{1,2},{2,3},{3,4},{4,5},{5,6},{6,7},{7,8},{8,9},{9,10},{10,1... | collective-permute-start | bytes 49160 | tf_op jit(solution)/shard_map/ppermute | solution.py:21
  103.6 5.4 %collective-permute-start.13 = (f32[32,128]{1,0:T(8,128)S(1)}, f32[32,128]{1,0:T(8,128)S(1)}, u32[]{:S(2)}, u32[]{:S(2)}) collective-permute-start(f32[32,128]{1,0:T(8,128)S(1)} %get-tuple-element.44.up), channel_id=1, source_target_pairs={{1,0},{2,1},{3,2},{4,3},{5,4},{6,5},{7,6},{8,7},{9,8},{10,9},{11,1... | collective-permute-start | bytes 49160 | tf_op jit(solution)/shard_map/ppermute | solution.py:21

commit v4 on v3

--- a/solution.py
+++ b/solution.py
@@ -77,7 +77,13 @@
     return right, left
 
 
-def pack_kernel(ens, q, valid, east, west, south, north):
+def rows_kernel(ens, south, north):
+    rows = ens.shape[1]
+    south[...] = ens[:, rows - HMAX :, :]
+    north[...] = ens[:, :HMAX, :]
+
+
+def columns_kernel(ens, q, _, __, east, west):
     members, rows, cols = ens.shape
     source = lax.broadcasted_iota(jnp.int32, (4 * cols, 2 * cols), 0)
     target = lax.broadcasted_iota(jnp.int32, (4 * cols, 2 * cols), 1)
@@ -100,11 +106,6 @@
         east[members // 4 + k] = part
     for k, part in enumerate(split3(left)):
         west[members // 4 + k] = part
-    mask = valid[...].astype(jnp.float32).astype(jnp.bfloat16)
-    south[:members] = ens[:, rows - HMAX :, :]
-    south[members] = mask[rows - HMAX :]
-    north[:members] = ens[:, :HMAX, :]
-    north[members] = mask[:HMAX]
 
 
 def sides_kernel(from_west, from_east, sides, q_sides):
@@ -188,6 +189,9 @@
     part[...] = image
     up[:HMAX] = upward
     down[:HMAX] = downward
+    if step == 0:
+        up[HMAX:] = maskf[:HMAX]
+        down[HMAX:] = maskf[rows - HMAX :]
     if step == 1:
         up[HMAX:] = image[:HMAX]
         down[HMAX:] = image[rows - HMAX :]
@@ -212,11 +216,9 @@
     out[...] = image
     east[...], west[...] = edge_tiles(maskf * image)
     if step == 1:
-        up, down, above, below = refs[:4]
+        up, down, north, south = refs[:4]
         q_north, q_south = refs[-2:]
-        edge = above.shape[0] - 1
-        mask_north = above[edge].astype(jnp.float32)
-        mask_south = below[edge].astype(jnp.float32)
+        mask_north, mask_south = north[HMAX:], south[HMAX:]
         q_north[...] = mask_north * (from_north[HMAX:] + mask_north * up[:HMAX])
         q_south[...] = mask_south * (from_south[HMAX:] + mask_south * down[:HMAX])
 
@@ -286,15 +288,16 @@
     lon_band, side_band = lon_bands(halfwidth[0], cols)
     lat = lat_band(halfwidth[1], rows)
     q = valid.astype(jnp.float32) * right_side
-    east, west, south, north = call(
-        pack_kernel,
-        [bf16((quads + 3, rows, cols))] * 2 + [bf16((members + 1, HMAX, cols))] * 2,
-        ensemble, q, valid,
+    south, north = call(rows_kernel, [bf16((members, HMAX, cols))] * 2, ensemble)
+    above = shift(south, "lat", 1, False)
+    below = shift(north, "lat", -1, False)
+    anywhere, plain = pl.BlockSpec(memory_space=pl.ANY), pl.BlockSpec(memory_space=pltpu.VMEM)
+    east, west = call(
+        columns_kernel, [bf16((quads + 3, rows, cols))] * 2, ensemble, q, south, north,
+        in_specs=[plain, plain, anywhere, anywhere],
     )
     from_west = shift(east, LON, 1, True)
     from_east = shift(west, LON, -1, True)
-    above = shift(south, "lat", 1, False)
-    below = shift(north, "lat", -1, False)
     sides, q_sides = call(
         sides_kernel, [bf16((planes, rows, cols)), f32((rows, cols))], from_west, from_east
     )
@@ -303,7 +306,7 @@
     flops = 8 * members * rows * cols * (cols + rows)
     for step in range(3):
         vector = vectors[-1]
-        message = f32((2 * HMAX if step == 1 else HMAX, cols))
+        message = f32((2 * HMAX if step < 2 else HMAX, cols))
         outs = [f32((rows, cols)), message, message]
         part, up, down = call(
             functools.partial(taper_kernel, step), outs,
@@ -317,11 +320,12 @@
         outs = [f32((rows, cols))] * 3
         if step == 1:
             outs += [f32((HMAX, cols))] * 2
-            more = [up, down, above, below]
+            more = [up, down] + masks
         image, east, west, *more = call(
             functools.partial(finish_kernel, step), outs, part, from_north, from_south, valid,
             *more, name=f"finish_{step}",
         )
+        masks = [from_north, from_south]
         vectors.append(image)
         around = [shift(east, LON, 1, True), shift(west, LON, -1, True)]
     gram = call(

time: 113 us -> 108 us (0.956)
  waiting for transfers between devices: 24.1 us -> 18.2 us
  starting transfers between devices: 59.9 us -> 64 us
  blocking collectives: 15.3 us -> 13.5 us
    ppermute x14, waiting for transfers between devices: 21.4 us -> 15.5 us  [shift(): return lax.ppermute(cells, axis, pairs)]
    ppermute x14, starting transfers between devices: 54.7 us -> 57.8 us  [shift(): return lax.ppermute(cells, axis, pairs)]
    all_to_all x1, blocking collectives: 15.3 us -> 13.5 us  [shards(): parts = lax.all_to_all(gram, ('far', 'lat'), 0, 0)]
    pallas_call x10 -> x11, Pallas kernels: 7.35 us -> 7.4 us  [call(): pl.pallas_call(kernel, out_shape=outs, compiler_params=pltpu.CompilerPara...]
  transfers between devices with their start and end apart: 15 -> 15, of which waited for: 8 -> 8; matrix products, arithmetic and copies ran while one was open for 1% -> 1% of each run, Pallas kernels for 0% -> 1%
where the time goes in v4:
time: 108 us
  starting transfers between devices  64 us (59%)
  waiting for transfers between devices  18.2 us (17%)
  blocking collectives  13.5 us (12%)
  Pallas kernels  7.4 us (7%)
  between operations  2.31 us (2%)
  local copies, waits for them, and re-layouts  1.83 us (2%)
    ppermute x14, starting transfers between devices, shift(): return lax.ppermute(cells, axis, pairs)  57.8 us
    ppermute x14, waiting for transfers between devices, shift(): return lax.ppermute(cells, axis, pairs)  15.5 us
    all_to_all x1, blocking collectives, shards(): parts = lax.all_to_all(gram, ('far', 'lat'), 0, 0)  13.5 us
    pallas_call x11, Pallas kernels, call(): pl.pallas_call(kernel, out_shape=outs, compiler_params=pltpu.CompilerPara...  7.4 us
    all_to_all x1, starting transfers between devices, shards(): parts = lax.all_to_all(parts, 'near', 0, 0)  6.2 us
    all_to_all x1, waiting for transfers between devices, shards(): parts = lax.all_to_all(parts, 'near', 0, 0)  2.73 us
  transfers between devices with their start and end apart: 15, of which 8 were waited for; matrix products, arithmetic and copies ran while one was open for 1% of the time, Pallas kernels for 1%

profile of v4, /device:TPU:1, one launch (start us, length us, event | category | flops | bytes accessed | tf_op | source)
XLA Modules:
  0.0 107.6 jit_solution(17594842360007800260)
XLA Ops:
  1.9 4.5 %collective-permute-start.2 = (bf16[64,32,128]{2,1,0:T(8,128)(2,1)S(1)}, bf16[64,32,128]{2,1,0:T(8,128)(2,1)S(1)}, u32[]{:S(2)}, u32[]{:S(2)}) collective-permute-start(bf16[64,32,128]{2,1,0:T(8,128)(2,1)S(1)} %get-tuple-element.25._), channel_id=1, source_target_pairs={{0,1},{1,2},{2,3},{3,4},{4,5},{5,6},{6,7},{7,8},{8,9},{9,10},{10,1... | collective-permute-start | bytes 1572872 | tf_op jit(solution)/shard_map/ppermute | solution.py:21
  6.5 5.6 %collective-permute-start.3 = (bf16[64,32,128]{2,1,0:T(8,128)(2,1)S(1)}, bf16[64,32,128]{2,1,0:T(8,128)(2,1)S(1)}, u32[]{:S(2)}, u32[]{:S(2)}) collective-permute-start(bf16[64,32,128]{2,1,0:T(8,128)(2,1)S(1)} %get-tuple-element.26.__), channel_id=1, source_target_pairs={{1,0},{2,1},{3,2},{4,3},{5,4},{6,5},{7,6},{8,7},{9,8},{10,9},{11,1... | collective-permute-start | bytes 1572872 | tf_op jit(solution)/shard_map/ppermute | solution.py:21
  12.6 2.1 %collective-permute-start = (bf16[19,64,128]{2,1,0:T(8,128)(2,1)S(1)}, bf16[19,64,128]{2,1,0:T(8,128)(2,1)S(1)}, u32[]{:S(2)}, u32[]{:S(2)}) collective-permute-start(bf16[19,64,128]{2,1,0:T(8,128)(2,1)S(1)} %get-tuple-element.27), channel_id=1, source_target_pairs={{0,16},{16,32},{32,48},{48,64},{64,80},{80,96},{96,112},{112,128},... | collective-permute-start | bytes 933896 | tf_op jit(solution)/shard_map/ppermute | solution.py:21
  14.6 9.6 %collective-permute-start.1 = (bf16[19,64,128]{2,1,0:T(8,128)(2,1)S(1)}, bf16[19,64,128]{2,1,0:T(8,128)(2,1)S(1)}, u32[]{:S(2)}, u32[]{:S(2)}) collective-permute-start(bf16[19,64,128]{2,1,0:T(8,128)(2,1)S(1)} %get-tuple-element.28), channel_id=1, source_target_pairs={{0,496},{16,0},{32,16},{48,32},{64,48},{80,64},{96,80},{112,96},{1... | collective-permute-start | bytes 933896 | tf_op jit(solution)/shard_map/ppermute | solution.py:21
  26.6 1.9 %collective-permute-done.from_west = bf16[19,64,128]{2,1,0:T(8,128)(2,1)S(1)} collective-permute-done((bf16[19,64,128]{2,1,0:T(8,128)(2,1)S(1)}, bf16[19,64,128]{2,1,0:T(8,128)(2,1)S(1)}, u32[]{:S(2)}, u32[]{:S(2)}) %collective-permute-start) | collective-permute-done | bytes 311328 | tf_op jit(solution)/shard_map/ppermute | solution.py:21
  28.5 1.8 %collective-permute-done.1.from_east = bf16[19,64,128]{2,1,0:T(8,128)(2,1)S(1)} collective-permute-done((bf16[19,64,128]{2,1,0:T(8,128)(2,1)S(1)}, bf16[19,64,128]{2,1,0:T(8,128)(2,1)S(1)}, u32[]{:S(2)}, u32[]{:S(2)}) %collective-permute-start.1) | collective-permute-done | bytes 311328 | tf_op jit(solution)/shard_map/ppermute | solution.py:21
  30.6 1.6 %taper_0.1 = (f32[64,128]{1,0:T(8,128)S(1)}, f32[64,128]{1,0:T(8,128)S(1)}, f32[64,128]{1,0:T(8,128)S(1)}) custom-call(f32[64,128]{1,0:T(8,128)S(1)} %copy-done.3, s32[64,128]{1,0:T(8,128)S(1)} %copy-done.2, f32[64,128]{1,0:T(8,128)S(1)} %copy-done.4, f32[64,128]{1,0:T(8,128)S(1)} %get-tuple-element.29.refs_0_, bf16[64,64,128]{2,1,0:T(8,128)(2,1)S(1)} %copy-done.1, ...), custom_call_target="tpu_custom_call" | custom-call | flops 805306368 | bytes 2981888 | tf_op jit(solution)/shard_map/taper_0/pallas_call | solution.py:271
  32.2 4.3 %collective-permute-start.4 = (f32[64,128]{1,0:T(8,128)S(1)}, f32[64,128]{1,0:T(8,128)S(1)}, u32[]{:S(2)}, u32[]{:S(2)}) collective-permute-start(f32[64,128]{1,0:T(8,128)S(1)} %get-tuple-element.32), channel_id=1, source_target_pairs={{0,1},{1,2},{2,3},{3,4},{4,5},{5,6},{6,7},{7,8},{8,9},{9,10},{10,1... | collective-permute-start | bytes 98312 | tf_op jit(solution)/shard_map/ppermute | solution.py:21
  36.5 1.9 %collective-permute-start.5 = (f32[64,128]{1,0:T(8,128)S(1)}, f32[64,128]{1,0:T(8,128)S(1)}, u32[]{:S(2)}, u32[]{:S(2)}) collective-permute-start(f32[64,128]{1,0:T(8,128)S(1)} %get-tuple-element.33), channel_id=1, source_target_pairs={{1,0},{2,1},{3,2},{4,3},{5,4},{6,5},{7,6},{8,7},{9,8},{10,9},{11,1... | collective-permute-start | bytes 98312 | tf_op jit(solution)/shard_map/ppermute | solution.py:21
  38.5 3.3 %collective-permute-done.5.from_south.refs_3_ = f32[64,128]{1,0:T(8,128)S(1)} collective-permute-done((f32[64,128]{1,0:T(8,128)S(1)}, f32[64,128]{1,0:T(8,128)S(1)}, u32[]{:S(2)}, u32[]{:S(2)}) %collective-permute-start.5) | collective-permute-done | bytes 32800 | tf_op jit(solution)/shard_map/ppermute | solution.py:21
  41.9 1.9 %collective-permute-start.6 = (f32[64,128]{1,0:T(8,128)S(1)}, f32[64,128]{1,0:T(8,128)S(1)}, u32[]{:S(2)}, u32[]{:S(2)}) collective-permute-start(f32[64,128]{1,0:T(8,128)S(1)} %get-tuple-element.35), channel_id=1, source_target_pairs={{0,16},{16,32},{32,48},{48,64},{64,80},{80,96},{96,112},{112,128},... | collective-permute-start | bytes 98312 | tf_op jit(solution)/shard_map/ppermute | solution.py:21
  43.8 8.4 %collective-permute-start.7 = (f32[64,128]{1,0:T(8,128)S(1)}, f32[64,128]{1,0:T(8,128)S(1)}, u32[]{:S(2)}, u32[]{:S(2)}) collective-permute-start(f32[64,128]{1,0:T(8,128)S(1)} %get-tuple-element.36), channel_id=1, source_target_pairs={{0,496},{16,0},{32,16},{48,32},{64,48},{80,64},{96,80},{112,96},{1... | collective-permute-start | bytes 98312 | tf_op jit(solution)/shard_map/ppermute | solution.py:21
  54.8 2.2 %collective-permute-start.8 = (f32[64,128]{1,0:T(8,128)S(1)}, f32[64,128]{1,0:T(8,128)S(1)}, u32[]{:S(2)}, u32[]{:S(2)}) collective-permute-start(f32[64,128]{1,0:T(8,128)S(1)} %get-tuple-element.38.refs_1_), channel_id=1, source_target_pairs={{0,1},{1,2},{2,3},{3,4},{4,5},{5,6},{6,7},{7,8},{8,9},{9,10},{10,1... | collective-permute-start | bytes 98312 | tf_op jit(solution)/shard_map/ppermute | solution.py:21
  57.0 2.2 %collective-permute-start.9 = (f32[64,128]{1,0:T(8,128)S(1)}, f32[64,128]{1,0:T(8,128)S(1)}, u32[]{:S(2)}, u32[]{:S(2)}) collective-permute-start(f32[64,128]{1,0:T(8,128)S(1)} %get-tuple-element.39.refs_0_), channel_id=1, source_target_pairs={{1,0},{2,1},{3,2},{4,3},{5,4},{6,5},{7,6},{8,7},{9,8},{10,9},{11,1... | collective-permute-start | bytes 98312 | tf_op jit(solution)/shard_map/ppermute | solution.py:21
  59.1 3.1 %collective-permute-done.9.from_south = f32[64,128]{1,0:T(8,128)S(1)} collective-permute-done((f32[64,128]{1,0:T(8,128)S(1)}, f32[64,128]{1,0:T(8,128)S(1)}, u32[]{:S(2)}, u32[]{:S(2)}) %collective-permute-start.9) | collective-permute-done | bytes 32800 | tf_op jit(solution)/shard_map/ppermute | solution.py:21
  62.4 1.9 %collective-permute-start.10 = (f32[64,128]{1,0:T(8,128)S(1)}, f32[64,128]{1,0:T(8,128)S(1)}, u32[]{:S(2)}, u32[]{:S(2)}) collective-permute-start(f32[64,128]{1,0:T(8,128)S(1)} %get-tuple-element.41), channel_id=1, source_target_pairs={{0,16},{16,32},{32,48},{48,64},{64,80},{80,96},{96,112},{112,128},... | collective-permute-start | bytes 98312 | tf_op jit(solution)/shard_map/ppermute | solution.py:21
  64.3 8.2 %collective-permute-start.11 = (f32[64,128]{1,0:T(8,128)S(1)}, f32[64,128]{1,0:T(8,128)S(1)}, u32[]{:S(2)}, u32[]{:S(2)}) collective-permute-start(f32[64,128]{1,0:T(8,128)S(1)} %get-tuple-element.42), channel_id=1, source_target_pairs={{0,496},{16,0},{32,16},{48,32},{64,48},{80,64},{96,80},{112,96},{1... | collective-permute-start | bytes 98312 | tf_op jit(solution)/shard_map/ppermute | solution.py:21
  73.5 1.6 %taper_2.1 = (f32[64,128]{1,0:T(8,128)S(1)}, f32[32,128]{1,0:T(8,128)S(1)}, f32[32,128]{1,0:T(8,128)S(1)}) custom-call(f32[64,128]{1,0:T(8,128)S(1)} %get-tuple-element.40.vector.v2, s32[64,128]{1,0:T(8,128)S(1)} %copy-done.2, f32[64,128]{1,0:T(8,128)S(1)} %copy-done.4, f32[64,128]{1,0:T(8,128)S(1)} %collective-permute-done.10.refs_0_, ...), custom_call_target="tpu_custom_call" | custom-call | flops 805306368 | bytes 3014656 | tf_op jit(solution)/shard_map/taper_2/pallas_call | solution.py:271
  75.2 13.5 %all_to_all.10.parts = f32[32,1,128]{2,1,0:T(1,128)S(1)} all-to-all(f32[32,1,128]{2,1,0:T(1,128)S(1)} %gram_kernel.1), channel_id=1, replica_groups=mesh['far'=2,'near'=16,'lat'=16] {'far','lat'}, dimensions={0} | all-to-all | bytes 32768 | tf_op jit(solution)/shard_map/all_to_all | solution.py:335
  89.3 6.2 %all-to-all-start.1 = ((f32[16,1,128]{2,1,0:T(1,128)}), f32[16,1,128]{2,1,0:T(1,128)S(1)}, u32[]{:S(2)}, u32[]{:S(2)}) async-start(f32[16,1,128]{2,1,0:T(1,128)} %sum_kernel.1), calls=%async_computation.1 | async-start | bytes 16384 | tf_op jit(solution)/shard_map/all_to_all | solution.py:337
  95.6 3.1 %collective-permute-start.12 = (f32[32,128]{1,0:T(8,128)S(1)}, f32[32,128]{1,0:T(8,128)S(1)}, u32[]{:S(2)}, u32[]{:S(2)}) collective-permute-start(f32[32,128]{1,0:T(8,128)S(1)} %get-tuple-element.45.down), channel_id=1, source_target_pairs={{0,1},{1,2},{2,3},{3,4},{4,5},{5,6},{6,7},{7,8},{8,9},{9,10},{10,1... | collective-permute-start | bytes 49160 | tf_op jit(solution)/shard_map/ppermute | solution.py:21
  98.7 1.9 %collective-permute-start.13 = (f32[32,128]{1,0:T(8,128)S(1)}, f32[32,128]{1,0:T(8,128)S(1)}, u32[]{:S(2)}, u32[]{:S(2)}) collective-permute-start(f32[32,128]{1,0:T(8,128)S(1)} %get-tuple-element.44.up), channel_id=1, source_target_pairs={{1,0},{2,1},{3,2},{4,3},{5,4},{6,5},{7,6},{8,7},{9,8},{10,9},{11,1... | collective-permute-start | bytes 49160 | tf_op jit(solution)/shard_map/ppermute | solution.py:21
  100.6 3.4 %collective-permute-done.13.from_south = f32[32,128]{1,0:T(8,128)S(1)} collective-permute-done((f32[32,128]{1,0:T(8,128)S(1)}, f32[32,128]{1,0:T(8,128)S(1)}, u32[]{:S(2)}, u32[]{:S(2)}) %collective-permute-start.13) | collective-permute-done | bytes 16416 | tf_op jit(solution)/shard_map/ppermute | solution.py:21
  104.0 2.7 %all-to-all-done.1.parts = f32[16,1,128]{2,1,0:T(1,128)S(1)} async-done(((f32[16,1,128]{2,1,0:T(1,128)}), f32[16,1,128]{2,1,0:T(1,128)S(1)}, u32[]{:S(2)}, u32[]{:S(2)}) %all-to-all-start.1) | async-done | bytes 8224 | tf_op jit(solution)/shard_map/all_to_all | solution.py:337
  (42 shorter events, 8.5 us)
Async XLA Ops:
  0.6 1.2 %copy-start = (bf16[64,64,128]{2,1,0:T(8,128)(2,1)S(1)}, bf16[64,64,128]{2,1,0:T(8,128)(2,1)}, u32[]{:S(2)}) copy-start(bf16[64,64,128]{2,1,0:T(8,128)(2,1)} %refs_2_.3) | copy-start | bytes 3145732
  1.9 10.2 %copy-start.2 = (s32[64,128]{1,0:T(8,128)S(1)}, s32[64,128]{1,0:T(8,128)}, u32[]{:S(2)}) copy-start(s32[64,128]{1,0:T(8,128)} %valid.11) | copy-start | bytes 98308
  1.9 10.2 %copy-start.3 = (f32[64,128]{1,0:T(8,128)S(1)}, f32[64,128]{1,0:T(8,128)}, u32[]{:S(2)}) copy-start(f32[64,128]{1,0:T(8,128)} %v0.3) | copy-start | bytes 98308
  1.9 28.7 %collective-permute-start.2 = (bf16[64,32,128]{2,1,0:T(8,128)(2,1)S(1)}, bf16[64,32,128]{2,1,0:T(8,128)(2,1)S(1)}, u32[]{:S(2)}, u32[]{:S(2)}) collective-permute-start(bf16[64,32,128]{2,1,0:T(8,128)(2,1)S(1)} %get-tuple-element.25._), channel_id=1, source_target_pairs={{0,1},{1,2},{2,3},{3,4},{4,5},{5,6},{6,7},{7,8},{8,9},{9,10},{10,1... | collective-permute-start | bytes 1572872 | tf_op jit(solution)/shard_map/ppermute | solution.py:21
  6.5 24.2 %collective-permute-start.3 = (bf16[64,32,128]{2,1,0:T(8,128)(2,1)S(1)}, bf16[64,32,128]{2,1,0:T(8,128)(2,1)S(1)}, u32[]{:S(2)}, u32[]{:S(2)}) collective-permute-start(bf16[64,32,128]{2,1,0:T(8,128)(2,1)S(1)} %get-tuple-element.26.__), channel_id=1, source_target_pairs={{1,0},{2,1},{3,2},{4,3},{5,4},{6,5},{7,6},{8,7},{9,8},{10,9},{11,1... | collective-permute-start | bytes 1572872 | tf_op jit(solution)/shard_map/ppermute | solution.py:21
  12.1 12.2 %copy-start.5 = (s32[2]{0:T(128)S(1)}, s32[2]{0:T(128)}, u32[]{:S(2)}) copy-start(s32[2]{0:T(128)} %param.9) | copy-start | bytes 28
  12.6 18.1 %copy-start.1 = (bf16[64,64,128]{2,1,0:T(8,128)(2,1)S(1)}, bf16[64,64,128]{2,1,0:T(8,128)(2,1)}, u32[]{:S(2)}) copy-start(bf16[64,64,128]{2,1,0:T(8,128)(2,1)} %refs_2_.3) | copy-start | bytes 3145732
  12.6 16.0 %collective-permute-start = (bf16[19,64,128]{2,1,0:T(8,128)(2,1)S(1)}, bf16[19,64,128]{2,1,0:T(8,128)(2,1)S(1)}, u32[]{:S(2)}, u32[]{:S(2)}) collective-permute-start(bf16[19,64,128]{2,1,0:T(8,128)(2,1)S(1)} %get-tuple-element.27), channel_id=1, source_target_pairs={{0,16},{16,32},{32,48},{48,64},{64,80},{80,96},{96,112},{112,128},... | collective-permute-start | bytes 933896 | tf_op jit(solution)/shard_map/ppermute | solution.py:21
  14.6 15.7 %collective-permute-start.1 = (bf16[19,64,128]{2,1,0:T(8,128)(2,1)S(1)}, bf16[19,64,128]{2,1,0:T(8,128)(2,1)S(1)}, u32[]{:S(2)}, u32[]{:S(2)}) collective-permute-start(bf16[19,64,128]{2,1,0:T(8,128)(2,1)S(1)} %get-tuple-element.28), channel_id=1, source_target_pairs={{0,496},{16,0},{32,16},{48,32},{64,48},{80,64},{96,80},{112,96},{1... | collective-permute-start | bytes 933896 | tf_op jit(solution)/shard_map/ppermute | solution.py:21
  26.6 4.1 %copy-start.4 = (f32[64,128]{1,0:T(8,128)S(1)}, f32[64,128]{1,0:T(8,128)}, u32[]{:S(2)}) copy-start(f32[64,128]{1,0:T(8,128)} %obs_error.5) | copy-start | bytes 98308
  32.2 6.2 %collective-permute-start.4 = (f32[64,128]{1,0:T(8,128)S(1)}, f32[64,128]{1,0:T(8,128)S(1)}, u32[]{:S(2)}, u32[]{:S(2)}) collective-permute-start(f32[64,128]{1,0:T(8,128)S(1)} %get-tuple-element.32), channel_id=1, source_target_pairs={{0,1},{1,2},{2,3},{3,4},{4,5},{5,6},{6,7},{7,8},{8,9},{9,10},{10,1... | collective-permute-start | bytes 98312 | tf_op jit(solution)/shard_map/ppermute | solution.py:21
  36.5 5.2 %collective-permute-start.5 = (f32[64,128]{1,0:T(8,128)S(1)}, f32[64,128]{1,0:T(8,128)S(1)}, u32[]{:S(2)}, u32[]{:S(2)}) collective-permute-start(f32[64,128]{1,0:T(8,128)S(1)} %get-tuple-element.33), channel_id=1, source_target_pairs={{1,0},{2,1},{3,2},{4,3},{5,4},{6,5},{7,6},{8,7},{9,8},{10,9},{11,1... | collective-permute-start | bytes 98312 | tf_op jit(solution)/shard_map/ppermute | solution.py:21
  41.9 10.3 %collective-permute-start.6 = (f32[64,128]{1,0:T(8,128)S(1)}, f32[64,128]{1,0:T(8,128)S(1)}, u32[]{:S(2)}, u32[]{:S(2)}) collective-permute-start(f32[64,128]{1,0:T(8,128)S(1)} %get-tuple-element.35), channel_id=1, source_target_pairs={{0,16},{16,32},{32,48},{48,64},{64,80},{80,96},{96,112},{112,128},... | collective-permute-start | bytes 98312 | tf_op jit(solution)/shard_map/ppermute | solution.py:21
  43.8 9.4 %collective-permute-start.7 = (f32[64,128]{1,0:T(8,128)S(1)}, f32[64,128]{1,0:T(8,128)S(1)}, u32[]{:S(2)}, u32[]{:S(2)}) collective-permute-start(f32[64,128]{1,0:T(8,128)S(1)} %get-tuple-element.36), channel_id=1, source_target_pairs={{0,496},{16,0},{32,16},{48,32},{64,48},{80,64},{96,80},{112,96},{1... | collective-permute-start | bytes 98312 | tf_op jit(solution)/shard_map/ppermute | solution.py:21
  54.8 4.3 %collective-permute-start.8 = (f32[64,128]{1,0:T(8,128)S(1)}, f32[64,128]{1,0:T(8,128)S(1)}, u32[]{:S(2)}, u32[]{:S(2)}) collective-permute-start(f32[64,128]{1,0:T(8,128)S(1)} %get-tuple-element.38.refs_1_), channel_id=1, source_target_pairs={{0,1},{1,2},{2,3},{3,4},{4,5},{5,6},{6,7},{7,8},{8,9},{9,10},{10,1... | collective-permute-start | bytes 98312 | tf_op jit(solution)/shard_map/ppermute | solution.py:21
  57.0 5.2 %collective-permute-start.9 = (f32[64,128]{1,0:T(8,128)S(1)}, f32[64,128]{1,0:T(8,128)S(1)}, u32[]{:S(2)}, u32[]{:S(2)}) collective-permute-start(f32[64,128]{1,0:T(8,128)S(1)} %get-tuple-element.39.refs_0_), channel_id=1, source_target_pairs={{1,0},{2,1},{3,2},{4,3},{5,4},{6,5},{7,6},{8,7},{9,8},{10,9},{11,1... | collective-permute-start | bytes 98312 | tf_op jit(solution)/shard_map/ppermute | solution.py:21
  62.4 10.1 %collective-permute-start.10 = (f32[64,128]{1,0:T(8,128)S(1)}, f32[64,128]{1,0:T(8,128)S(1)}, u32[]{:S(2)}, u32[]{:S(2)}) collective-permute-start(f32[64,128]{1,0:T(8,128)S(1)} %get-tuple-element.41), channel_id=1, source_target_pairs={{0,16},{16,32},{32,48},{48,64},{64,80},{80,96},{96,112},{112,128},... | collective-permute-start | bytes 98312 | tf_op jit(solution)/shard_map/ppermute | solution.py:21
  64.3 9.2 %collective-permute-start.11 = (f32[64,128]{1,0:T(8,128)S(1)}, f32[64,128]{1,0:T(8,128)S(1)}, u32[]{:S(2)}, u32[]{:S(2)}) collective-permute-start(f32[64,128]{1,0:T(8,128)S(1)} %get-tuple-element.42), channel_id=1, source_target_pairs={{0,496},{16,0},{32,16},{48,32},{64,48},{80,64},{96,80},{112,96},{1... | collective-permute-start | bytes 98312 | tf_op jit(solution)/shard_map/ppermute | solution.py:21
  89.3 17.4 %all-to-all-start.1 = ((f32[16,1,128]{2,1,0:T(1,128)}), f32[16,1,128]{2,1,0:T(1,128)S(1)}, u32[]{:S(2)}, u32[]{:S(2)}) async-start(f32[16,1,128]{2,1,0:T(1,128)} %sum_kernel.1), calls=%async_computation.1 | async-start | bytes 16384 | tf_op jit(solution)/shard_map/all_to_all | solution.py:337
  95.6 5.1 %collective-permute-start.12 = (f32[32,128]{1,0:T(8,128)S(1)}, f32[32,128]{1,0:T(8,128)S(1)}, u32[]{:S(2)}, u32[]{:S(2)}) collective-permute-start(f32[32,128]{1,0:T(8,128)S(1)} %get-tuple-element.45.down), channel_id=1, source_target_pairs={{0,1},{1,2},{2,3},{3,4},{4,5},{5,6},{6,7},{7,8},{8,9},{9,10},{10,1... | collective-permute-start | bytes 49160 | tf_op jit(solution)/shard_map/ppermute | solution.py:21
  98.7 5.4 %collective-permute-start.13 = (f32[32,128]{1,0:T(8,128)S(1)}, f32[32,128]{1,0:T(8,128)S(1)}, u32[]{:S(2)}, u32[]{:S(2)}) collective-permute-start(f32[32,128]{1,0:T(8,128)S(1)} %get-tuple-element.44.up), channel_id=1, source_target_pairs={{1,0},{2,1},{3,2},{4,3},{5,4},{6,5},{7,6},{8,7},{9,8},{10,9},{11,1... | collective-permute-start | bytes 49160 | tf_op jit(solution)/shard_map/ppermute | solution.py:21

commit v5 on v4

v5 whole, which is shorter than its diff:
```python
import functools

import jax
import jax.numpy as jnp
from jax import lax
from jax.experimental import pallas as pl
from jax.experimental.pallas import tpu as pltpu
from jax.sharding import Mesh
from jax.sharding import PartitionSpec as P

HMAX = 32
VMEM_LIMIT = 40 * 1024 * 1024


LON = ("far", "near")


def swap(cells, axis, second, closed):
    count = lax.axis_size(axis)
    partner = [((i - second) ^ 1) + second for i in range(count)]
    pairs = [(i, j % count) for i, j in enumerate(partner) if closed or 0 <= j < count]
    return lax.ppermute(cells, axis, pairs)


def taper_weight(offset, half):
    offset = offset.astype(jnp.float32)
    scale = half.astype(jnp.float32)
    ratio = offset / scale
    return jnp.where(jnp.abs(offset) <= scale, jnp.exp(-4.5 * ratio * ratio), 0.0).astype(
        jnp.bfloat16
    )


def lon_bands(half, cols, odd):
    lane = jnp.arange(cols)
    own = taper_weight(lane[:, None] - lane[None, :], half)
    first = lane % 64 < 32
    strip = jnp.where(first == (odd == 1), lane % 32 - HMAX, cols + lane % 32)
    both = jnp.arange(2 * cols)
    weight = taper_weight(strip[:, None] - both[None, :] % cols, half)
    keep = lane[:, None] // 64 == both[None, :] // cols
    side = jnp.where(keep, weight, jnp.zeros((), jnp.bfloat16))
    return jnp.concatenate([own, own]), jnp.concatenate([side, side])


def lat_band(half, rows, odd):
    row = jnp.arange(rows)
    halo = jnp.arange(HMAX)
    north, south = halo - HMAX, rows + halo
    target = jnp.concatenate(
        [row, jnp.where(odd == 1, north, south), jnp.where(odd == 1, south, north)]
    )
    source = jnp.concatenate([row, row])
    return taper_weight(source[None, :] - target[:, None], half)


def split3(x):
    hi = x.astype(jnp.bfloat16)
    rest = x - hi.astype(jnp.float32)
    mid = rest.astype(jnp.bfloat16)
    low = (rest - mid.astype(jnp.float32)).astype(jnp.bfloat16)
    return hi, mid, low


def join3(ref, first):
    parts = [ref[first + k].astype(jnp.float32) for k in range(3)]
    return parts[0] + parts[1] + parts[2]


def lanes(shape):
    return lax.broadcasted_iota(jnp.int32, shape, len(shape) - 1)


def edge_tiles(q, odd):
    lane = lanes(q.shape)
    right = jnp.where(lane >= 96, q, 0.0)
    right = right + pltpu.roll(right, 64, 1)
    right = right + pltpu.roll(right, 32, 1)
    left = jnp.where(lane < 32, q, 0.0)
    left = left + pltpu.roll(left, 64, 1)
    left = left + pltpu.roll(left, 32, 1)
    west_first = odd[0:1, :] == 1
    return jnp.where(west_first, left, right), jnp.where(west_first, right, left)


def edge_rows(x, odd):
    top, bottom = x[:HMAX], x[x.shape[0] - HMAX :]
    north_first = odd[8:9, :] == 1
    return jnp.where(north_first, top, bottom), jnp.where(north_first, bottom, top)


def rows_kernel(odd, ens, second, first):
    rows = ens.shape[1]
    north_first = odd[8:9, :] == 1
    for m in range(ens.shape[0]):
        top, bottom = ens[m, :HMAX, :], ens[m, rows - HMAX :, :]
        first[m] = jnp.where(north_first, top, bottom)
        second[m] = jnp.where(north_first, bottom, top)


def columns_kernel(odd, ens, q, _, __, second, first):
    members, rows, cols = ens.shape
    source = lax.broadcasted_iota(jnp.int32, (4 * cols, 2 * cols), 0)
    target = lax.broadcasted_iota(jnp.int32, (4 * cols, 2 * cols), 1)
    lane = target % cols
    flag = odd[0:1, :]
    east = 96 * jnp.concatenate([flag, flag], axis=1)
    wanted = (lane // 32) * cols + lane % 32 + jnp.where(target < cols, 96 - east, east)
    select = jnp.where(source == wanted, 1.0, 0.0).astype(jnp.bfloat16)
    quads = jnp.concatenate(
        [
            jnp.concatenate([ens[4 * i + g] for g in range(4)], axis=1)
            for i in range(members // 4)
        ],
        axis=0,
    )
    both = jnp.dot(quads, select, preferred_element_type=jnp.float32).astype(jnp.bfloat16)
    for i in range(members // 4):
        first[i] = both[rows * i : rows * (i + 1), :cols]
        second[i] = both[rows * i : rows * (i + 1), cols:]
    for ref, tile in zip((first, second), edge_tiles(q[...], odd)):
        for k, part in enumerate(split3(tile)):
            ref[members // 4 + k] = part


def sides_kernel(from_second, from_first, sides, q_sides):
    planes, rows, cols = sides.shape
    quads = planes // 2
    source = lax.broadcasted_iota(jnp.int32, (2 * cols, 2 * cols), 0)
    target = lax.broadcasted_iota(jnp.int32, (2 * cols, 2 * cols), 1)
    wanted = (target // 64) * 32 + target % 32 + jnp.where(target % 64 < 32, 0, cols)
    select = jnp.where(source == wanted, 1.0, 0.0).astype(jnp.bfloat16)
    pairs = jnp.concatenate(
        [jnp.concatenate([from_first[i], from_second[i]], axis=1) for i in range(quads)], axis=0
    )
    both = jnp.dot(pairs, select, preferred_element_type=jnp.float32).astype(jnp.bfloat16)
    for i in range(quads):
        for k in range(2):
            sides[2 * i + k] = both[rows * i : rows * (i + 1), k * cols : (k + 1) * cols]
    first = lanes((rows, cols)) % 64 < 32
    q_sides[...] = jnp.where(first, join3(from_first, quads), join3(from_second, quads))


def gram_lanes(vectors, last):
    lane = lanes((1, 128))
    out = jnp.where(lane == len(GRAM), last, 0.0)
    for k, (i, j) in enumerate(GRAM):
        out = jnp.where(lane == k, jnp.sum(vectors[i] * vectors[j], keepdims=True), out)
    return out


GRAM = [(0, 0), (0, 1), (0, 2), (1, 1), (1, 2), (2, 2)]


def high_low(x):
    high = x.astype(jnp.bfloat16)
    return high, (x - high.astype(jnp.float32)).astype(jnp.bfloat16)


def taper_kernel(step, odd, vector, valid, obs_error, *refs):
    if step == 0:
        q_sides, refs = refs[0][...], refs[1:]
    else:
        second, first, refs = refs[0], refs[1], refs[2:]
        q_sides = jnp.where(lanes(first.shape) % 64 < 32, first[...], second[...])
    ens, sides, rows_second, rows_first, lon_band, side_band, lat = refs[:7]
    part, to_second, to_first = refs[-3:]
    members, rows, cols = ens.shape
    count = members // 2
    maskf = valid[...].astype(jnp.float32)
    q = maskf * vector[...]
    side = jnp.concatenate(
        [
            jnp.concatenate(high_low(sides[j].astype(jnp.float32) * q_sides), axis=1)
            for j in range(count)
        ],
        axis=0,
    )
    side = jnp.dot(side, side_band[...], preferred_element_type=jnp.float32)
    main = jnp.concatenate(
        [
            jnp.concatenate(high_low(ens[m].astype(jnp.float32) * q), axis=1)
            for m in range(members)
        ],
        axis=0,
    )
    main = jnp.dot(main, lon_band[...], preferred_element_type=jnp.float32)
    total = jnp.zeros((rows + 2 * HMAX, cols), jnp.float32)
    for j in range(count):
        first = [
            main[rows * (2 * j + k) : rows * (2 * j + k + 1)]
            + side[rows * j : rows * (j + 1), cols * k : cols * (k + 1)]
            for k in range(2)
        ]
        pair = jnp.concatenate(high_low(jnp.concatenate(first, axis=1)), axis=0)
        second = jnp.dot(lat[...], pair, preferred_element_type=jnp.float32)
        for k in range(2):
            m = 2 * j + k
            there = jnp.concatenate([ens[m], rows_first[m], rows_second[m]], axis=0).astype(jnp.float32)
            total = total + there * second[:, cols * k : cols * (k + 1)]
    total = total / (members - 1)
    image = maskf * total[:rows] + obs_error[...] * vector[...]
    to_first[:HMAX] = total[rows : rows + HMAX]
    to_second[:HMAX] = total[rows + HMAX :]
    part[...] = image
    if step < 2:
        to_first[HMAX:], to_second[HMAX:] = edge_rows(maskf if step == 0 else image, odd)


def gram_kernel(v0, v1, v2, part, to_second, to_first, q_second, q_first, gram):
    vectors = [v0[...], v1[...], v2[...]]
    around = q_second[...] * to_second[...] + q_first[...] * to_first[...]
    last = jnp.sum(vectors[2] * part[...], keepdims=True) + jnp.sum(around, keepdims=True)
    gram[...] = jnp.broadcast_to(gram_lanes(vectors, last)[None], gram.shape)


def whole_image(odd, part, from_second, from_first, valid):
    first, second = from_first[:HMAX], from_second[:HMAX]
    north_first = odd[8:9, :] == 1
    around = jnp.concatenate(
        [jnp.where(north_first, first, second), jnp.where(north_first, second, first)], axis=0
    )
    maskf = valid[...].astype(jnp.float32)
    return part[...] + maskf * around, maskf


def finish_kernel(step, odd, part, from_second, from_first, valid, *refs):
    out, second, first = refs[-5:-2] if step == 1 else refs
    image, maskf = whole_image(odd, part, from_second, from_first, valid)
    out[...] = image
    first[...], second[...] = edge_tiles(maskf * image, odd)
    if step == 1:
        to_second, to_first, masks_second, masks_first = refs[:4]
        q_second, q_first = refs[-2:]
        mask = masks_second[HMAX:]
        q_second[...] = mask * (from_second[HMAX:] + mask * to_second[:HMAX])
        mask = masks_first[HMAX:]
        q_first[...] = mask * (from_first[HMAX:] + mask * to_first[:HMAX])


def sum_kernel(parts, out):
    out[...] = jnp.broadcast_to(jnp.sum(parts[...], axis=0, keepdims=True), out.shape)


def solve_kernel(odd, parts, v0, v1, v2, part, from_second, from_first, valid, weights, residual):
    sums = jnp.sum(parts[...], axis=0)
    lane = lanes(sums.shape)
    gram = {}
    for k, (i, j) in enumerate(GRAM + [(2, 3)]):
        value = jnp.sum(jnp.where(lane == k, sums, 0.0), keepdims=True)
        gram[i, j] = gram[j, i] = value
    gram[0, 3], gram[1, 3] = gram[1, 2], gram[2, 2]

    def inner(a, b):
        total = None
        for i, x in a.items():
            for j, y in b.items():
                term = x * y * gram[i, j]
                total = term if total is None else total + term
        return total

    def combine(a, scale, b):
        out = dict(a)
        for i, y in b.items():
            out[i] = out[i] + scale * y if i in out else scale * y
        return out

    one = jnp.ones((1, 1), jnp.float32)
    w, r, d = {}, {0: one}, {0: one}
    now = inner(r, r)
    for step in range(3):
        image = {i + 1: x for i, x in d.items()}
        alpha = now / inner(d, image)
        w = combine(w, alpha, d)
        r = combine(r, -alpha, image)
        if step < 2:
            later = inner(r, r)
            d = combine(r, later / now, d)
            now = later
    basis = [v0[...], v1[...], v2[...], whole_image(odd, part, from_second, from_first, valid)[0]]
    weights[...] = w[0] * basis[0] + w[1] * basis[1] + w[2] * basis[2]
    residual[...] = r[0] * basis[0] + r[1] * basis[1] + r[2] * basis[2] + r[3] * basis[3]


def call(kernel, outs, *args, name=None, flops=0, **more):
    return pl.pallas_call(
        kernel,
        out_shape=outs,
        compiler_params=pltpu.CompilerParams(vmem_limit_bytes=VMEM_LIMIT),
        cost_estimate=pl.CostEstimate(
            flops=flops, transcendentals=0, bytes_accessed=sum(a.size * a.dtype.itemsize for a in args)
        ),
        name=name or kernel.__name__,
        **more,
    )(*args)


def shards(ensemble, right_side, obs_error, valid, halfwidth):
    members, rows, cols = ensemble.shape
    quads, planes = members // 4, members // 2
    bf16 = functools.partial(jax.ShapeDtypeStruct, dtype=jnp.bfloat16)
    f32 = functools.partial(jax.ShapeDtypeStruct, dtype=jnp.float32)
    odd_lon, odd_lat = lax.axis_index(LON) % 2, lax.axis_index("lat") % 2
    odd = jnp.where(jnp.arange(16)[:, None] < 8, odd_lon, odd_lat)
    odd = jnp.broadcast_to(odd, (16, cols)).astype(jnp.int32)
    lon_band, side_band = lon_bands(halfwidth[0], cols, odd_lon)
    lat = lat_band(halfwidth[1], rows, odd_lat)
    plain = pl.BlockSpec(memory_space=pltpu.VMEM)
    anywhere = pl.BlockSpec(memory_space=pl.ANY)

    def with_odd(kernel, outs, *args, **more):
        return call(kernel, outs, odd, *args, in_specs=[plain] * (1 + len(args)), **more)

    q = valid.astype(jnp.float32) * right_side
    second, first = with_odd(rows_kernel, [bf16((members, HMAX, cols))] * 2, ensemble)
    rows_second = swap(second, "lat", 1, False)
    rows_first = swap(first, "lat", 0, False)
    second, first = call(
        columns_kernel, [bf16((quads + 3, rows, cols))] * 2, odd, ensemble, q, second, first,
        in_specs=[plain, plain, plain, anywhere, anywhere],
    )
    sides, q_sides = call(
        sides_kernel, [bf16((planes, rows, cols)), f32((rows, cols))],
        swap(second, LON, 1, True), swap(first, LON, 0, True),
    )
    around = [q_sides]
    vectors, more = [right_side], []
    flops = 8 * members * rows * cols * (cols + rows)
    for step in range(3):
        vector = vectors[-1]
        message = f32((2 * HMAX if step < 2 else HMAX, cols))
        part, to_second, to_first = with_odd(
            functools.partial(taper_kernel, step), [f32((rows, cols)), message, message],
            vector, valid, obs_error, *around, ensemble, sides, rows_second, rows_first,
            lon_band, side_band, lat, name=f"taper_{step}", flops=flops,
        )
        from_second = swap(to_second, "lat", 1, False)
        from_first = swap(to_first, "lat", 0, False)
        if step == 2:
            break
        outs = [f32((rows, cols))] * 3
        if step == 1:
            outs += [f32((HMAX, cols))] * 2
            more = [to_second, to_first] + masks
        image, second, first, *more = with_odd(
            functools.partial(finish_kernel, step), outs, part, from_second, from_first, valid,
            *more, name=f"finish_{step}",
        )
        masks = [from_second, from_first]
        vectors.append(image)
        around = [swap(second, LON, 1, True), swap(first, LON, 0, True)]
    gram = call(
        gram_kernel, f32((lax.axis_size("far") * lax.axis_size("lat"), 1, 128)),
        *vectors, part, to_second, to_first, *more,
    )
    parts = lax.all_to_all(gram, ("far", "lat"), 0, 0)
    parts = call(sum_kernel, f32((lax.axis_size("near"), 1, 128)), parts)
    parts = lax.all_to_all(parts, "near", 0, 0)
    return tuple(
        with_odd(
            solve_kernel, [f32((rows, cols))] * 2, parts, *vectors, part, from_second,
            from_first, valid,
        )
    )


def solution(mesh):
    devices = mesh.devices
    parts = 2 if devices.shape[0] % 2 == 0 else 1
    mesh = Mesh(
        devices.reshape(parts, devices.shape[0] // parts, devices.shape[1]), LON + ("lat",)
    )
    in_specs = (P(None, "lat", LON), P("lat", LON), P("lat", LON), P("lat", LON), P())
    out_specs = (P("lat", LON), P("lat", LON))
    return jax.shard_map(shards, mesh=mesh, in_specs=in_specs, out_specs=out_specs, check_vma=False)
```

time: 108 us -> 104 us (0.963)
  starting transfers between devices: 64 us -> 56.2 us
  waiting for transfers between devices: 18.2 us -> 20.5 us
  Pallas kernels: 7.4 us -> 9.35 us
    ppermute x14, starting transfers between devices: 57.8 us -> 52.7 us  [swap(): return lax.ppermute(cells, axis, pairs)]
    all_to_all x1, starting transfers between devices: 6.2 us -> 3.47 us  [shards(): parts = lax.all_to_all(parts, 'near', 0, 0)]
    all_to_all x1, waiting for transfers between devices: 2.73 us -> 5.19 us  [shards(): parts = lax.all_to_all(parts, 'near', 0, 0)]
    pallas_call x11, Pallas kernels: 7.4 us -> 9.35 us  [call(): pl.pallas_call(kernel, out_shape=outs, compiler_params=pltpu.CompilerPara...]
  transfers between devices with their start and end apart: 15 -> 15, of which waited for: 8 -> 11; matrix products, arithmetic and copies ran while one was open for 1% -> 1% of each run, Pallas kernels for 1% -> 2%
where the time goes in v5:
time: 104 us; the launch traced here: 103 us
  starting transfers between devices  56.2 us (54%)
  waiting for transfers between devices  20.5 us (20%)
  blocking collectives  12.8 us (12%)
  Pallas kernels  9.35 us (9%)
  between operations  2.3 us (2%)
  local copies, waits for them, and re-layouts  1.91 us (2%)
    ppermute x14, starting transfers between devices, swap(): return lax.ppermute(cells, axis, pairs)  52.7 us
    ppermute x14, waiting for transfers between devices, swap(): return lax.ppermute(cells, axis, pairs)  15.3 us
    all_to_all x1, blocking collectives, shards(): parts = lax.all_to_all(gram, ('far', 'lat'), 0, 0)  12.8 us
    pallas_call x11, Pallas kernels, call(): pl.pallas_call(kernel, out_shape=outs, compiler_params=pltpu.CompilerPara...  9.35 us
    all_to_all x1, waiting for transfers between devices, shards(): parts = lax.all_to_all(parts, 'near', 0, 0)  5.19 us
    all_to_all x1, starting transfers between devices, shards(): parts = lax.all_to_all(parts, 'near', 0, 0)  3.47 us
  transfers between devices with their start and end apart: 15, of which 11 were waited for; matrix products, arithmetic and copies ran while one was open for 1% of the time, Pallas kernels for 2%

profile of v5, /device:TPU:1, one launch (start us, length us, event | category | flops | bytes accessed | tf_op | source)
XLA Modules:
  0.0 103.5 jit_solution(5173913177056054798)
XLA Ops:
  2.1 4.5 %collective-permute-start.2 = (bf16[64,32,128]{2,1,0:T(8,128)(2,1)S(1)}, bf16[64,32,128]{2,1,0:T(8,128)(2,1)S(1)}, u32[]{:S(2)}, u32[]{:S(2)}) collective-permute-start(bf16[64,32,128]{2,1,0:T(8,128)(2,1)S(1)} %get-tuple-element.25._), channel_id=1, source_target_pairs={{1,2},{2,1},{3,4},{4,3},{5,6},{6,5},{7,8},{8,7},{9,10},{10,9},{11,... | collective-permute-start | bytes 1572872 | tf_op jit(solution)/shard_map/ppermute | solution.py:22
  6.7 5.0 %collective-permute-start.3 = (bf16[64,32,128]{2,1,0:T(8,128)(2,1)S(1)}, bf16[64,32,128]{2,1,0:T(8,128)(2,1)S(1)}, u32[]{:S(2)}, u32[]{:S(2)}) collective-permute-start(bf16[64,32,128]{2,1,0:T(8,128)(2,1)S(1)} %get-tuple-element.26.__), channel_id=1, source_target_pairs={{0,1},{1,0},{2,3},{3,2},{4,5},{5,4},{6,7},{7,6},{8,9},{9,8},{10,11... | collective-permute-start | bytes 1572872 | tf_op jit(solution)/shard_map/ppermute | solution.py:22
  13.0 10.4 %collective-permute-start = (bf16[19,64,128]{2,1,0:T(8,128)(2,1)}, bf16[19,64,128]{2,1,0:T(8,128)(2,1)S(1)}, u32[]{:S(2)}, u32[]{:S(2)}) collective-permute-start(bf16[19,64,128]{2,1,0:T(8,128)(2,1)} %get-tuple-element.27), channel_id=1, source_target_pairs={{0,496},{16,32},{32,16},{48,64},{64,48},{80,96},{96,80},{112,128},... | collective-permute-start | bytes 933896 | tf_op jit(solution)/shard_map/ppermute | solution.py:22
  23.3 1.9 %collective-permute-start.1 = (bf16[19,64,128]{2,1,0:T(8,128)(2,1)}, bf16[19,64,128]{2,1,0:T(8,128)(2,1)}, u32[]{:S(2)}, u32[]{:S(2)}) collective-permute-start(bf16[19,64,128]{2,1,0:T(8,128)(2,1)} %get-tuple-element.28), channel_id=1, source_target_pairs={{0,16},{16,0},{32,48},{48,32},{64,80},{80,64},{96,112},{112,96},{1... | collective-permute-start | bytes 933896 | tf_op jit(solution)/shard_map/ppermute | solution.py:22
  27.6 3.2 %collective-permute-done.from_second = bf16[19,64,128]{2,1,0:T(8,128)(2,1)S(1)} collective-permute-done((bf16[19,64,128]{2,1,0:T(8,128)(2,1)}, bf16[19,64,128]{2,1,0:T(8,128)(2,1)S(1)}, u32[]{:S(2)}, u32[]{:S(2)}) %collective-permute-start) | collective-permute-done | bytes 311328 | tf_op jit(solution)/shard_map/ppermute | solution.py:22
  30.8 2.8 %collective-permute-done.1.from_first = bf16[19,64,128]{2,1,0:T(8,128)(2,1)} collective-permute-done((bf16[19,64,128]{2,1,0:T(8,128)(2,1)}, bf16[19,64,128]{2,1,0:T(8,128)(2,1)}, u32[]{:S(2)}, u32[]{:S(2)}) %collective-permute-start.1) | collective-permute-done | bytes 311328 | tf_op jit(solution)/shard_map/ppermute | solution.py:22
  35.0 1.6 %taper_0.1 = (f32[64,128]{1,0:T(8,128)S(1)}, f32[64,128]{1,0:T(8,128)S(1)}, f32[64,128]{1,0:T(8,128)S(1)}) custom-call(s32[16,128]{1,0:T(8,128)S(1)} %broadcast_in_dim.37.odd, f32[64,128]{1,0:T(8,128)S(1)} %copy-done.3, s32[64,128]{1,0:T(8,128)S(1)} %copy-done.2, f32[64,128]{1,0:T(8,128)S(1)} %copy-done.4, f32[64,128]{1,0:T(8,128)S(1)} %get-tuple-element.29.refs_0_, ...), custom_call_target="tpu_custom_call" | custom-call | flops 805306368 | bytes 2990080 | tf_op jit(solution)/shard_map/taper_0/pallas_call | solution.py:286
  36.5 4.4 %collective-permute-start.4 = (f32[64,128]{1,0:T(8,128)S(1)}, f32[64,128]{1,0:T(8,128)S(1)}, u32[]{:S(2)}, u32[]{:S(2)}) collective-permute-start(f32[64,128]{1,0:T(8,128)S(1)} %get-tuple-element.32), channel_id=1, source_target_pairs={{1,2},{2,1},{3,4},{4,3},{5,6},{6,5},{7,8},{8,7},{9,10},{10,9},{11,... | collective-permute-start | bytes 98312 | tf_op jit(solution)/shard_map/ppermute | solution.py:22
  41.0 1.9 %collective-permute-start.5 = (f32[64,128]{1,0:T(8,128)S(1)}, f32[64,128]{1,0:T(8,128)S(1)}, u32[]{:S(2)}, u32[]{:S(2)}) collective-permute-start(f32[64,128]{1,0:T(8,128)S(1)} %get-tuple-element.33), channel_id=1, source_target_pairs={{0,1},{1,0},{2,3},{3,2},{4,5},{5,4},{6,7},{7,6},{8,9},{9,8},{10,11... | collective-permute-start | bytes 98312 | tf_op jit(solution)/shard_map/ppermute | solution.py:22
  44.2 4.2 %collective-permute-start.6 = (f32[64,128]{1,0:T(8,128)S(1)}, f32[64,128]{1,0:T(8,128)S(1)}, u32[]{:S(2)}, u32[]{:S(2)}) collective-permute-start(f32[64,128]{1,0:T(8,128)S(1)} %get-tuple-element.35), channel_id=1, source_target_pairs={{0,496},{16,32},{32,16},{48,64},{64,48},{80,96},{96,80},{112,128},... | collective-permute-start | bytes 98312 | tf_op jit(solution)/shard_map/ppermute | solution.py:22
  48.4 1.9 %collective-permute-start.7 = (f32[64,128]{1,0:T(8,128)S(1)}, f32[64,128]{1,0:T(8,128)S(1)}, u32[]{:S(2)}, u32[]{:S(2)}) collective-permute-start(f32[64,128]{1,0:T(8,128)S(1)} %get-tuple-element.36), channel_id=1, source_target_pairs={{0,16},{16,0},{32,48},{48,32},{64,80},{80,64},{96,112},{112,96},{1... | collective-permute-start | bytes 98312 | tf_op jit(solution)/shard_map/ppermute | solution.py:22
  50.4 2.1 %collective-permute-done.6.refs_0_ = f32[64,128]{1,0:T(8,128)S(1)} collective-permute-done((f32[64,128]{1,0:T(8,128)S(1)}, f32[64,128]{1,0:T(8,128)S(1)}, u32[]{:S(2)}, u32[]{:S(2)}) %collective-permute-start.6) | collective-permute-done | bytes 32800 | tf_op jit(solution)/shard_map/ppermute | solution.py:22
  53.4 1.6 %taper_1.1 = (f32[64,128]{1,0:T(8,128)S(1)}, f32[64,128]{1,0:T(8,128)S(1)}, f32[64,128]{1,0:T(8,128)S(1)}) custom-call(s32[16,128]{1,0:T(8,128)S(1)} %broadcast_in_dim.37.odd, f32[64,128]{1,0:T(8,128)S(1)} %get-tuple-element.34.vector.v1, s32[64,128]{1,0:T(8,128)S(1)} %copy-done.2, f32[64,128]{1,0:T(8,128)S(1)} %copy-done.4, ...), custom_call_target="tpu_custom_call" | custom-call | flops 805306368 | bytes 3022848 | tf_op jit(solution)/shard_map/taper_1/pallas_call | solution.py:286
  55.0 3.7 %collective-permute-start.8 = (f32[64,128]{1,0:T(8,128)S(1)}, f32[64,128]{1,0:T(8,128)S(1)}, u32[]{:S(2)}, u32[]{:S(2)}) collective-permute-start(f32[64,128]{1,0:T(8,128)S(1)} %get-tuple-element.38.refs_0_), channel_id=1, source_target_pairs={{1,2},{2,1},{3,4},{4,3},{5,6},{6,5},{7,8},{8,7},{9,10},{10,9},{11,... | collective-permute-start | bytes 98312 | tf_op jit(solution)/shard_map/ppermute | solution.py:22
  58.7 1.9 %collective-permute-start.9 = (f32[64,128]{1,0:T(8,128)S(1)}, f32[64,128]{1,0:T(8,128)S(1)}, u32[]{:S(2)}, u32[]{:S(2)}) collective-permute-start(f32[64,128]{1,0:T(8,128)S(1)} %get-tuple-element.39.refs_1_), channel_id=1, source_target_pairs={{0,1},{1,0},{2,3},{3,2},{4,5},{5,4},{6,7},{7,6},{8,9},{9,8},{10,11... | collective-permute-start | bytes 98312 | tf_op jit(solution)/shard_map/ppermute | solution.py:22
  62.0 6.2 %collective-permute-start.10 = (f32[64,128]{1,0:T(8,128)S(1)}, f32[64,128]{1,0:T(8,128)S(1)}, u32[]{:S(2)}, u32[]{:S(2)}) collective-permute-start(f32[64,128]{1,0:T(8,128)S(1)} %get-tuple-element.41), channel_id=1, source_target_pairs={{0,496},{16,32},{32,16},{48,64},{64,48},{80,96},{96,80},{112,128},... | collective-permute-start | bytes 98312 | tf_op jit(solution)/shard_map/ppermute | solution.py:22
  68.2 1.9 %collective-permute-start.11 = (f32[64,128]{1,0:T(8,128)S(1)}, f32[64,128]{1,0:T(8,128)S(1)}, u32[]{:S(2)}, u32[]{:S(2)}) collective-permute-start(f32[64,128]{1,0:T(8,128)S(1)} %get-tuple-element.42), channel_id=1, source_target_pairs={{0,16},{16,0},{32,48},{48,32},{64,80},{80,64},{96,112},{112,96},{1... | collective-permute-start | bytes 98312 | tf_op jit(solution)/shard_map/ppermute | solution.py:22
  70.2 2.6 %collective-permute-done.11.refs_1_ = f32[64,128]{1,0:T(8,128)S(1)} collective-permute-done((f32[64,128]{1,0:T(8,128)S(1)}, f32[64,128]{1,0:T(8,128)S(1)}, u32[]{:S(2)}, u32[]{:S(2)}) %collective-permute-start.11) | collective-permute-done | bytes 32800 | tf_op jit(solution)/shard_map/ppermute | solution.py:22
  72.8 1.6 %taper_2.1 = (f32[64,128]{1,0:T(8,128)S(1)}, f32[32,128]{1,0:T(8,128)S(1)}, f32[32,128]{1,0:T(8,128)S(1)}) custom-call(s32[16,128]{1,0:T(8,128)S(1)} %broadcast_in_dim.37.odd, f32[64,128]{1,0:T(8,128)S(1)} %get-tuple-element.40.vector.v2, s32[64,128]{1,0:T(8,128)S(1)} %copy-done.2, f32[64,128]{1,0:T(8,128)S(1)} %copy-done.4, ...), custom_call_target="tpu_custom_call" | custom-call | flops 805306368 | bytes 3022848 | tf_op jit(solution)/shard_map/taper_2/pallas_call | solution.py:286
  74.5 12.8 %all_to_all.10.parts = f32[32,1,128]{2,1,0:T(1,128)S(1)} all-to-all(f32[32,1,128]{2,1,0:T(1,128)S(1)} %gram_kernel.1), channel_id=1, replica_groups=mesh['far'=2,'near'=16,'lat'=16] {'far','lat'}, dimensions={0} | all-to-all | bytes 32768 | tf_op jit(solution)/shard_map/all_to_all | solution.py:356
  88.0 3.5 %all-to-all-start.1 = ((f32[16,1,128]{2,1,0:T(1,128)}), f32[16,1,128]{2,1,0:T(1,128)S(1)}, u32[]{:S(2)}, u32[]{:S(2)}) async-start(f32[16,1,128]{2,1,0:T(1,128)} %sum_kernel.1), calls=%async_computation.1 | async-start | bytes 16384 | tf_op jit(solution)/shard_map/all_to_all | solution.py:358
  91.5 2.9 %collective-permute-start.12 = (f32[32,128]{1,0:T(8,128)S(1)}, f32[32,128]{1,0:T(8,128)S(1)}, u32[]{:S(2)}, u32[]{:S(2)}) collective-permute-start(f32[32,128]{1,0:T(8,128)S(1)} %get-tuple-element.44.to_second), channel_id=1, source_target_pairs={{1,2},{2,1},{3,4},{4,3},{5,6},{6,5},{7,8},{8,7},{9,10},{10,9},{11,... | collective-permute-start | bytes 49160 | tf_op jit(solution)/shard_map/ppermute | solution.py:22
  94.3 1.9 %collective-permute-start.13 = (f32[32,128]{1,0:T(8,128)S(1)}, f32[32,128]{1,0:T(8,128)S(1)}, u32[]{:S(2)}, u32[]{:S(2)}) collective-permute-start(f32[32,128]{1,0:T(8,128)S(1)} %get-tuple-element.45.to_first), channel_id=1, source_target_pairs={{0,1},{1,0},{2,3},{3,2},{4,5},{5,4},{6,7},{7,6},{8,9},{9,8},{10,11... | collective-permute-start | bytes 49160 | tf_op jit(solution)/shard_map/ppermute | solution.py:22
  97.4 5.2 %all-to-all-done.1.parts = f32[16,1,128]{2,1,0:T(1,128)S(1)} async-done(((f32[16,1,128]{2,1,0:T(1,128)}), f32[16,1,128]{2,1,0:T(1,128)S(1)}, u32[]{:S(2)}, u32[]{:S(2)}) %all-to-all-start.1) | async-done | bytes 8224 | tf_op jit(solution)/shard_map/all_to_all | solution.py:358
  (44 shorter events, 11.5 us)
Async XLA Ops:
  0.7 1.2 %copy-start = (bf16[64,64,128]{2,1,0:T(8,128)(2,1)S(1)}, bf16[64,64,128]{2,1,0:T(8,128)(2,1)}, u32[]{:S(2)}) copy-start(bf16[64,64,128]{2,1,0:T(8,128)(2,1)} %refs_2_.3) | copy-start | bytes 3145732
  2.0 9.7 %copy-start.2 = (s32[64,128]{1,0:T(8,128)S(1)}, s32[64,128]{1,0:T(8,128)}, u32[]{:S(2)}) copy-start(s32[64,128]{1,0:T(8,128)} %valid.11) | copy-start | bytes 98308
  2.0 9.7 %copy-start.3 = (f32[64,128]{1,0:T(8,128)S(1)}, f32[64,128]{1,0:T(8,128)}, u32[]{:S(2)}) copy-start(f32[64,128]{1,0:T(8,128)} %v0.3) | copy-start | bytes 98308
  2.1 32.8 %collective-permute-start.2 = (bf16[64,32,128]{2,1,0:T(8,128)(2,1)S(1)}, bf16[64,32,128]{2,1,0:T(8,128)(2,1)S(1)}, u32[]{:S(2)}, u32[]{:S(2)}) collective-permute-start(bf16[64,32,128]{2,1,0:T(8,128)(2,1)S(1)} %get-tuple-element.25._), channel_id=1, source_target_pairs={{1,2},{2,1},{3,4},{4,3},{5,6},{6,5},{7,8},{8,7},{9,10},{10,9},{11,... | collective-permute-start | bytes 1572872 | tf_op jit(solution)/shard_map/ppermute | solution.py:22
  6.7 28.3 %collective-permute-start.3 = (bf16[64,32,128]{2,1,0:T(8,128)(2,1)S(1)}, bf16[64,32,128]{2,1,0:T(8,128)(2,1)S(1)}, u32[]{:S(2)}, u32[]{:S(2)}) collective-permute-start(bf16[64,32,128]{2,1,0:T(8,128)(2,1)S(1)} %get-tuple-element.26.__), channel_id=1, source_target_pairs={{0,1},{1,0},{2,3},{3,2},{4,5},{5,4},{6,7},{7,6},{8,9},{9,8},{10,11... | collective-permute-start | bytes 1572872 | tf_op jit(solution)/shard_map/ppermute | solution.py:22
  11.7 13.6 %copy-start.5 = (s32[2]{0:T(128)S(1)}, s32[2]{0:T(128)}, u32[]{:S(2)}) copy-start(s32[2]{0:T(128)} %param.9) | copy-start | bytes 28
  13.0 22.0 %copy-start.1 = (bf16[64,64,128]{2,1,0:T(8,128)(2,1)S(1)}, bf16[64,64,128]{2,1,0:T(8,128)(2,1)}, u32[]{:S(2)}) copy-start(bf16[64,64,128]{2,1,0:T(8,128)(2,1)} %refs_2_.3) | copy-start | bytes 3145732
  13.0 17.8 %collective-permute-start = (bf16[19,64,128]{2,1,0:T(8,128)(2,1)}, bf16[19,64,128]{2,1,0:T(8,128)(2,1)S(1)}, u32[]{:S(2)}, u32[]{:S(2)}) collective-permute-start(bf16[19,64,128]{2,1,0:T(8,128)(2,1)} %get-tuple-element.27), channel_id=1, source_target_pairs={{0,496},{16,32},{32,16},{48,64},{64,48},{80,96},{96,80},{112,128},... | collective-permute-start | bytes 933896 | tf_op jit(solution)/shard_map/ppermute | solution.py:22
  23.3 10.3 %collective-permute-start.1 = (bf16[19,64,128]{2,1,0:T(8,128)(2,1)}, bf16[19,64,128]{2,1,0:T(8,128)(2,1)}, u32[]{:S(2)}, u32[]{:S(2)}) collective-permute-start(bf16[19,64,128]{2,1,0:T(8,128)(2,1)} %get-tuple-element.28), channel_id=1, source_target_pairs={{0,16},{16,0},{32,48},{48,32},{64,80},{80,64},{96,112},{112,96},{1... | collective-permute-start | bytes 933896 | tf_op jit(solution)/shard_map/ppermute | solution.py:22
  27.6 7.3 %copy-start.4 = (f32[64,128]{1,0:T(8,128)S(1)}, f32[64,128]{1,0:T(8,128)}, u32[]{:S(2)}) copy-start(f32[64,128]{1,0:T(8,128)} %obs_error.5) | copy-start | bytes 98308
  36.5 6.4 %collective-permute-start.4 = (f32[64,128]{1,0:T(8,128)S(1)}, f32[64,128]{1,0:T(8,128)S(1)}, u32[]{:S(2)}, u32[]{:S(2)}) collective-permute-start(f32[64,128]{1,0:T(8,128)S(1)} %get-tuple-element.32), channel_id=1, source_target_pairs={{1,2},{2,1},{3,4},{4,3},{5,6},{6,5},{7,8},{8,7},{9,10},{10,9},{11,... | collective-permute-start | bytes 98312 | tf_op jit(solution)/shard_map/ppermute | solution.py:22
  41.0 3.1 %collective-permute-start.5 = (f32[64,128]{1,0:T(8,128)S(1)}, f32[64,128]{1,0:T(8,128)S(1)}, u32[]{:S(2)}, u32[]{:S(2)}) collective-permute-start(f32[64,128]{1,0:T(8,128)S(1)} %get-tuple-element.33), channel_id=1, source_target_pairs={{0,1},{1,0},{2,3},{3,2},{4,5},{5,4},{6,7},{7,6},{8,9},{9,8},{10,11... | collective-permute-start | bytes 98312 | tf_op jit(solution)/shard_map/ppermute | solution.py:22
  44.2 8.3 %collective-permute-start.6 = (f32[64,128]{1,0:T(8,128)S(1)}, f32[64,128]{1,0:T(8,128)S(1)}, u32[]{:S(2)}, u32[]{:S(2)}) collective-permute-start(f32[64,128]{1,0:T(8,128)S(1)} %get-tuple-element.35), channel_id=1, source_target_pairs={{0,496},{16,32},{32,16},{48,64},{64,48},{80,96},{96,80},{112,128},... | collective-permute-start | bytes 98312 | tf_op jit(solution)/shard_map/ppermute | solution.py:22
  48.4 5.0 %collective-permute-start.7 = (f32[64,128]{1,0:T(8,128)S(1)}, f32[64,128]{1,0:T(8,128)S(1)}, u32[]{:S(2)}, u32[]{:S(2)}) collective-permute-start(f32[64,128]{1,0:T(8,128)S(1)} %get-tuple-element.36), channel_id=1, source_target_pairs={{0,16},{16,0},{32,48},{48,32},{64,80},{80,64},{96,112},{112,96},{1... | collective-permute-start | bytes 98312 | tf_op jit(solution)/shard_map/ppermute | solution.py:22
  55.0 5.7 %collective-permute-start.8 = (f32[64,128]{1,0:T(8,128)S(1)}, f32[64,128]{1,0:T(8,128)S(1)}, u32[]{:S(2)}, u32[]{:S(2)}) collective-permute-start(f32[64,128]{1,0:T(8,128)S(1)} %get-tuple-element.38.refs_0_), channel_id=1, source_target_pairs={{1,2},{2,1},{3,4},{4,3},{5,6},{6,5},{7,8},{8,7},{9,10},{10,9},{11,... | collective-permute-start | bytes 98312 | tf_op jit(solution)/shard_map/ppermute | solution.py:22
  58.7 3.1 %collective-permute-start.9 = (f32[64,128]{1,0:T(8,128)S(1)}, f32[64,128]{1,0:T(8,128)S(1)}, u32[]{:S(2)}, u32[]{:S(2)}) collective-permute-start(f32[64,128]{1,0:T(8,128)S(1)} %get-tuple-element.39.refs_1_), channel_id=1, source_target_pairs={{0,1},{1,0},{2,3},{3,2},{4,5},{5,4},{6,7},{7,6},{8,9},{9,8},{10,11... | collective-permute-start | bytes 98312 | tf_op jit(solution)/shard_map/ppermute | solution.py:22
  62.0 8.3 %collective-permute-start.10 = (f32[64,128]{1,0:T(8,128)S(1)}, f32[64,128]{1,0:T(8,128)S(1)}, u32[]{:S(2)}, u32[]{:S(2)}) collective-permute-start(f32[64,128]{1,0:T(8,128)S(1)} %get-tuple-element.41), channel_id=1, source_target_pairs={{0,496},{16,32},{32,16},{48,64},{64,48},{80,96},{96,80},{112,128},... | collective-permute-start | bytes 98312 | tf_op jit(solution)/shard_map/ppermute | solution.py:22
  68.2 4.7 %collective-permute-start.11 = (f32[64,128]{1,0:T(8,128)S(1)}, f32[64,128]{1,0:T(8,128)S(1)}, u32[]{:S(2)}, u32[]{:S(2)}) collective-permute-start(f32[64,128]{1,0:T(8,128)S(1)} %get-tuple-element.42), channel_id=1, source_target_pairs={{0,16},{16,0},{32,48},{48,32},{64,80},{80,64},{96,112},{112,96},{1... | collective-permute-start | bytes 98312 | tf_op jit(solution)/shard_map/ppermute | solution.py:22
  88.0 14.6 %all-to-all-start.1 = ((f32[16,1,128]{2,1,0:T(1,128)}), f32[16,1,128]{2,1,0:T(1,128)S(1)}, u32[]{:S(2)}, u32[]{:S(2)}) async-start(f32[16,1,128]{2,1,0:T(1,128)} %sum_kernel.1), calls=%async_computation.1 | async-start | bytes 16384 | tf_op jit(solution)/shard_map/all_to_all | solution.py:358
  91.5 5.4 %collective-permute-start.12 = (f32[32,128]{1,0:T(8,128)S(1)}, f32[32,128]{1,0:T(8,128)S(1)}, u32[]{:S(2)}, u32[]{:S(2)}) collective-permute-start(f32[32,128]{1,0:T(8,128)S(1)} %get-tuple-element.44.to_second), channel_id=1, source_target_pairs={{1,2},{2,1},{3,4},{4,3},{5,6},{6,5},{7,8},{8,7},{9,10},{10,9},{11,... | collective-permute-start | bytes 49160 | tf_op jit(solution)/shard_map/ppermute | solution.py:22
  94.3 3.1 %collective-permute-start.13 = (f32[32,128]{1,0:T(8,128)S(1)}, f32[32,128]{1,0:T(8,128)S(1)}, u32[]{:S(2)}, u32[]{:S(2)}) collective-permute-start(f32[32,128]{1,0:T(8,128)S(1)} %get-tuple-element.45.to_first), channel_id=1, source_target_pairs={{0,1},{1,0},{2,3},{3,2},{4,5},{5,4},{6,7},{7,6},{8,9},{9,8},{10,11... | collective-permute-start | bytes 49160 | tf_op jit(solution)/shard_map/ppermute | solution.py:22

commit v6 on v5

--- a/solution.py
+++ b/solution.py
@@ -48,23 +48,16 @@
     halo = jnp.arange(HMAX)
     north, south = halo - HMAX, rows + halo
     target = jnp.concatenate(
-        [row, jnp.where(odd == 1, north, south), jnp.where(odd == 1, south, north)]
-    )
-    source = jnp.concatenate([row, row])
+        [jnp.where(odd == 1, north, south), jnp.where(odd == 1, south, north)]
+    )
+    own = jnp.where(odd == 1, row, (row + HMAX) % rows)
+    target = jnp.concatenate([own, target])
+    source = jnp.concatenate([own, own])
     return taper_weight(source[None, :] - target[:, None], half)
 
 
-def split3(x):
-    hi = x.astype(jnp.bfloat16)
-    rest = x - hi.astype(jnp.float32)
-    mid = rest.astype(jnp.bfloat16)
-    low = (rest - mid.astype(jnp.float32)).astype(jnp.bfloat16)
-    return hi, mid, low
-
-
-def join3(ref, first):
-    parts = [ref[first + k].astype(jnp.float32) for k in range(3)]
-    return parts[0] + parts[1] + parts[2]
+def joined(ref, first):
+    return ref[first].astype(jnp.float32) + ref[first + 1].astype(jnp.float32)
 
 
 def lanes(shape):
@@ -83,23 +76,29 @@
     return jnp.where(west_first, left, right), jnp.where(west_first, right, left)
 
 
+def by_partner(x, odd):
+    turned = jnp.concatenate([x[HMAX:], x[:HMAX]], axis=0)
+    return jnp.where(odd[1:2, :] == 1, x, turned)
+
+
 def edge_rows(x, odd):
     top, bottom = x[:HMAX], x[x.shape[0] - HMAX :]
-    north_first = odd[8:9, :] == 1
+    north_first = odd[1:2, :] == 1
     return jnp.where(north_first, top, bottom), jnp.where(north_first, bottom, top)
 
 
 def rows_kernel(odd, ens, second, first):
     rows = ens.shape[1]
-    north_first = odd[8:9, :] == 1
+    north_first = odd[1:2, :] == 1
     for m in range(ens.shape[0]):
         top, bottom = ens[m, :HMAX, :], ens[m, rows - HMAX :, :]
         first[m] = jnp.where(north_first, top, bottom)
         second[m] = jnp.where(north_first, bottom, top)
 
 
-def columns_kernel(odd, ens, q, _, __, second, first):
-    members, rows, cols = ens.shape
+def columns_kernel(odd, q, half_second, half_first, second, first):
+    members, half, cols = half_first.shape
+    rows = 2 * half
     source = lax.broadcasted_iota(jnp.int32, (4 * cols, 2 * cols), 0)
     target = lax.broadcasted_iota(jnp.int32, (4 * cols, 2 * cols), 1)
     lane = target % cols
@@ -109,8 +108,9 @@
     select = jnp.where(source == wanted, 1.0, 0.0).astype(jnp.bfloat16)
     quads = jnp.concatenate(
         [
-            jnp.concatenate([ens[4 * i + g] for g in range(4)], axis=1)
+            jnp.concatenate([ref[4 * i + g] for g in range(4)], axis=1)
             for i in range(members // 4)
+            for ref in (half_first, half_second)
         ],
         axis=0,
     )
@@ -118,8 +118,8 @@
     for i in range(members // 4):
         first[i] = both[rows * i : rows * (i + 1), :cols]
         second[i] = both[rows * i : rows * (i + 1), cols:]
-    for ref, tile in zip((first, second), edge_tiles(q[...], odd)):
-        for k, part in enumerate(split3(tile)):
+    for ref, tile in zip((first, second), edge_tiles(by_partner(q[...], odd), odd)):
+        for k, part in enumerate(high_low(tile)):
             ref[members // 4 + k] = part
 
 
@@ -138,7 +138,7 @@
         for k in range(2):
             sides[2 * i + k] = both[rows * i : rows * (i + 1), k * cols : (k + 1) * cols]
     first = lanes((rows, cols)) % 64 < 32
-    q_sides[...] = jnp.where(first, join3(from_first, quads), join3(from_second, quads))
+    q_sides[...] = jnp.where(first, joined(from_first, quads), joined(from_second, quads))
 
 
 def gram_lanes(vectors, last):
@@ -163,12 +163,15 @@
     else:
         second, first, refs = refs[0], refs[1], refs[2:]
         q_sides = jnp.where(lanes(first.shape) % 64 < 32, first[...], second[...])
-    ens, sides, rows_second, rows_first, lon_band, side_band, lat = refs[:7]
+    half_second, half_first, sides, rows_second, rows_first = refs[:5]
+    lon_band, side_band, lat = refs[5:8]
     part, to_second, to_first = refs[-3:]
-    members, rows, cols = ens.shape
+    rows, cols = vector.shape
+    members = half_first.shape[0]
     count = members // 2
     maskf = valid[...].astype(jnp.float32)
-    q = maskf * vector[...]
+    q = by_partner(maskf * vector[...], odd)
+    ens = [jnp.concatenate([half_first[m], half_second[m]], axis=0) for m in range(members)]
     side = jnp.concatenate(
         [
             jnp.concatenate(high_low(sides[j].astype(jnp.float32) * q_sides), axis=1)
@@ -199,7 +202,7 @@
             there = jnp.concatenate([ens[m], rows_first[m], rows_second[m]], axis=0).astype(jnp.float32)
             total = total + there * second[:, cols * k : cols * (k + 1)]
     total = total / (members - 1)
-    image = maskf * total[:rows] + obs_error[...] * vector[...]
+    image = maskf * by_partner(total[:rows], odd) + obs_error[...] * vector[...]
     to_first[:HMAX] = total[rows : rows + HMAX]
     to_second[:HMAX] = total[rows + HMAX :]
     part[...] = image
@@ -216,7 +219,7 @@
 
 def whole_image(odd, part, from_second, from_first, valid):
     first, second = from_first[:HMAX], from_second[:HMAX]
-    north_first = odd[8:9, :] == 1
+    north_first = odd[1:2, :] == 1
     around = jnp.concatenate(
         [jnp.where(north_first, first, second), jnp.where(north_first, second, first)], axis=0
     )
@@ -228,7 +231,7 @@
     out, second, first = refs[-5:-2] if step == 1 else refs
     image, maskf = whole_image(odd, part, from_second, from_first, valid)
     out[...] = image
-    first[...], second[...] = edge_tiles(maskf * image, odd)
+    first[...], second[...] = edge_tiles(by_partner(maskf * image, odd), odd)
     if step == 1:
         to_second, to_first, masks_second, masks_first = refs[:4]
         q_second, q_first = refs[-2:]
@@ -301,23 +304,21 @@
     bf16 = functools.partial(jax.ShapeDtypeStruct, dtype=jnp.bfloat16)
     f32 = functools.partial(jax.ShapeDtypeStruct, dtype=jnp.float32)
     odd_lon, odd_lat = lax.axis_index(LON) % 2, lax.axis_index("lat") % 2
-    odd = jnp.where(jnp.arange(16)[:, None] < 8, odd_lon, odd_lat)
-    odd = jnp.broadcast_to(odd, (16, cols)).astype(jnp.int32)
+    odd = jnp.where(jnp.arange(8)[:, None] == 0, odd_lon, odd_lat)
+    odd = jnp.broadcast_to(odd, (8, cols)).astype(jnp.int32)
     lon_band, side_band = lon_bands(halfwidth[0], cols, odd_lon)
     lat = lat_band(halfwidth[1], rows, odd_lat)
     plain = pl.BlockSpec(memory_space=pltpu.VMEM)
-    anywhere = pl.BlockSpec(memory_space=pl.ANY)
 
     def with_odd(kernel, outs, *args, **more):
         return call(kernel, outs, odd, *args, in_specs=[plain] * (1 + len(args)), **more)
 
     q = valid.astype(jnp.float32) * right_side
-    second, first = with_odd(rows_kernel, [bf16((members, HMAX, cols))] * 2, ensemble)
-    rows_second = swap(second, "lat", 1, False)
-    rows_first = swap(first, "lat", 0, False)
-    second, first = call(
-        columns_kernel, [bf16((quads + 3, rows, cols))] * 2, odd, ensemble, q, second, first,
-        in_specs=[plain, plain, plain, anywhere, anywhere],
+    halves = with_odd(rows_kernel, [bf16((members, HMAX, cols))] * 2, ensemble)
+    rows_second = swap(halves[0], "lat", 1, False)
+    rows_first = swap(halves[1], "lat", 0, False)
+    second, first = with_odd(
+        columns_kernel, [bf16((quads + 2, rows, cols))] * 2, q, *halves
     )
     sides, q_sides = call(
         sides_kernel, [bf16((planes, rows, cols)), f32((rows, cols))],
@@ -331,7 +332,7 @@
         message = f32((2 * HMAX if step < 2 else HMAX, cols))
         part, to_second, to_first = with_odd(
             functools.partial(taper_kernel, step), [f32((rows, cols)), message, message],
-            vector, valid, obs_error, *around, ensemble, sides, rows_second, rows_first,
+            vector, valid, obs_error, *around, *halves, sides, rows_second, rows_first,
             lon_band, side_band, lat, name=f"taper_{step}", flops=flops,
         )
         from_second = swap(to_second, "lat", 1, False)

time: 104 us -> 103 us (level)
  Pallas kernels: 9.35 us -> 7.55 us
  waiting for transfers between devices: 20.5 us -> 18.9 us
  starting transfers between devices: 56.2 us -> 57.7 us
    pallas_call x11, Pallas kernels: 9.35 us -> 7.55 us  [call(): pl.pallas_call(kernel, out_shape=outs, compiler_params=pltpu.CompilerPara...]
    ppermute x14, waiting for transfers between devices: 15.3 us -> 13.9 us  [swap(): return lax.ppermute(cells, axis, pairs)]
    all_to_all x1, starting transfers between devices: 3.47 us -> 4.74 us  [shards(): parts = lax.all_to_all(parts, 'near', 0, 0)]
  transfers between devices with their start and end apart: 15 -> 15, of which waited for: 11 -> 11; matrix products, arithmetic and copies ran while one was open for 1% -> 1% of each run, Pallas kernels for 2% -> 1%
where the time goes in v6:
time: 103 us
  starting transfers between devices  57.7 us (56%)
  waiting for transfers between devices  18.9 us (18%)
  blocking collectives  13.3 us (13%)
  Pallas kernels  7.55 us (7%)
  local copies, waits for them, and re-layouts  2.53 us (2%)
  between operations  2.3 us (2%)
    ppermute x14, starting transfers between devices, swap(): return lax.ppermute(cells, axis, pairs)  53 us
    ppermute x14, waiting for transfers between devices, swap(): return lax.ppermute(cells, axis, pairs)  13.9 us
    all_to_all x1, blocking collectives, shards(): parts = lax.all_to_all(gram, ('far', 'lat'), 0, 0)  13.3 us
    pallas_call x11, Pallas kernels, call(): pl.pallas_call(kernel, out_shape=outs, compiler_params=pltpu.CompilerPara...  7.55 us
    all_to_all x1, waiting for transfers between devices, shards(): parts = lax.all_to_all(parts, 'near', 0, 0)  5.01 us
    all_to_all x1, starting transfers between devices, shards(): parts = lax.all_to_all(parts, 'near', 0, 0)  4.74 us
  transfers between devices with their start and end apart: 15, of which 11 were waited for; matrix products, arithmetic and copies ran while one was open for 1% of the time, Pallas kernels for 1%

profile of v6, /device:TPU:1, one launch (start us, length us, event | category | flops | bytes accessed | tf_op | source)
XLA Modules:
  0.0 102.7 jit_solution(3463095013509206673)
XLA Ops:
  2.1 4.5 %collective-permute-start.2 = (bf16[64,32,128]{2,1,0:T(8,128)(2,1)S(1)}, bf16[64,32,128]{2,1,0:T(8,128)(2,1)S(1)}, u32[]{:S(2)}, u32[]{:S(2)}) collective-permute-start(bf16[64,32,128]{2,1,0:T(8,128)(2,1)S(1)} %get-tuple-element.25.half_second.refs_1_.refs_2_), channel_id=1, source_target_pairs={{1,2},{2,1},{3,4},{4,3},{5,6},{6,5},{7,8},{8,7},{9,10},{10,9},{11,... | collective-permute-start | bytes 1572872 | tf_op jit(solution)/shard_map/ppermute | solution.py:22
  6.7 5.0 %collective-permute-start.3 = (bf16[64,32,128]{2,1,0:T(8,128)(2,1)S(1)}, bf16[64,32,128]{2,1,0:T(8,128)(2,1)S(1)}, u32[]{:S(2)}, u32[]{:S(2)}) collective-permute-start(bf16[64,32,128]{2,1,0:T(8,128)(2,1)S(1)} %get-tuple-element.26.half_first.refs_2_.refs_3_), channel_id=1, source_target_pairs={{0,1},{1,0},{2,3},{3,2},{4,5},{5,4},{6,7},{7,6},{8,9},{9,8},{10,11... | collective-permute-start | bytes 1572872 | tf_op jit(solution)/shard_map/ppermute | solution.py:22
  12.1 10.2 %collective-permute-start = (bf16[18,64,128]{2,1,0:T(8,128)(2,1)S(1)}, bf16[18,64,128]{2,1,0:T(8,128)(2,1)S(1)}, u32[]{:S(2)}, u32[]{:S(2)}) collective-permute-start(bf16[18,64,128]{2,1,0:T(8,128)(2,1)S(1)} %get-tuple-element.27), channel_id=1, source_target_pairs={{0,496},{16,32},{32,16},{48,64},{64,48},{80,96},{96,80},{112,128},... | collective-permute-start | bytes 884744 | tf_op jit(solution)/shard_map/ppermute | solution.py:22
  22.4 1.9 %collective-permute-start.1 = (bf16[18,64,128]{2,1,0:T(8,128)(2,1)S(1)}, bf16[18,64,128]{2,1,0:T(8,128)(2,1)S(1)}, u32[]{:S(2)}, u32[]{:S(2)}) collective-permute-start(bf16[18,64,128]{2,1,0:T(8,128)(2,1)S(1)} %get-tuple-element.28), channel_id=1, source_target_pairs={{0,16},{16,0},{32,48},{48,32},{64,80},{80,64},{96,112},{112,96},{1... | collective-permute-start | bytes 884744 | tf_op jit(solution)/shard_map/ppermute | solution.py:22
  27.3 2.0 %collective-permute-done.from_second = bf16[18,64,128]{2,1,0:T(8,128)(2,1)S(1)} collective-permute-done((bf16[18,64,128]{2,1,0:T(8,128)(2,1)S(1)}, bf16[18,64,128]{2,1,0:T(8,128)(2,1)S(1)}, u32[]{:S(2)}, u32[]{:S(2)}) %collective-permute-start) | collective-permute-done | bytes 294944 | tf_op jit(solution)/shard_map/ppermute | solution.py:22
  29.3 2.7 %collective-permute-done.1.from_first = bf16[18,64,128]{2,1,0:T(8,128)(2,1)S(1)} collective-permute-done((bf16[18,64,128]{2,1,0:T(8,128)(2,1)S(1)}, bf16[18,64,128]{2,1,0:T(8,128)(2,1)S(1)}, u32[]{:S(2)}, u32[]{:S(2)}) %collective-permute-start.1) | collective-permute-done | bytes 294944 | tf_op jit(solution)/shard_map/ppermute | solution.py:22
  32.4 1.6 %taper_0.1 = (f32[64,128]{1,0:T(8,128)S(1)}, f32[64,128]{1,0:T(8,128)S(1)}, f32[64,128]{1,0:T(8,128)S(1)}) custom-call(s32[8,128]{1,0:T(8,128)S(1)} %broadcast_in_dim.37.odd, f32[64,128]{1,0:T(8,128)S(1)} %copy-done.2, s32[64,128]{1,0:T(8,128)S(1)} %copy-done, f32[64,128]{1,0:T(8,128)S(1)} %copy-done.3, f32[64,128]{1,0:T(8,128)S(1)} %get-tuple-element.29.refs_0_, ...), custom_call_target="tpu_custom_call" | custom-call | flops 805306368 | bytes 2985984 | tf_op jit(solution)/shard_map/taper_0/pallas_call | solution.py:289
  34.0 4.4 %collective-permute-start.4 = (f32[64,128]{1,0:T(8,128)S(1)}, f32[64,128]{1,0:T(8,128)S(1)}, u32[]{:S(2)}, u32[]{:S(2)}) collective-permute-start(f32[64,128]{1,0:T(8,128)S(1)} %get-tuple-element.32), channel_id=1, source_target_pairs={{1,2},{2,1},{3,4},{4,3},{5,6},{6,5},{7,8},{8,7},{9,10},{10,9},{11,... | collective-permute-start | bytes 98312 | tf_op jit(solution)/shard_map/ppermute | solution.py:22
  38.4 1.9 %collective-permute-start.5 = (f32[64,128]{1,0:T(8,128)S(1)}, f32[64,128]{1,0:T(8,128)S(1)}, u32[]{:S(2)}, u32[]{:S(2)}) collective-permute-start(f32[64,128]{1,0:T(8,128)S(1)} %get-tuple-element.33), channel_id=1, source_target_pairs={{0,1},{1,0},{2,3},{3,2},{4,5},{5,4},{6,7},{7,6},{8,9},{9,8},{10,11... | collective-permute-start | bytes 98312 | tf_op jit(solution)/shard_map/ppermute | solution.py:22
  41.6 4.3 %collective-permute-start.6 = (f32[64,128]{1,0:T(8,128)S(1)}, f32[64,128]{1,0:T(8,128)S(1)}, u32[]{:S(2)}, u32[]{:S(2)}) collective-permute-start(f32[64,128]{1,0:T(8,128)S(1)} %get-tuple-element.35), channel_id=1, source_target_pairs={{0,496},{16,32},{32,16},{48,64},{64,48},{80,96},{96,80},{112,128},... | collective-permute-start | bytes 98312 | tf_op jit(solution)/shard_map/ppermute | solution.py:22
  46.0 1.9 %collective-permute-start.7 = (f32[64,128]{1,0:T(8,128)S(1)}, f32[64,128]{1,0:T(8,128)S(1)}, u32[]{:S(2)}, u32[]{:S(2)}) collective-permute-start(f32[64,128]{1,0:T(8,128)S(1)} %get-tuple-element.36), channel_id=1, source_target_pairs={{0,16},{16,0},{32,48},{48,32},{64,80},{80,64},{96,112},{112,96},{1... | collective-permute-start | bytes 98312 | tf_op jit(solution)/shard_map/ppermute | solution.py:22
  47.9 2.0 %collective-permute-done.6.refs_0_ = f32[64,128]{1,0:T(8,128)S(1)} collective-permute-done((f32[64,128]{1,0:T(8,128)S(1)}, f32[64,128]{1,0:T(8,128)S(1)}, u32[]{:S(2)}, u32[]{:S(2)}) %collective-permute-start.6) | collective-permute-done | bytes 32800 | tf_op jit(solution)/shard_map/ppermute | solution.py:22
  50.8 1.6 %taper_1.1 = (f32[64,128]{1,0:T(8,128)S(1)}, f32[64,128]{1,0:T(8,128)S(1)}, f32[64,128]{1,0:T(8,128)S(1)}) custom-call(s32[8,128]{1,0:T(8,128)S(1)} %broadcast_in_dim.37.odd, f32[64,128]{1,0:T(8,128)S(1)} %get-tuple-element.34.vector.v1, s32[64,128]{1,0:T(8,128)S(1)} %copy-done, f32[64,128]{1,0:T(8,128)S(1)} %copy-done.3, ...), custom_call_target="tpu_custom_call" | custom-call | flops 805306368 | bytes 3018752 | tf_op jit(solution)/shard_map/taper_1/pallas_call | solution.py:289
  52.4 5.3 %collective-permute-start.8 = (f32[64,128]{1,0:T(8,128)S(1)}, f32[64,128]{1,0:T(8,128)S(1)}, u32[]{:S(2)}, u32[]{:S(2)}) collective-permute-start(f32[64,128]{1,0:T(8,128)S(1)} %get-tuple-element.38.refs_0_), channel_id=1, source_target_pairs={{1,2},{2,1},{3,4},{4,3},{5,6},{6,5},{7,8},{8,7},{9,10},{10,9},{11,... | collective-permute-start | bytes 98312 | tf_op jit(solution)/shard_map/ppermute | solution.py:22
  57.7 1.9 %collective-permute-start.9 = (f32[64,128]{1,0:T(8,128)S(1)}, f32[64,128]{1,0:T(8,128)S(1)}, u32[]{:S(2)}, u32[]{:S(2)}) collective-permute-start(f32[64,128]{1,0:T(8,128)S(1)} %get-tuple-element.39.refs_1_), channel_id=1, source_target_pairs={{0,1},{1,0},{2,3},{3,2},{4,5},{5,4},{6,7},{7,6},{8,9},{9,8},{10,11... | collective-permute-start | bytes 98312 | tf_op jit(solution)/shard_map/ppermute | solution.py:22
  61.0 4.6 %collective-permute-start.10 = (f32[64,128]{1,0:T(8,128)S(1)}, f32[64,128]{1,0:T(8,128)S(1)}, u32[]{:S(2)}, u32[]{:S(2)}) collective-permute-start(f32[64,128]{1,0:T(8,128)S(1)} %get-tuple-element.41), channel_id=1, source_target_pairs={{0,496},{16,32},{32,16},{48,64},{64,48},{80,96},{96,80},{112,128},... | collective-permute-start | bytes 98312 | tf_op jit(solution)/shard_map/ppermute | solution.py:22
  65.6 1.9 %collective-permute-start.11 = (f32[64,128]{1,0:T(8,128)S(1)}, f32[64,128]{1,0:T(8,128)S(1)}, u32[]{:S(2)}, u32[]{:S(2)}) collective-permute-start(f32[64,128]{1,0:T(8,128)S(1)} %get-tuple-element.42), channel_id=1, source_target_pairs={{0,16},{16,0},{32,48},{48,32},{64,80},{80,64},{96,112},{112,96},{1... | collective-permute-start | bytes 98312 | tf_op jit(solution)/shard_map/ppermute | solution.py:22
  67.5 1.8 %collective-permute-done.10.refs_0_ = f32[64,128]{1,0:T(8,128)S(1)} collective-permute-done((f32[64,128]{1,0:T(8,128)S(1)}, f32[64,128]{1,0:T(8,128)S(1)}, u32[]{:S(2)}, u32[]{:S(2)}) %collective-permute-start.10) | collective-permute-done | bytes 32800 | tf_op jit(solution)/shard_map/ppermute | solution.py:22
  70.2 1.6 %taper_2.1 = (f32[64,128]{1,0:T(8,128)S(1)}, f32[32,128]{1,0:T(8,128)S(1)}, f32[32,128]{1,0:T(8,128)S(1)}) custom-call(s32[8,128]{1,0:T(8,128)S(1)} %broadcast_in_dim.37.odd, f32[64,128]{1,0:T(8,128)S(1)} %get-tuple-element.40.vector.v2, s32[64,128]{1,0:T(8,128)S(1)} %copy-done, f32[64,128]{1,0:T(8,128)S(1)} %copy-done.3, ...), custom_call_target="tpu_custom_call" | custom-call | flops 805306368 | bytes 3018752 | tf_op jit(solution)/shard_map/taper_2/pallas_call | solution.py:289
  71.9 13.3 %all_to_all.10.parts = f32[32,1,128]{2,1,0:T(1,128)S(1)} all-to-all(f32[32,1,128]{2,1,0:T(1,128)S(1)} %gram_kernel.1), channel_id=1, replica_groups=mesh['far'=2,'near'=16,'lat'=16] {'far','lat'}, dimensions={0} | all-to-all | bytes 32768 | tf_op jit(solution)/shard_map/all_to_all | solution.py:357
  85.9 4.7 %all-to-all-start.1 = ((f32[16,1,128]{2,1,0:T(1,128)}), f32[16,1,128]{2,1,0:T(1,128)S(1)}, u32[]{:S(2)}, u32[]{:S(2)}) async-start(f32[16,1,128]{2,1,0:T(1,128)} %sum_kernel.1), calls=%async_computation.1 | async-start | bytes 16384 | tf_op jit(solution)/shard_map/all_to_all | solution.py:359
  90.6 3.1 %collective-permute-start.12 = (f32[32,128]{1,0:T(8,128)S(1)}, f32[32,128]{1,0:T(8,128)S(1)}, u32[]{:S(2)}, u32[]{:S(2)}) collective-permute-start(f32[32,128]{1,0:T(8,128)S(1)} %get-tuple-element.44.to_second), channel_id=1, source_target_pairs={{1,2},{2,1},{3,4},{4,3},{5,6},{6,5},{7,8},{8,7},{9,10},{10,9},{11,... | collective-permute-start | bytes 49160 | tf_op jit(solution)/shard_map/ppermute | solution.py:22
  93.8 1.9 %collective-permute-start.13 = (f32[32,128]{1,0:T(8,128)S(1)}, f32[32,128]{1,0:T(8,128)S(1)}, u32[]{:S(2)}, u32[]{:S(2)}) collective-permute-start(f32[32,128]{1,0:T(8,128)S(1)} %get-tuple-element.45.to_first), channel_id=1, source_target_pairs={{0,1},{1,0},{2,3},{3,2},{4,5},{5,4},{6,7},{7,6},{8,9},{9,8},{10,11... | collective-permute-start | bytes 49160 | tf_op jit(solution)/shard_map/ppermute | solution.py:22
  96.8 5.0 %all-to-all-done.1.parts = f32[16,1,128]{2,1,0:T(1,128)S(1)} async-done(((f32[16,1,128]{2,1,0:T(1,128)}), f32[16,1,128]{2,1,0:T(1,128)S(1)}, u32[]{:S(2)}, u32[]{:S(2)}) %all-to-all-start.1) | async-done | bytes 8224 | tf_op jit(solution)/shard_map/all_to_all | solution.py:359
  (42 shorter events, 11.2 us)
Async XLA Ops:
  0.7 1.2 %copy-start.1 = (bf16[64,64,128]{2,1,0:T(8,128)(2,1)S(1)}, bf16[64,64,128]{2,1,0:T(8,128)(2,1)}, u32[]{:S(2)}) copy-start(bf16[64,64,128]{2,1,0:T(8,128)(2,1)} %ens.1) | copy-start | bytes 3145732
  2.0 9.7 %copy-start = (s32[64,128]{1,0:T(8,128)S(1)}, s32[64,128]{1,0:T(8,128)}, u32[]{:S(2)}) copy-start(s32[64,128]{1,0:T(8,128)} %valid.11) | copy-start | bytes 98308
  2.0 9.7 %copy-start.2 = (f32[64,128]{1,0:T(8,128)S(1)}, f32[64,128]{1,0:T(8,128)}, u32[]{:S(2)}) copy-start(f32[64,128]{1,0:T(8,128)} %v0.3) | copy-start | bytes 98308
  2.1 30.2 %collective-permute-start.2 = (bf16[64,32,128]{2,1,0:T(8,128)(2,1)S(1)}, bf16[64,32,128]{2,1,0:T(8,128)(2,1)S(1)}, u32[]{:S(2)}, u32[]{:S(2)}) collective-permute-start(bf16[64,32,128]{2,1,0:T(8,128)(2,1)S(1)} %get-tuple-element.25.half_second.refs_1_.refs_2_), channel_id=1, source_target_pairs={{1,2},{2,1},{3,4},{4,3},{5,6},{6,5},{7,8},{8,7},{9,10},{10,9},{11,... | collective-permute-start | bytes 1572872 | tf_op jit(solution)/shard_map/ppermute | solution.py:22
  6.7 25.7 %collective-permute-start.3 = (bf16[64,32,128]{2,1,0:T(8,128)(2,1)S(1)}, bf16[64,32,128]{2,1,0:T(8,128)(2,1)S(1)}, u32[]{:S(2)}, u32[]{:S(2)}) collective-permute-start(bf16[64,32,128]{2,1,0:T(8,128)(2,1)S(1)} %get-tuple-element.26.half_first.refs_2_.refs_3_), channel_id=1, source_target_pairs={{0,1},{1,0},{2,3},{3,2},{4,5},{5,4},{6,7},{7,6},{8,9},{9,8},{10,11... | collective-permute-start | bytes 1572872 | tf_op jit(solution)/shard_map/ppermute | solution.py:22
  12.1 17.2 %collective-permute-start = (bf16[18,64,128]{2,1,0:T(8,128)(2,1)S(1)}, bf16[18,64,128]{2,1,0:T(8,128)(2,1)S(1)}, u32[]{:S(2)}, u32[]{:S(2)}) collective-permute-start(bf16[18,64,128]{2,1,0:T(8,128)(2,1)S(1)} %get-tuple-element.27), channel_id=1, source_target_pairs={{0,496},{16,32},{32,16},{48,64},{64,48},{80,96},{96,80},{112,128},... | collective-permute-start | bytes 884744 | tf_op jit(solution)/shard_map/ppermute | solution.py:22
  22.4 9.6 %collective-permute-start.1 = (bf16[18,64,128]{2,1,0:T(8,128)(2,1)S(1)}, bf16[18,64,128]{2,1,0:T(8,128)(2,1)S(1)}, u32[]{:S(2)}, u32[]{:S(2)}) collective-permute-start(bf16[18,64,128]{2,1,0:T(8,128)(2,1)S(1)} %get-tuple-element.28), channel_id=1, source_target_pairs={{0,16},{16,0},{32,48},{48,32},{64,80},{80,64},{96,112},{112,96},{1... | collective-permute-start | bytes 884744 | tf_op jit(solution)/shard_map/ppermute | solution.py:22
  24.3 0.7 copy-start.4
  27.3 5.1 %copy-start.3 = (f32[64,128]{1,0:T(8,128)S(1)}, f32[64,128]{1,0:T(8,128)}, u32[]{:S(2)}) copy-start(f32[64,128]{1,0:T(8,128)} %obs_error.5) | copy-start | bytes 98308
  34.0 6.3 %collective-permute-start.4 = (f32[64,128]{1,0:T(8,128)S(1)}, f32[64,128]{1,0:T(8,128)S(1)}, u32[]{:S(2)}, u32[]{:S(2)}) collective-permute-start(f32[64,128]{1,0:T(8,128)S(1)} %get-tuple-element.32), channel_id=1, source_target_pairs={{1,2},{2,1},{3,4},{4,3},{5,6},{6,5},{7,8},{8,7},{9,10},{10,9},{11,... | collective-permute-start | bytes 98312 | tf_op jit(solution)/shard_map/ppermute | solution.py:22
  38.4 3.1 %collective-permute-start.5 = (f32[64,128]{1,0:T(8,128)S(1)}, f32[64,128]{1,0:T(8,128)S(1)}, u32[]{:S(2)}, u32[]{:S(2)}) collective-permute-start(f32[64,128]{1,0:T(8,128)S(1)} %get-tuple-element.33), channel_id=1, source_target_pairs={{0,1},{1,0},{2,3},{3,2},{4,5},{5,4},{6,7},{7,6},{8,9},{9,8},{10,11... | collective-permute-start | bytes 98312 | tf_op jit(solution)/shard_map/ppermute | solution.py:22
  41.6 8.3 %collective-permute-start.6 = (f32[64,128]{1,0:T(8,128)S(1)}, f32[64,128]{1,0:T(8,128)S(1)}, u32[]{:S(2)}, u32[]{:S(2)}) collective-permute-start(f32[64,128]{1,0:T(8,128)S(1)} %get-tuple-element.35), channel_id=1, source_target_pairs={{0,496},{16,32},{32,16},{48,64},{64,48},{80,96},{96,80},{112,128},... | collective-permute-start | bytes 98312 | tf_op jit(solution)/shard_map/ppermute | solution.py:22
  46.0 4.9 %collective-permute-start.7 = (f32[64,128]{1,0:T(8,128)S(1)}, f32[64,128]{1,0:T(8,128)S(1)}, u32[]{:S(2)}, u32[]{:S(2)}) collective-permute-start(f32[64,128]{1,0:T(8,128)S(1)} %get-tuple-element.36), channel_id=1, source_target_pairs={{0,16},{16,0},{32,48},{48,32},{64,80},{80,64},{96,112},{112,96},{1... | collective-permute-start | bytes 98312 | tf_op jit(solution)/shard_map/ppermute | solution.py:22
  52.4 7.3 %collective-permute-start.8 = (f32[64,128]{1,0:T(8,128)S(1)}, f32[64,128]{1,0:T(8,128)S(1)}, u32[]{:S(2)}, u32[]{:S(2)}) collective-permute-start(f32[64,128]{1,0:T(8,128)S(1)} %get-tuple-element.38.refs_0_), channel_id=1, source_target_pairs={{1,2},{2,1},{3,4},{4,3},{5,6},{6,5},{7,8},{8,7},{9,10},{10,9},{11,... | collective-permute-start | bytes 98312 | tf_op jit(solution)/shard_map/ppermute | solution.py:22
  57.7 3.1 %collective-permute-start.9 = (f32[64,128]{1,0:T(8,128)S(1)}, f32[64,128]{1,0:T(8,128)S(1)}, u32[]{:S(2)}, u32[]{:S(2)}) collective-permute-start(f32[64,128]{1,0:T(8,128)S(1)} %get-tuple-element.39.refs_1_), channel_id=1, source_target_pairs={{0,1},{1,0},{2,3},{3,2},{4,5},{5,4},{6,7},{7,6},{8,9},{9,8},{10,11... | collective-permute-start | bytes 98312 | tf_op jit(solution)/shard_map/ppermute | solution.py:22
  61.0 8.3 %collective-permute-start.10 = (f32[64,128]{1,0:T(8,128)S(1)}, f32[64,128]{1,0:T(8,128)S(1)}, u32[]{:S(2)}, u32[]{:S(2)}) collective-permute-start(f32[64,128]{1,0:T(8,128)S(1)} %get-tuple-element.41), channel_id=1, source_target_pairs={{0,496},{16,32},{32,16},{48,64},{64,48},{80,96},{96,80},{112,128},... | collective-permute-start | bytes 98312 | tf_op jit(solution)/shard_map/ppermute | solution.py:22
  65.6 4.7 %collective-permute-start.11 = (f32[64,128]{1,0:T(8,128)S(1)}, f32[64,128]{1,0:T(8,128)S(1)}, u32[]{:S(2)}, u32[]{:S(2)}) collective-permute-start(f32[64,128]{1,0:T(8,128)S(1)} %get-tuple-element.42), channel_id=1, source_target_pairs={{0,16},{16,0},{32,48},{48,32},{64,80},{80,64},{96,112},{112,96},{1... | collective-permute-start | bytes 98312 | tf_op jit(solution)/shard_map/ppermute | solution.py:22
  85.9 16.0 %all-to-all-start.1 = ((f32[16,1,128]{2,1,0:T(1,128)}), f32[16,1,128]{2,1,0:T(1,128)S(1)}, u32[]{:S(2)}, u32[]{:S(2)}) async-start(f32[16,1,128]{2,1,0:T(1,128)} %sum_kernel.1), calls=%async_computation.1 | async-start | bytes 16384 | tf_op jit(solution)/shard_map/all_to_all | solution.py:359
  90.6 5.4 %collective-permute-start.12 = (f32[32,128]{1,0:T(8,128)S(1)}, f32[32,128]{1,0:T(8,128)S(1)}, u32[]{:S(2)}, u32[]{:S(2)}) collective-permute-start(f32[32,128]{1,0:T(8,128)S(1)} %get-tuple-element.44.to_second), channel_id=1, source_target_pairs={{1,2},{2,1},{3,4},{4,3},{5,6},{6,5},{7,8},{8,7},{9,10},{10,9},{11,... | collective-permute-start | bytes 49160 | tf_op jit(solution)/shard_map/ppermute | solution.py:22
  93.8 3.1 %collective-permute-start.13 = (f32[32,128]{1,0:T(8,128)S(1)}, f32[32,128]{1,0:T(8,128)S(1)}, u32[]{:S(2)}, u32[]{:S(2)}) collective-permute-start(f32[32,128]{1,0:T(8,128)S(1)} %get-tuple-element.45.to_first), channel_id=1, source_target_pairs={{0,1},{1,0},{2,3},{3,2},{4,5},{5,4},{6,7},{7,6},{8,9},{9,8},{10,11... | collective-permute-start | bytes 49160 | tf_op jit(solution)/shard_map/ppermute | solution.py:22

commit v7 on v6

--- a/solution.py
+++ b/solution.py
@@ -94,6 +94,10 @@
         top, bottom = ens[m, :HMAX, :], ens[m, rows - HMAX :, :]
         first[m] = jnp.where(north_first, top, bottom)
         second[m] = jnp.where(north_first, bottom, top)
+
+
+def after_kernel(*refs):
+    del refs
 
 
 def columns_kernel(odd, q, half_second, half_first, second, first):
@@ -316,10 +320,16 @@
     q = valid.astype(jnp.float32) * right_side
     halves = with_odd(rows_kernel, [bf16((members, HMAX, cols))] * 2, ensemble)
     rows_second = swap(halves[0], "lat", 1, False)
-    rows_first = swap(halves[1], "lat", 0, False)
     second, first = with_odd(
         columns_kernel, [bf16((quads + 2, rows, cols))] * 2, q, *halves
     )
+    anywhere = pl.BlockSpec(memory_space=pl.ANY)
+    half_first = pl.pallas_call(
+        after_kernel, out_shape=bf16(halves[1].shape), in_specs=[anywhere] * 2,
+        out_specs=anywhere, input_output_aliases={0: 0}, name="after_kernel",
+    )(halves[1], first)
+    halves = [halves[0], half_first]
+    rows_first = swap(half_first, "lat", 0, False)
     sides, q_sides = call(
         sides_kernel, [bf16((planes, rows, cols)), f32((rows, cols))],
         swap(second, LON, 1, True), swap(first, LON, 0, True),

time: 103 us -> 103 us (level)
  waiting for transfers between devices: 18.9 us -> 16.7 us
  starting transfers between devices: 57.7 us -> 59.5 us
    ppermute x14, waiting for transfers between devices: 13.9 us -> 11.7 us  [swap(): return lax.ppermute(cells, axis, pairs)]
    ppermute x14, starting transfers between devices: 53 us -> 54.8 us  [swap(): return lax.ppermute(cells, axis, pairs)]
  transfers between devices with their start and end apart: 15 -> 15, of which waited for: 11 -> 10; matrix products, arithmetic and copies ran while one was open for 1% -> 1% of each run, Pallas kernels for 1% -> 1%
where the time goes in v7:
time: 103 us
  starting transfers between devices  59.5 us (58%)
  waiting for transfers between devices  16.7 us (16%)
  blocking collectives  13.6 us (13%)
  Pallas kernels  7.53 us (7%)
  local copies, waits for them, and re-layouts  2.54 us (2%)
  between operations  2.36 us (2%)
    ppermute x14, starting transfers between devices, swap(): return lax.ppermute(cells, axis, pairs)  54.8 us
    all_to_all x1, blocking collectives, shards(): parts = lax.all_to_all(gram, ('far', 'lat'), 0, 0)  13.6 us
    ppermute x14, waiting for transfers between devices, swap(): return lax.ppermute(cells, axis, pairs)  11.7 us
    pallas_call x11, Pallas kernels, call(): pl.pallas_call(kernel, out_shape=outs, compiler_params=pltpu.CompilerPara...  7.53 us
    all_to_all x1, waiting for transfers between devices, shards(): parts = lax.all_to_all(parts, 'near', 0, 0)  5.01 us
    all_to_all x1, starting transfers between devices, shards(): parts = lax.all_to_all(parts, 'near', 0, 0)  4.74 us
  transfers between devices with their start and end apart: 15, of which 10 were waited for; matrix products, arithmetic and copies ran while one was open for 1% of the time, Pallas kernels for 1%

profile of v7, /device:TPU:1, one launch (start us, length us, event | category | flops | bytes accessed | tf_op | source)
XLA Modules:
  0.0 102.7 jit_solution(7327461902915054944)
XLA Ops:
  0.7 1.2 %copy-done.3 = bf16[64,64,128]{2,1,0:T(8,128)(2,1)S(1)} copy-done((bf16[64,64,128]{2,1,0:T(8,128)(2,1)S(1)}, bf16[64,64,128]{2,1,0:T(8,128)(2,1)}, u32[]{:S(2)}) %copy-start.3) | copy-done | bytes 1048600
  2.2 4.5 %collective-permute-start.2 = (bf16[64,32,128]{2,1,0:T(8,128)(2,1)S(1)}, bf16[64,32,128]{2,1,0:T(8,128)(2,1)S(1)}, u32[]{:S(2)}, u32[]{:S(2)}) collective-permute-start(bf16[64,32,128]{2,1,0:T(8,128)(2,1)S(1)} %get-tuple-element.25.half_second.refs_1_.refs_2_), channel_id=1, source_target_pairs={{1,2},{2,1},{3,4},{4,3},{5,6},{6,5},{7,8},{8,7},{9,10},{10,9},{11,... | collective-permute-start | bytes 1572872 | tf_op jit(solution)/shard_map/ppermute | solution.py:22
  7.2 13.3 %collective-permute-start = (bf16[18,64,128]{2,1,0:T(8,128)(2,1)S(1)}, bf16[18,64,128]{2,1,0:T(8,128)(2,1)S(1)}, u32[]{:S(2)}, u32[]{:S(2)}) collective-permute-start(bf16[18,64,128]{2,1,0:T(8,128)(2,1)S(1)} %get-tuple-element.27), channel_id=1, source_target_pairs={{0,496},{16,32},{32,16},{48,64},{64,48},{80,96},{96,80},{112,128},... | collective-permute-start | bytes 884744 | tf_op jit(solution)/shard_map/ppermute | solution.py:22
  20.5 1.9 %collective-permute-start.1 = (bf16[18,64,128]{2,1,0:T(8,128)(2,1)S(1)}, bf16[18,64,128]{2,1,0:T(8,128)(2,1)S(1)}, u32[]{:S(2)}, u32[]{:S(2)}) collective-permute-start(bf16[18,64,128]{2,1,0:T(8,128)(2,1)S(1)} %get-tuple-element.28.refs_1_), channel_id=1, source_target_pairs={{0,16},{16,0},{32,48},{48,32},{64,80},{80,64},{96,112},{112,96},{1... | collective-permute-start | bytes 884744 | tf_op jit(solution)/shard_map/ppermute | solution.py:22
  22.4 1.9 %collective-permute-start.3 = (bf16[64,32,128]{2,1,0:T(8,128)(2,1)}, bf16[64,32,128]{2,1,0:T(8,128)(2,1)S(1)}, u32[]{:S(2)}, u32[]{:S(2)}) collective-permute-start(bf16[64,32,128]{2,1,0:T(8,128)(2,1)} %after_kernel.1.refs_2_.refs_3_), channel_id=1, source_target_pairs={{0,1},{1,0},{2,3},{3,2},{4,5},{5,4},{6,7},{7,6},{8,9},{9,8},{10,11... | collective-permute-start | bytes 1572872 | tf_op jit(solution)/shard_map/ppermute | solution.py:22
  27.4 2.5 %collective-permute-done.1.from_first = bf16[18,64,128]{2,1,0:T(8,128)(2,1)S(1)} collective-permute-done((bf16[18,64,128]{2,1,0:T(8,128)(2,1)S(1)}, bf16[18,64,128]{2,1,0:T(8,128)(2,1)S(1)}, u32[]{:S(2)}, u32[]{:S(2)}) %collective-permute-start.1) | collective-permute-done | bytes 294944 | tf_op jit(solution)/shard_map/ppermute | solution.py:22
  30.2 1.6 %taper_0.1 = (f32[64,128]{1,0:T(8,128)S(1)}, f32[64,128]{1,0:T(8,128)S(1)}, f32[64,128]{1,0:T(8,128)S(1)}) custom-call(s32[8,128]{1,0:T(8,128)S(1)} %broadcast_in_dim.37.odd, f32[64,128]{1,0:T(8,128)S(1)} %copy-done.4, s32[64,128]{1,0:T(8,128)S(1)} %copy-done.2, f32[64,128]{1,0:T(8,128)S(1)} %copy-done.5, f32[64,128]{1,0:T(8,128)S(1)} %get-tuple-element.29.refs_0_, ...), custom_call_target="tpu_custom_call" | custom-call | flops 805306368 | bytes 2985984 | tf_op jit(solution)/shard_map/taper_0/pallas_call | solution.py:293
  31.7 3.9 %collective-permute-start.4 = (f32[64,128]{1,0:T(8,128)S(1)}, f32[64,128]{1,0:T(8,128)S(1)}, u32[]{:S(2)}, u32[]{:S(2)}) collective-permute-start(f32[64,128]{1,0:T(8,128)S(1)} %get-tuple-element.32), channel_id=1, source_target_pairs={{1,2},{2,1},{3,4},{4,3},{5,6},{6,5},{7,8},{8,7},{9,10},{10,9},{11,... | collective-permute-start | bytes 98312 | tf_op jit(solution)/shard_map/ppermute | solution.py:22
  35.7 1.9 %collective-permute-start.5 = (f32[64,128]{1,0:T(8,128)S(1)}, f32[64,128]{1,0:T(8,128)S(1)}, u32[]{:S(2)}, u32[]{:S(2)}) collective-permute-start(f32[64,128]{1,0:T(8,128)S(1)} %get-tuple-element.33), channel_id=1, source_target_pairs={{0,1},{1,0},{2,3},{3,2},{4,5},{5,4},{6,7},{7,6},{8,9},{9,8},{10,11... | collective-permute-start | bytes 98312 | tf_op jit(solution)/shard_map/ppermute | solution.py:22
  38.9 6.0 %collective-permute-start.6 = (f32[64,128]{1,0:T(8,128)S(1)}, f32[64,128]{1,0:T(8,128)S(1)}, u32[]{:S(2)}, u32[]{:S(2)}) collective-permute-start(f32[64,128]{1,0:T(8,128)S(1)} %get-tuple-element.35), channel_id=1, source_target_pairs={{0,496},{16,32},{32,16},{48,64},{64,48},{80,96},{96,80},{112,128},... | collective-permute-start | bytes 98312 | tf_op jit(solution)/shard_map/ppermute | solution.py:22
  45.0 1.9 %collective-permute-start.7 = (f32[64,128]{1,0:T(8,128)S(1)}, f32[64,128]{1,0:T(8,128)S(1)}, u32[]{:S(2)}, u32[]{:S(2)}) collective-permute-start(f32[64,128]{1,0:T(8,128)S(1)} %get-tuple-element.36), channel_id=1, source_target_pairs={{0,16},{16,0},{32,48},{48,32},{64,80},{80,64},{96,112},{112,96},{1... | collective-permute-start | bytes 98312 | tf_op jit(solution)/shard_map/ppermute | solution.py:22
  47.2 2.4 %collective-permute-done.7.refs_1_ = f32[64,128]{1,0:T(8,128)S(1)} collective-permute-done((f32[64,128]{1,0:T(8,128)S(1)}, f32[64,128]{1,0:T(8,128)S(1)}, u32[]{:S(2)}, u32[]{:S(2)}) %collective-permute-start.7) | collective-permute-done | bytes 32800 | tf_op jit(solution)/shard_map/ppermute | solution.py:22
  49.6 1.6 %taper_1.1 = (f32[64,128]{1,0:T(8,128)S(1)}, f32[64,128]{1,0:T(8,128)S(1)}, f32[64,128]{1,0:T(8,128)S(1)}) custom-call(s32[8,128]{1,0:T(8,128)S(1)} %broadcast_in_dim.37.odd, f32[64,128]{1,0:T(8,128)S(1)} %get-tuple-element.34.vector.v1, s32[64,128]{1,0:T(8,128)S(1)} %copy-done.2, f32[64,128]{1,0:T(8,128)S(1)} %copy-done.5, ...), custom_call_target="tpu_custom_call" | custom-call | flops 805306368 | bytes 3018752 | tf_op jit(solution)/shard_map/taper_1/pallas_call | solution.py:293
  51.2 6.5 %collective-permute-start.8 = (f32[64,128]{1,0:T(8,128)S(1)}, f32[64,128]{1,0:T(8,128)S(1)}, u32[]{:S(2)}, u32[]{:S(2)}) collective-permute-start(f32[64,128]{1,0:T(8,128)S(1)} %get-tuple-element.38.refs_0_), channel_id=1, source_target_pairs={{1,2},{2,1},{3,4},{4,3},{5,6},{6,5},{7,8},{8,7},{9,10},{10,9},{11,... | collective-permute-start | bytes 98312 | tf_op jit(solution)/shard_map/ppermute | solution.py:22
  57.7 1.9 %collective-permute-start.9 = (f32[64,128]{1,0:T(8,128)S(1)}, f32[64,128]{1,0:T(8,128)S(1)}, u32[]{:S(2)}, u32[]{:S(2)}) collective-permute-start(f32[64,128]{1,0:T(8,128)S(1)} %get-tuple-element.39.refs_1_), channel_id=1, source_target_pairs={{0,1},{1,0},{2,3},{3,2},{4,5},{5,4},{6,7},{7,6},{8,9},{9,8},{10,11... | collective-permute-start | bytes 98312 | tf_op jit(solution)/shard_map/ppermute | solution.py:22
  61.0 3.9 %collective-permute-start.10 = (f32[64,128]{1,0:T(8,128)S(1)}, f32[64,128]{1,0:T(8,128)S(1)}, u32[]{:S(2)}, u32[]{:S(2)}) collective-permute-start(f32[64,128]{1,0:T(8,128)S(1)} %get-tuple-element.41), channel_id=1, source_target_pairs={{0,496},{16,32},{32,16},{48,64},{64,48},{80,96},{96,80},{112,128},... | collective-permute-start | bytes 98312 | tf_op jit(solution)/shard_map/ppermute | solution.py:22
  64.9 1.9 %collective-permute-start.11 = (f32[64,128]{1,0:T(8,128)S(1)}, f32[64,128]{1,0:T(8,128)S(1)}, u32[]{:S(2)}, u32[]{:S(2)}) collective-permute-start(f32[64,128]{1,0:T(8,128)S(1)} %get-tuple-element.42), channel_id=1, source_target_pairs={{0,16},{16,0},{32,48},{48,32},{64,80},{80,64},{96,112},{112,96},{1... | collective-permute-start | bytes 98312 | tf_op jit(solution)/shard_map/ppermute | solution.py:22
  66.9 2.4 %collective-permute-done.10.refs_0_ = f32[64,128]{1,0:T(8,128)S(1)} collective-permute-done((f32[64,128]{1,0:T(8,128)S(1)}, f32[64,128]{1,0:T(8,128)S(1)}, u32[]{:S(2)}, u32[]{:S(2)}) %collective-permute-start.10) | collective-permute-done | bytes 32800 | tf_op jit(solution)/shard_map/ppermute | solution.py:22
  69.9 1.5 %taper_2.1 = (f32[64,128]{1,0:T(8,128)S(1)}, f32[32,128]{1,0:T(8,128)S(1)}, f32[32,128]{1,0:T(8,128)S(1)}) custom-call(s32[8,128]{1,0:T(8,128)S(1)} %broadcast_in_dim.37.odd, f32[64,128]{1,0:T(8,128)S(1)} %get-tuple-element.40.vector.v2, s32[64,128]{1,0:T(8,128)S(1)} %copy-done.2, f32[64,128]{1,0:T(8,128)S(1)} %copy-done.5, ...), custom_call_target="tpu_custom_call" | custom-call | flops 805306368 | bytes 3018752 | tf_op jit(solution)/shard_map/taper_2/pallas_call | solution.py:293
  71.6 13.6 %all_to_all.10.parts = f32[32,1,128]{2,1,0:T(1,128)S(1)} all-to-all(f32[32,1,128]{2,1,0:T(1,128)S(1)} %gram_kernel.1), channel_id=1, replica_groups=mesh['far'=2,'near'=16,'lat'=16] {'far','lat'}, dimensions={0} | all-to-all | bytes 32768 | tf_op jit(solution)/shard_map/all_to_all | solution.py:367
  85.9 4.7 %all-to-all-start.1 = ((f32[16,1,128]{2,1,0:T(1,128)}), f32[16,1,128]{2,1,0:T(1,128)S(1)}, u32[]{:S(2)}, u32[]{:S(2)}) async-start(f32[16,1,128]{2,1,0:T(1,128)} %sum_kernel.1), calls=%async_computation.1 | async-start | bytes 16384 | tf_op jit(solution)/shard_map/all_to_all | solution.py:369
  90.6 3.1 %collective-permute-start.12 = (f32[32,128]{1,0:T(8,128)S(1)}, f32[32,128]{1,0:T(8,128)S(1)}, u32[]{:S(2)}, u32[]{:S(2)}) collective-permute-start(f32[32,128]{1,0:T(8,128)S(1)} %get-tuple-element.44.to_second), channel_id=1, source_target_pairs={{1,2},{2,1},{3,4},{4,3},{5,6},{6,5},{7,8},{8,7},{9,10},{10,9},{11,... | collective-permute-start | bytes 49160 | tf_op jit(solution)/shard_map/ppermute | solution.py:22
  93.8 1.9 %collective-permute-start.13 = (f32[32,128]{1,0:T(8,128)S(1)}, f32[32,128]{1,0:T(8,128)S(1)}, u32[]{:S(2)}, u32[]{:S(2)}) collective-permute-start(f32[32,128]{1,0:T(8,128)S(1)} %get-tuple-element.45.to_first), channel_id=1, source_target_pairs={{0,1},{1,0},{2,3},{3,2},{4,5},{5,4},{6,7},{7,6},{8,9},{9,8},{10,11... | collective-permute-start | bytes 49160 | tf_op jit(solution)/shard_map/ppermute | solution.py:22
  96.9 5.0 %all-to-all-done.1.parts = f32[16,1,128]{2,1,0:T(1,128)S(1)} async-done(((f32[16,1,128]{2,1,0:T(1,128)}), f32[16,1,128]{2,1,0:T(1,128)S(1)}, u32[]{:S(2)}, u32[]{:S(2)}) %all-to-all-start.1) | async-done | bytes 8224 | tf_op jit(solution)/shard_map/all_to_all | solution.py:369
  (49 shorter events, 9.0 us)
Async XLA Ops:
  0.7 1.2 %copy-start.3 = (bf16[64,64,128]{2,1,0:T(8,128)(2,1)S(1)}, bf16[64,64,128]{2,1,0:T(8,128)(2,1)}, u32[]{:S(2)}) copy-start(bf16[64,64,128]{2,1,0:T(8,128)(2,1)} %ens.1) | copy-start | bytes 3145732
  2.0 4.7 %copy-start.2 = (s32[64,128]{1,0:T(8,128)S(1)}, s32[64,128]{1,0:T(8,128)}, u32[]{:S(2)}) copy-start(s32[64,128]{1,0:T(8,128)} %valid.11) | copy-start | bytes 98308
  2.0 4.7 %copy-start.4 = (f32[64,128]{1,0:T(8,128)S(1)}, f32[64,128]{1,0:T(8,128)}, u32[]{:S(2)}) copy-start(f32[64,128]{1,0:T(8,128)} %v0.3) | copy-start | bytes 98308
  2.1 5.0 %copy-start = (bf16[64,32,128]{2,1,0:T(8,128)(2,1)}, bf16[64,32,128]{2,1,0:T(8,128)(2,1)S(1)}, u32[]{:S(2)}) copy-start(bf16[64,32,128]{2,1,0:T(8,128)(2,1)S(1)} %get-tuple-element.26.half_first.refs_0_) | copy-start | bytes 1572868
  2.2 28.0 %collective-permute-start.2 = (bf16[64,32,128]{2,1,0:T(8,128)(2,1)S(1)}, bf16[64,32,128]{2,1,0:T(8,128)(2,1)S(1)}, u32[]{:S(2)}, u32[]{:S(2)}) collective-permute-start(bf16[64,32,128]{2,1,0:T(8,128)(2,1)S(1)} %get-tuple-element.25.half_second.refs_1_.refs_2_), channel_id=1, source_target_pairs={{1,2},{2,1},{3,4},{4,3},{5,6},{6,5},{7,8},{8,7},{9,10},{10,9},{11,... | collective-permute-start | bytes 1572872 | tf_op jit(solution)/shard_map/ppermute | solution.py:22
  7.2 15.2 %copy-start.6 = (bf16[18,64,128]{2,1,0:T(8,128)(2,1)}, bf16[18,64,128]{2,1,0:T(8,128)(2,1)S(1)}, u32[]{:S(2)}) copy-start(bf16[18,64,128]{2,1,0:T(8,128)(2,1)S(1)} %get-tuple-element.28.refs_1_) | copy-start | bytes 884740
  7.2 20.2 %collective-permute-start = (bf16[18,64,128]{2,1,0:T(8,128)(2,1)S(1)}, bf16[18,64,128]{2,1,0:T(8,128)(2,1)S(1)}, u32[]{:S(2)}, u32[]{:S(2)}) collective-permute-start(bf16[18,64,128]{2,1,0:T(8,128)(2,1)S(1)} %get-tuple-element.27), channel_id=1, source_target_pairs={{0,496},{16,32},{32,16},{48,64},{64,48},{80,96},{96,80},{112,128},... | collective-permute-start | bytes 884744 | tf_op jit(solution)/shard_map/ppermute | solution.py:22
  20.5 9.3 %collective-permute-start.1 = (bf16[18,64,128]{2,1,0:T(8,128)(2,1)S(1)}, bf16[18,64,128]{2,1,0:T(8,128)(2,1)S(1)}, u32[]{:S(2)}, u32[]{:S(2)}) collective-permute-start(bf16[18,64,128]{2,1,0:T(8,128)(2,1)S(1)} %get-tuple-element.28.refs_1_), channel_id=1, source_target_pairs={{0,16},{16,0},{32,48},{48,32},{64,80},{80,64},{96,112},{112,96},{1... | collective-permute-start | bytes 884744 | tf_op jit(solution)/shard_map/ppermute | solution.py:22
  22.4 7.7 %collective-permute-start.3 = (bf16[64,32,128]{2,1,0:T(8,128)(2,1)}, bf16[64,32,128]{2,1,0:T(8,128)(2,1)S(1)}, u32[]{:S(2)}, u32[]{:S(2)}) collective-permute-start(bf16[64,32,128]{2,1,0:T(8,128)(2,1)} %after_kernel.1.refs_2_.refs_3_), channel_id=1, source_target_pairs={{0,1},{1,0},{2,3},{3,2},{4,5},{5,4},{6,7},{7,6},{8,9},{9,8},{10,11... | collective-permute-start | bytes 1572872 | tf_op jit(solution)/shard_map/ppermute | solution.py:22
  24.4 0.7 copy-start.7
  26.9 3.2 %copy-start.1 = (bf16[64,32,128]{2,1,0:T(8,128)(2,1)S(1)}, bf16[64,32,128]{2,1,0:T(8,128)(2,1)}, u32[]{:S(2)}) copy-start(bf16[64,32,128]{2,1,0:T(8,128)(2,1)} %after_kernel.1.refs_2_.refs_3_) | copy-start | bytes 1572868
  27.4 2.8 %copy-start.5 = (f32[64,128]{1,0:T(8,128)S(1)}, f32[64,128]{1,0:T(8,128)}, u32[]{:S(2)}) copy-start(f32[64,128]{1,0:T(8,128)} %obs_error.5) | copy-start | bytes 98308
  31.7 5.9 %collective-permute-start.4 = (f32[64,128]{1,0:T(8,128)S(1)}, f32[64,128]{1,0:T(8,128)S(1)}, u32[]{:S(2)}, u32[]{:S(2)}) collective-permute-start(f32[64,128]{1,0:T(8,128)S(1)} %get-tuple-element.32), channel_id=1, source_target_pairs={{1,2},{2,1},{3,4},{4,3},{5,6},{6,5},{7,8},{8,7},{9,10},{10,9},{11,... | collective-permute-start | bytes 98312 | tf_op jit(solution)/shard_map/ppermute | solution.py:22
  35.7 3.1 %collective-permute-start.5 = (f32[64,128]{1,0:T(8,128)S(1)}, f32[64,128]{1,0:T(8,128)S(1)}, u32[]{:S(2)}, u32[]{:S(2)}) collective-permute-start(f32[64,128]{1,0:T(8,128)S(1)} %get-tuple-element.33), channel_id=1, source_target_pairs={{0,1},{1,0},{2,3},{3,2},{4,5},{5,4},{6,7},{7,6},{8,9},{9,8},{10,11... | collective-permute-start | bytes 98312 | tf_op jit(solution)/shard_map/ppermute | solution.py:22
  38.9 8.3 %collective-permute-start.6 = (f32[64,128]{1,0:T(8,128)S(1)}, f32[64,128]{1,0:T(8,128)S(1)}, u32[]{:S(2)}, u32[]{:S(2)}) collective-permute-start(f32[64,128]{1,0:T(8,128)S(1)} %get-tuple-element.35), channel_id=1, source_target_pairs={{0,496},{16,32},{32,16},{48,64},{64,48},{80,96},{96,80},{112,128},... | collective-permute-start | bytes 98312 | tf_op jit(solution)/shard_map/ppermute | solution.py:22
  45.0 4.7 %collective-permute-start.7 = (f32[64,128]{1,0:T(8,128)S(1)}, f32[64,128]{1,0:T(8,128)S(1)}, u32[]{:S(2)}, u32[]{:S(2)}) collective-permute-start(f32[64,128]{1,0:T(8,128)S(1)} %get-tuple-element.36), channel_id=1, source_target_pairs={{0,16},{16,0},{32,48},{48,32},{64,80},{80,64},{96,112},{112,96},{1... | collective-permute-start | bytes 98312 | tf_op jit(solution)/shard_map/ppermute | solution.py:22
  51.2 8.5 %collective-permute-start.8 = (f32[64,128]{1,0:T(8,128)S(1)}, f32[64,128]{1,0:T(8,128)S(1)}, u32[]{:S(2)}, u32[]{:S(2)}) collective-permute-start(f32[64,128]{1,0:T(8,128)S(1)} %get-tuple-element.38.refs_0_), channel_id=1, source_target_pairs={{1,2},{2,1},{3,4},{4,3},{5,6},{6,5},{7,8},{8,7},{9,10},{10,9},{11,... | collective-permute-start | bytes 98312 | tf_op jit(solution)/shard_map/ppermute | solution.py:22
  57.7 3.1 %collective-permute-start.9 = (f32[64,128]{1,0:T(8,128)S(1)}, f32[64,128]{1,0:T(8,128)S(1)}, u32[]{:S(2)}, u32[]{:S(2)}) collective-permute-start(f32[64,128]{1,0:T(8,128)S(1)} %get-tuple-element.39.refs_1_), channel_id=1, source_target_pairs={{0,1},{1,0},{2,3},{3,2},{4,5},{5,4},{6,7},{7,6},{8,9},{9,8},{10,11... | collective-permute-start | bytes 98312 | tf_op jit(solution)/shard_map/ppermute | solution.py:22
  61.0 8.3 %collective-permute-start.10 = (f32[64,128]{1,0:T(8,128)S(1)}, f32[64,128]{1,0:T(8,128)S(1)}, u32[]{:S(2)}, u32[]{:S(2)}) collective-permute-start(f32[64,128]{1,0:T(8,128)S(1)} %get-tuple-element.41), channel_id=1, source_target_pairs={{0,496},{16,32},{32,16},{48,64},{64,48},{80,96},{96,80},{112,128},... | collective-permute-start | bytes 98312 | tf_op jit(solution)/shard_map/ppermute | solution.py:22
  64.9 5.0 %collective-permute-start.11 = (f32[64,128]{1,0:T(8,128)S(1)}, f32[64,128]{1,0:T(8,128)S(1)}, u32[]{:S(2)}, u32[]{:S(2)}) collective-permute-start(f32[64,128]{1,0:T(8,128)S(1)} %get-tuple-element.42), channel_id=1, source_target_pairs={{0,16},{16,0},{32,48},{48,32},{64,80},{80,64},{96,112},{112,96},{1... | collective-permute-start | bytes 98312 | tf_op jit(solution)/shard_map/ppermute | solution.py:22
  85.9 16.0 %all-to-all-start.1 = ((f32[16,1,128]{2,1,0:T(1,128)}), f32[16,1,128]{2,1,0:T(1,128)S(1)}, u32[]{:S(2)}, u32[]{:S(2)}) async-start(f32[16,1,128]{2,1,0:T(1,128)} %sum_kernel.1), calls=%async_computation.1 | async-start | bytes 16384 | tf_op jit(solution)/shard_map/all_to_all | solution.py:369
  90.6 5.4 %collective-permute-start.12 = (f32[32,128]{1,0:T(8,128)S(1)}, f32[32,128]{1,0:T(8,128)S(1)}, u32[]{:S(2)}, u32[]{:S(2)}) collective-permute-start(f32[32,128]{1,0:T(8,128)S(1)} %get-tuple-element.44.to_second), channel_id=1, source_target_pairs={{1,2},{2,1},{3,4},{4,3},{5,6},{6,5},{7,8},{8,7},{9,10},{10,9},{11,... | collective-permute-start | bytes 49160 | tf_op jit(solution)/shard_map/ppermute | solution.py:22
  93.8 3.1 %collective-permute-start.13 = (f32[32,128]{1,0:T(8,128)S(1)}, f32[32,128]{1,0:T(8,128)S(1)}, u32[]{:S(2)}, u32[]{:S(2)}) collective-permute-start(f32[32,128]{1,0:T(8,128)S(1)} %get-tuple-element.45.to_first), channel_id=1, source_target_pairs={{0,1},{1,0},{2,3},{3,2},{4,5},{5,4},{6,7},{7,6},{8,9},{9,8},{10,11... | collective-permute-start | bytes 49160 | tf_op jit(solution)/shard_map/ppermute | solution.py:22

commit v8 on v6

--- a/solution.py
+++ b/solution.py
@@ -197,10 +197,12 @@
         ]
         pair = jnp.concatenate(high_low(jnp.concatenate(first, axis=1)), axis=0)
         second = jnp.dot(lat[...], pair, preferred_element_type=jnp.float32)
+        terms = []
         for k in range(2):
             m = 2 * j + k
             there = jnp.concatenate([ens[m], rows_first[m], rows_second[m]], axis=0).astype(jnp.float32)
-            total = total + there * second[:, cols * k : cols * (k + 1)]
+            terms.append(there * second[:, cols * k : cols * (k + 1)])
+        total = total + (terms[0] + terms[1])
     total = total / (members - 1)
     image = maskf * by_partner(total[:rows], odd) + obs_error[...] * vector[...]
     to_first[:HMAX] = total[rows : rows + HMAX]

time: 103 us -> 103 us (level)
  no operation moved by 1% of the time
where the time goes in v8:
time: 103 us
  starting transfers between devices  57.7 us (56%)
  waiting for transfers between devices  18.9 us (18%)
  blocking collectives  13.3 us (13%)
  Pallas kernels  7.55 us (7%)
  local copies, waits for them, and re-layouts  2.53 us (2%)
  between operations  2.29 us (2%)
    ppermute x14, starting transfers between devices, swap(): return lax.ppermute(cells, axis, pairs)  53 us
    ppermute x14, waiting for transfers between devices, swap(): return lax.ppermute(cells, axis, pairs)  13.9 us
    all_to_all x1, blocking collectives, shards(): parts = lax.all_to_all(gram, ('far', 'lat'), 0, 0)  13.3 us
    pallas_call x11, Pallas kernels, call(): pl.pallas_call(kernel, out_shape=outs, compiler_params=pltpu.CompilerPara...  7.55 us
    all_to_all x1, waiting for transfers between devices, shards(): parts = lax.all_to_all(parts, 'near', 0, 0)  5.01 us
    all_to_all x1, starting transfers between devices, shards(): parts = lax.all_to_all(parts, 'near', 0, 0)  4.74 us
  transfers between devices with their start and end apart: 15, of which 11 were waited for; matrix products, arithmetic and copies ran while one was open for 1% of the time, Pallas kernels for 1%

profile of v8, /device:TPU:1, one launch (start us, length us, event | category | flops | bytes accessed | tf_op | source)
XLA Modules:
  0.0 102.7 jit_solution(7590058291580168229)
XLA Ops:
  2.1 4.5 %collective-permute-start.2 = (bf16[64,32,128]{2,1,0:T(8,128)(2,1)S(1)}, bf16[64,32,128]{2,1,0:T(8,128)(2,1)S(1)}, u32[]{:S(2)}, u32[]{:S(2)}) collective-permute-start(bf16[64,32,128]{2,1,0:T(8,128)(2,1)S(1)} %get-tuple-element.25.half_second.refs_1_.refs_2_), channel_id=1, source_target_pairs={{1,2},{2,1},{3,4},{4,3},{5,6},{6,5},{7,8},{8,7},{9,10},{10,9},{11,... | collective-permute-start | bytes 1572872 | tf_op jit(solution)/shard_map/ppermute | solution.py:22
  6.7 5.0 %collective-permute-start.3 = (bf16[64,32,128]{2,1,0:T(8,128)(2,1)S(1)}, bf16[64,32,128]{2,1,0:T(8,128)(2,1)S(1)}, u32[]{:S(2)}, u32[]{:S(2)}) collective-permute-start(bf16[64,32,128]{2,1,0:T(8,128)(2,1)S(1)} %get-tuple-element.26.half_first.refs_2_.refs_3_), channel_id=1, source_target_pairs={{0,1},{1,0},{2,3},{3,2},{4,5},{5,4},{6,7},{7,6},{8,9},{9,8},{10,11... | collective-permute-start | bytes 1572872 | tf_op jit(solution)/shard_map/ppermute | solution.py:22
  12.1 10.2 %collective-permute-start = (bf16[18,64,128]{2,1,0:T(8,128)(2,1)S(1)}, bf16[18,64,128]{2,1,0:T(8,128)(2,1)S(1)}, u32[]{:S(2)}, u32[]{:S(2)}) collective-permute-start(bf16[18,64,128]{2,1,0:T(8,128)(2,1)S(1)} %get-tuple-element.27), channel_id=1, source_target_pairs={{0,496},{16,32},{32,16},{48,64},{64,48},{80,96},{96,80},{112,128},... | collective-permute-start | bytes 884744 | tf_op jit(solution)/shard_map/ppermute | solution.py:22
  22.4 1.9 %collective-permute-start.1 = (bf16[18,64,128]{2,1,0:T(8,128)(2,1)S(1)}, bf16[18,64,128]{2,1,0:T(8,128)(2,1)S(1)}, u32[]{:S(2)}, u32[]{:S(2)}) collective-permute-start(bf16[18,64,128]{2,1,0:T(8,128)(2,1)S(1)} %get-tuple-element.28), channel_id=1, source_target_pairs={{0,16},{16,0},{32,48},{48,32},{64,80},{80,64},{96,112},{112,96},{1... | collective-permute-start | bytes 884744 | tf_op jit(solution)/shard_map/ppermute | solution.py:22
  27.3 2.0 %collective-permute-done.from_second = bf16[18,64,128]{2,1,0:T(8,128)(2,1)S(1)} collective-permute-done((bf16[18,64,128]{2,1,0:T(8,128)(2,1)S(1)}, bf16[18,64,128]{2,1,0:T(8,128)(2,1)S(1)}, u32[]{:S(2)}, u32[]{:S(2)}) %collective-permute-start) | collective-permute-done | bytes 294944 | tf_op jit(solution)/shard_map/ppermute | solution.py:22
  29.3 2.7 %collective-permute-done.1.from_first = bf16[18,64,128]{2,1,0:T(8,128)(2,1)S(1)} collective-permute-done((bf16[18,64,128]{2,1,0:T(8,128)(2,1)S(1)}, bf16[18,64,128]{2,1,0:T(8,128)(2,1)S(1)}, u32[]{:S(2)}, u32[]{:S(2)}) %collective-permute-start.1) | collective-permute-done | bytes 294944 | tf_op jit(solution)/shard_map/ppermute | solution.py:22
  32.4 1.6 %taper_0.1 = (f32[64,128]{1,0:T(8,128)S(1)}, f32[64,128]{1,0:T(8,128)S(1)}, f32[64,128]{1,0:T(8,128)S(1)}) custom-call(s32[8,128]{1,0:T(8,128)S(1)} %broadcast_in_dim.37.odd, f32[64,128]{1,0:T(8,128)S(1)} %copy-done.2, s32[64,128]{1,0:T(8,128)S(1)} %copy-done, f32[64,128]{1,0:T(8,128)S(1)} %copy-done.3, f32[64,128]{1,0:T(8,128)S(1)} %get-tuple-element.29.refs_0_, ...), custom_call_target="tpu_custom_call" | custom-call | flops 805306368 | bytes 2985984 | tf_op jit(solution)/shard_map/taper_0/pallas_call | solution.py:291
  34.0 4.4 %collective-permute-start.4 = (f32[64,128]{1,0:T(8,128)S(1)}, f32[64,128]{1,0:T(8,128)S(1)}, u32[]{:S(2)}, u32[]{:S(2)}) collective-permute-start(f32[64,128]{1,0:T(8,128)S(1)} %get-tuple-element.32), channel_id=1, source_target_pairs={{1,2},{2,1},{3,4},{4,3},{5,6},{6,5},{7,8},{8,7},{9,10},{10,9},{11,... | collective-permute-start | bytes 98312 | tf_op jit(solution)/shard_map/ppermute | solution.py:22
  38.4 1.9 %collective-permute-start.5 = (f32[64,128]{1,0:T(8,128)S(1)}, f32[64,128]{1,0:T(8,128)S(1)}, u32[]{:S(2)}, u32[]{:S(2)}) collective-permute-start(f32[64,128]{1,0:T(8,128)S(1)} %get-tuple-element.33), channel_id=1, source_target_pairs={{0,1},{1,0},{2,3},{3,2},{4,5},{5,4},{6,7},{7,6},{8,9},{9,8},{10,11... | collective-permute-start | bytes 98312 | tf_op jit(solution)/shard_map/ppermute | solution.py:22
  41.6 4.3 %collective-permute-start.6 = (f32[64,128]{1,0:T(8,128)S(1)}, f32[64,128]{1,0:T(8,128)S(1)}, u32[]{:S(2)}, u32[]{:S(2)}) collective-permute-start(f32[64,128]{1,0:T(8,128)S(1)} %get-tuple-element.35), channel_id=1, source_target_pairs={{0,496},{16,32},{32,16},{48,64},{64,48},{80,96},{96,80},{112,128},... | collective-permute-start | bytes 98312 | tf_op jit(solution)/shard_map/ppermute | solution.py:22
  46.0 1.9 %collective-permute-start.7 = (f32[64,128]{1,0:T(8,128)S(1)}, f32[64,128]{1,0:T(8,128)S(1)}, u32[]{:S(2)}, u32[]{:S(2)}) collective-permute-start(f32[64,128]{1,0:T(8,128)S(1)} %get-tuple-element.36), channel_id=1, source_target_pairs={{0,16},{16,0},{32,48},{48,32},{64,80},{80,64},{96,112},{112,96},{1... | collective-permute-start | bytes 98312 | tf_op jit(solution)/shard_map/ppermute | solution.py:22
  47.9 2.0 %collective-permute-done.6.refs_0_ = f32[64,128]{1,0:T(8,128)S(1)} collective-permute-done((f32[64,128]{1,0:T(8,128)S(1)}, f32[64,128]{1,0:T(8,128)S(1)}, u32[]{:S(2)}, u32[]{:S(2)}) %collective-permute-start.6) | collective-permute-done | bytes 32800 | tf_op jit(solution)/shard_map/ppermute | solution.py:22
  50.8 1.6 %taper_1.1 = (f32[64,128]{1,0:T(8,128)S(1)}, f32[64,128]{1,0:T(8,128)S(1)}, f32[64,128]{1,0:T(8,128)S(1)}) custom-call(s32[8,128]{1,0:T(8,128)S(1)} %broadcast_in_dim.37.odd, f32[64,128]{1,0:T(8,128)S(1)} %get-tuple-element.34.vector.v1, s32[64,128]{1,0:T(8,128)S(1)} %copy-done, f32[64,128]{1,0:T(8,128)S(1)} %copy-done.3, ...), custom_call_target="tpu_custom_call" | custom-call | flops 805306368 | bytes 3018752 | tf_op jit(solution)/shard_map/taper_1/pallas_call | solution.py:291
  52.4 5.3 %collective-permute-start.8 = (f32[64,128]{1,0:T(8,128)S(1)}, f32[64,128]{1,0:T(8,128)S(1)}, u32[]{:S(2)}, u32[]{:S(2)}) collective-permute-start(f32[64,128]{1,0:T(8,128)S(1)} %get-tuple-element.38.refs_0_), channel_id=1, source_target_pairs={{1,2},{2,1},{3,4},{4,3},{5,6},{6,5},{7,8},{8,7},{9,10},{10,9},{11,... | collective-permute-start | bytes 98312 | tf_op jit(solution)/shard_map/ppermute | solution.py:22
  57.7 1.9 %collective-permute-start.9 = (f32[64,128]{1,0:T(8,128)S(1)}, f32[64,128]{1,0:T(8,128)S(1)}, u32[]{:S(2)}, u32[]{:S(2)}) collective-permute-start(f32[64,128]{1,0:T(8,128)S(1)} %get-tuple-element.39.refs_1_), channel_id=1, source_target_pairs={{0,1},{1,0},{2,3},{3,2},{4,5},{5,4},{6,7},{7,6},{8,9},{9,8},{10,11... | collective-permute-start | bytes 98312 | tf_op jit(solution)/shard_map/ppermute | solution.py:22
  61.0 4.6 %collective-permute-start.10 = (f32[64,128]{1,0:T(8,128)S(1)}, f32[64,128]{1,0:T(8,128)S(1)}, u32[]{:S(2)}, u32[]{:S(2)}) collective-permute-start(f32[64,128]{1,0:T(8,128)S(1)} %get-tuple-element.41), channel_id=1, source_target_pairs={{0,496},{16,32},{32,16},{48,64},{64,48},{80,96},{96,80},{112,128},... | collective-permute-start | bytes 98312 | tf_op jit(solution)/shard_map/ppermute | solution.py:22
  65.6 1.9 %collective-permute-start.11 = (f32[64,128]{1,0:T(8,128)S(1)}, f32[64,128]{1,0:T(8,128)S(1)}, u32[]{:S(2)}, u32[]{:S(2)}) collective-permute-start(f32[64,128]{1,0:T(8,128)S(1)} %get-tuple-element.42), channel_id=1, source_target_pairs={{0,16},{16,0},{32,48},{48,32},{64,80},{80,64},{96,112},{112,96},{1... | collective-permute-start | bytes 98312 | tf_op jit(solution)/shard_map/ppermute | solution.py:22
  67.5 1.8 %collective-permute-done.10.refs_0_ = f32[64,128]{1,0:T(8,128)S(1)} collective-permute-done((f32[64,128]{1,0:T(8,128)S(1)}, f32[64,128]{1,0:T(8,128)S(1)}, u32[]{:S(2)}, u32[]{:S(2)}) %collective-permute-start.10) | collective-permute-done | bytes 32800 | tf_op jit(solution)/shard_map/ppermute | solution.py:22
  70.2 1.6 %taper_2.1 = (f32[64,128]{1,0:T(8,128)S(1)}, f32[32,128]{1,0:T(8,128)S(1)}, f32[32,128]{1,0:T(8,128)S(1)}) custom-call(s32[8,128]{1,0:T(8,128)S(1)} %broadcast_in_dim.37.odd, f32[64,128]{1,0:T(8,128)S(1)} %get-tuple-element.40.vector.v2, s32[64,128]{1,0:T(8,128)S(1)} %copy-done, f32[64,128]{1,0:T(8,128)S(1)} %copy-done.3, ...), custom_call_target="tpu_custom_call" | custom-call | flops 805306368 | bytes 3018752 | tf_op jit(solution)/shard_map/taper_2/pallas_call | solution.py:291
  71.9 13.3 %all_to_all.10.parts = f32[32,1,128]{2,1,0:T(1,128)S(1)} all-to-all(f32[32,1,128]{2,1,0:T(1,128)S(1)} %gram_kernel.1), channel_id=1, replica_groups=mesh['far'=2,'near'=16,'lat'=16] {'far','lat'}, dimensions={0} | all-to-all | bytes 32768 | tf_op jit(solution)/shard_map/all_to_all | solution.py:359
  85.9 4.7 %all-to-all-start.1 = ((f32[16,1,128]{2,1,0:T(1,128)}), f32[16,1,128]{2,1,0:T(1,128)S(1)}, u32[]{:S(2)}, u32[]{:S(2)}) async-start(f32[16,1,128]{2,1,0:T(1,128)} %sum_kernel.1), calls=%async_computation.1 | async-start | bytes 16384 | tf_op jit(solution)/shard_map/all_to_all | solution.py:361
  90.6 3.1 %collective-permute-start.12 = (f32[32,128]{1,0:T(8,128)S(1)}, f32[32,128]{1,0:T(8,128)S(1)}, u32[]{:S(2)}, u32[]{:S(2)}) collective-permute-start(f32[32,128]{1,0:T(8,128)S(1)} %get-tuple-element.44.to_second), channel_id=1, source_target_pairs={{1,2},{2,1},{3,4},{4,3},{5,6},{6,5},{7,8},{8,7},{9,10},{10,9},{11,... | collective-permute-start | bytes 49160 | tf_op jit(solution)/shard_map/ppermute | solution.py:22
  93.8 1.9 %collective-permute-start.13 = (f32[32,128]{1,0:T(8,128)S(1)}, f32[32,128]{1,0:T(8,128)S(1)}, u32[]{:S(2)}, u32[]{:S(2)}) collective-permute-start(f32[32,128]{1,0:T(8,128)S(1)} %get-tuple-element.45.to_first), channel_id=1, source_target_pairs={{0,1},{1,0},{2,3},{3,2},{4,5},{5,4},{6,7},{7,6},{8,9},{9,8},{10,11... | collective-permute-start | bytes 49160 | tf_op jit(solution)/shard_map/ppermute | solution.py:22
  96.8 5.0 %all-to-all-done.1.parts = f32[16,1,128]{2,1,0:T(1,128)S(1)} async-done(((f32[16,1,128]{2,1,0:T(1,128)}), f32[16,1,128]{2,1,0:T(1,128)S(1)}, u32[]{:S(2)}, u32[]{:S(2)}) %all-to-all-start.1) | async-done | bytes 8224 | tf_op jit(solution)/shard_map/all_to_all | solution.py:361
  (42 shorter events, 11.2 us)
Async XLA Ops:
  0.7 1.2 %copy-start.1 = (bf16[64,64,128]{2,1,0:T(8,128)(2,1)S(1)}, bf16[64,64,128]{2,1,0:T(8,128)(2,1)}, u32[]{:S(2)}) copy-start(bf16[64,64,128]{2,1,0:T(8,128)(2,1)} %ens.1) | copy-start | bytes 3145732
  2.0 9.7 %copy-start = (s32[64,128]{1,0:T(8,128)S(1)}, s32[64,128]{1,0:T(8,128)}, u32[]{:S(2)}) copy-start(s32[64,128]{1,0:T(8,128)} %valid.11) | copy-start | bytes 98308
  2.0 9.7 %copy-start.2 = (f32[64,128]{1,0:T(8,128)S(1)}, f32[64,128]{1,0:T(8,128)}, u32[]{:S(2)}) copy-start(f32[64,128]{1,0:T(8,128)} %v0.3) | copy-start | bytes 98308
  2.1 30.2 %collective-permute-start.2 = (bf16[64,32,128]{2,1,0:T(8,128)(2,1)S(1)}, bf16[64,32,128]{2,1,0:T(8,128)(2,1)S(1)}, u32[]{:S(2)}, u32[]{:S(2)}) collective-permute-start(bf16[64,32,128]{2,1,0:T(8,128)(2,1)S(1)} %get-tuple-element.25.half_second.refs_1_.refs_2_), channel_id=1, source_target_pairs={{1,2},{2,1},{3,4},{4,3},{5,6},{6,5},{7,8},{8,7},{9,10},{10,9},{11,... | collective-permute-start | bytes 1572872 | tf_op jit(solution)/shard_map/ppermute | solution.py:22
  6.7 25.7 %collective-permute-start.3 = (bf16[64,32,128]{2,1,0:T(8,128)(2,1)S(1)}, bf16[64,32,128]{2,1,0:T(8,128)(2,1)S(1)}, u32[]{:S(2)}, u32[]{:S(2)}) collective-permute-start(bf16[64,32,128]{2,1,0:T(8,128)(2,1)S(1)} %get-tuple-element.26.half_first.refs_2_.refs_3_), channel_id=1, source_target_pairs={{0,1},{1,0},{2,3},{3,2},{4,5},{5,4},{6,7},{7,6},{8,9},{9,8},{10,11... | collective-permute-start | bytes 1572872 | tf_op jit(solution)/shard_map/ppermute | solution.py:22
  12.1 17.2 %collective-permute-start = (bf16[18,64,128]{2,1,0:T(8,128)(2,1)S(1)}, bf16[18,64,128]{2,1,0:T(8,128)(2,1)S(1)}, u32[]{:S(2)}, u32[]{:S(2)}) collective-permute-start(bf16[18,64,128]{2,1,0:T(8,128)(2,1)S(1)} %get-tuple-element.27), channel_id=1, source_target_pairs={{0,496},{16,32},{32,16},{48,64},{64,48},{80,96},{96,80},{112,128},... | collective-permute-start | bytes 884744 | tf_op jit(solution)/shard_map/ppermute | solution.py:22
  22.4 9.6 %collective-permute-start.1 = (bf16[18,64,128]{2,1,0:T(8,128)(2,1)S(1)}, bf16[18,64,128]{2,1,0:T(8,128)(2,1)S(1)}, u32[]{:S(2)}, u32[]{:S(2)}) collective-permute-start(bf16[18,64,128]{2,1,0:T(8,128)(2,1)S(1)} %get-tuple-element.28), channel_id=1, source_target_pairs={{0,16},{16,0},{32,48},{48,32},{64,80},{80,64},{96,112},{112,96},{1... | collective-permute-start | bytes 884744 | tf_op jit(solution)/shard_map/ppermute | solution.py:22
  24.3 0.7 copy-start.4
  27.3 5.1 %copy-start.3 = (f32[64,128]{1,0:T(8,128)S(1)}, f32[64,128]{1,0:T(8,128)}, u32[]{:S(2)}) copy-start(f32[64,128]{1,0:T(8,128)} %obs_error.5) | copy-start | bytes 98308
  34.0 6.3 %collective-permute-start.4 = (f32[64,128]{1,0:T(8,128)S(1)}, f32[64,128]{1,0:T(8,128)S(1)}, u32[]{:S(2)}, u32[]{:S(2)}) collective-permute-start(f32[64,128]{1,0:T(8,128)S(1)} %get-tuple-element.32), channel_id=1, source_target_pairs={{1,2},{2,1},{3,4},{4,3},{5,6},{6,5},{7,8},{8,7},{9,10},{10,9},{11,... | collective-permute-start | bytes 98312 | tf_op jit(solution)/shard_map/ppermute | solution.py:22
  38.4 3.1 %collective-permute-start.5 = (f32[64,128]{1,0:T(8,128)S(1)}, f32[64,128]{1,0:T(8,128)S(1)}, u32[]{:S(2)}, u32[]{:S(2)}) collective-permute-start(f32[64,128]{1,0:T(8,128)S(1)} %get-tuple-element.33), channel_id=1, source_target_pairs={{0,1},{1,0},{2,3},{3,2},{4,5},{5,4},{6,7},{7,6},{8,9},{9,8},{10,11... | collective-permute-start | bytes 98312 | tf_op jit(solution)/shard_map/ppermute | solution.py:22
  41.6 8.3 %collective-permute-start.6 = (f32[64,128]{1,0:T(8,128)S(1)}, f32[64,128]{1,0:T(8,128)S(1)}, u32[]{:S(2)}, u32[]{:S(2)}) collective-permute-start(f32[64,128]{1,0:T(8,128)S(1)} %get-tuple-element.35), channel_id=1, source_target_pairs={{0,496},{16,32},{32,16},{48,64},{64,48},{80,96},{96,80},{112,128},... | collective-permute-start | bytes 98312 | tf_op jit(solution)/shard_map/ppermute | solution.py:22
  46.0 4.9 %collective-permute-start.7 = (f32[64,128]{1,0:T(8,128)S(1)}, f32[64,128]{1,0:T(8,128)S(1)}, u32[]{:S(2)}, u32[]{:S(2)}) collective-permute-start(f32[64,128]{1,0:T(8,128)S(1)} %get-tuple-element.36), channel_id=1, source_target_pairs={{0,16},{16,0},{32,48},{48,32},{64,80},{80,64},{96,112},{112,96},{1... | collective-permute-start | bytes 98312 | tf_op jit(solution)/shard_map/ppermute | solution.py:22
  52.4 7.3 %collective-permute-start.8 = (f32[64,128]{1,0:T(8,128)S(1)}, f32[64,128]{1,0:T(8,128)S(1)}, u32[]{:S(2)}, u32[]{:S(2)}) collective-permute-start(f32[64,128]{1,0:T(8,128)S(1)} %get-tuple-element.38.refs_0_), channel_id=1, source_target_pairs={{1,2},{2,1},{3,4},{4,3},{5,6},{6,5},{7,8},{8,7},{9,10},{10,9},{11,... | collective-permute-start | bytes 98312 | tf_op jit(solution)/shard_map/ppermute | solution.py:22
  57.7 3.1 %collective-permute-start.9 = (f32[64,128]{1,0:T(8,128)S(1)}, f32[64,128]{1,0:T(8,128)S(1)}, u32[]{:S(2)}, u32[]{:S(2)}) collective-permute-start(f32[64,128]{1,0:T(8,128)S(1)} %get-tuple-element.39.refs_1_), channel_id=1, source_target_pairs={{0,1},{1,0},{2,3},{3,2},{4,5},{5,4},{6,7},{7,6},{8,9},{9,8},{10,11... | collective-permute-start | bytes 98312 | tf_op jit(solution)/shard_map/ppermute | solution.py:22
  61.0 8.3 %collective-permute-start.10 = (f32[64,128]{1,0:T(8,128)S(1)}, f32[64,128]{1,0:T(8,128)S(1)}, u32[]{:S(2)}, u32[]{:S(2)}) collective-permute-start(f32[64,128]{1,0:T(8,128)S(1)} %get-tuple-element.41), channel_id=1, source_target_pairs={{0,496},{16,32},{32,16},{48,64},{64,48},{80,96},{96,80},{112,128},... | collective-permute-start | bytes 98312 | tf_op jit(solution)/shard_map/ppermute | solution.py:22
  65.6 4.7 %collective-permute-start.11 = (f32[64,128]{1,0:T(8,128)S(1)}, f32[64,128]{1,0:T(8,128)S(1)}, u32[]{:S(2)}, u32[]{:S(2)}) collective-permute-start(f32[64,128]{1,0:T(8,128)S(1)} %get-tuple-element.42), channel_id=1, source_target_pairs={{0,16},{16,0},{32,48},{48,32},{64,80},{80,64},{96,112},{112,96},{1... | collective-permute-start | bytes 98312 | tf_op jit(solution)/shard_map/ppermute | solution.py:22
  85.9 16.0 %all-to-all-start.1 = ((f32[16,1,128]{2,1,0:T(1,128)}), f32[16,1,128]{2,1,0:T(1,128)S(1)}, u32[]{:S(2)}, u32[]{:S(2)}) async-start(f32[16,1,128]{2,1,0:T(1,128)} %sum_kernel.1), calls=%async_computation.1 | async-start | bytes 16384 | tf_op jit(solution)/shard_map/all_to_all | solution.py:361
  90.6 5.4 %collective-permute-start.12 = (f32[32,128]{1,0:T(8,128)S(1)}, f32[32,128]{1,0:T(8,128)S(1)}, u32[]{:S(2)}, u32[]{:S(2)}) collective-permute-start(f32[32,128]{1,0:T(8,128)S(1)} %get-tuple-element.44.to_second), channel_id=1, source_target_pairs={{1,2},{2,1},{3,4},{4,3},{5,6},{6,5},{7,8},{8,7},{9,10},{10,9},{11,... | collective-permute-start | bytes 49160 | tf_op jit(solution)/shard_map/ppermute | solution.py:22
  93.8 3.1 %collective-permute-start.13 = (f32[32,128]{1,0:T(8,128)S(1)}, f32[32,128]{1,0:T(8,128)S(1)}, u32[]{:S(2)}, u32[]{:S(2)}) collective-permute-start(f32[32,128]{1,0:T(8,128)S(1)} %get-tuple-element.45.to_first), channel_id=1, source_target_pairs={{0,1},{1,0},{2,3},{3,2},{4,5},{5,4},{6,7},{7,6},{8,9},{9,8},{10,11... | collective-permute-start | bytes 49160 | tf_op jit(solution)/shard_map/ppermute | solution.py:22
